TPU v7x, 32 devices: a whole 2x2x4 slice. The times are simulated.
32 devices in a mesh: section: 2 (over core), seq: 4 (over z), head: 4 (over y, x).
Axes of the slice: x: 2, y: 2, z: 4, core: 2. Of those that a mesh axis runs over, the one named last changes fastest.
Arguments:
- inputs: bfloat16 [4, 1024, 1536], P(None, 'seq'), may hold values from -6 to 6
- cotangent: bfloat16 [4, 1024, 1536], P(None, 'seq'), may hold values from -6 to 6
- norm_gain: float32 [2, 1536], P('section'), may hold values from 0.5 to 1.5
- w_z: bfloat16 [2, 1536, 3072], P('section', None, 'head'), may hold values from -0.15625 to 0.15625
- w_x: bfloat16 [2, 1536, 3072], P('section', None, 'head'), may hold values from -0.15625 to 0.15625
- w_bc: bfloat16 [2, 1536, 256], P('section'), may hold values from -0.15625 to 0.15625
- w_dt: bfloat16 [2, 1536, 48], P('section', None, 'head'), may hold values from -0.15625 to 0.15625
- conv_x: float32 [2, 4, 3072], P('section', None, 'head'), may hold values from -3 to 3
- conv_x_bias: float32 [2, 3072], P('section', 'head'), may hold values from -3 to 3
- conv_bc: float32 [2, 4, 256], P('section'), may hold values from -3 to 3
- conv_bc_bias: float32 [2, 256], P('section'), may hold values from -3 to 3
- dt_bias: float32 [2, 48], P('section', 'head'), may hold values from -4 to -1
- a_log: float32 [2, 48], P('section', 'head'), may hold values from -12 to 1
- d_skip: float32 [2, 48], P('section', 'head'), may hold values from 0.5 to 1.5
- gate_gain: float32 [2, 3072], P('section', 'head'), may hold values from 0.5 to 1.5
- w_out: bfloat16 [2, 3072, 1536], P('section', 'head'), may hold values from -0.109375 to 0.109375
Outputs:
- layer_outputs: bfloat16 [2, 4, 1024, 1536], P('section', None, 'seq')
- input_grads: bfloat16 [2, 4, 1024, 1536], P('section', None, 'seq')
- grad_norm_gain: float32 [2, 1536], P('section')
- grad_w_z: float32 [2, 1536, 3072], P('section', None, 'head')
- grad_w_x: float32 [2, 1536, 3072], P('section', None, 'head')
- grad_w_bc: float32 [2, 1536, 256], P('section')
- grad_w_dt: float32 [2, 1536, 48], P('section', None, 'head')
- grad_conv_x: float32 [2, 4, 3072], P('section', None, 'head')
- grad_conv_x_bias: float32 [2, 3072], P('section', 'head')
- grad_conv_bc: float32 [2, 4, 256], P('section')
- grad_conv_bc_bias: float32 [2, 256], P('section')
- grad_dt_bias: float32 [2, 48], P('section', 'head')
- grad_a_log: float32 [2, 48], P('section', 'head')
- grad_d_skip: float32 [2, 48], P('section', 'head')
- grad_gate_gain: float32 [2, 3072], P('section', 'head')
- grad_w_out: float32 [2, 3072, 1536], P('section', 'head')
All inputs are finite; a program needn't handle non-finite values.
Results may differ from a plain program's by a relative error of at most 0.035.
Values may be sent and summed in bfloat16 or wider, within the bound.
A program may use at most 320 MiB of HBM per device.

v0:
```python
import jax
import jax.numpy as jnp
from jax import lax
from jax.sharding import PartitionSpec as P

EPSILON = 1e-05
PRECISION = lax.Precision.HIGHEST


def from_behind(block, axis, distance):
    devices = range(lax.axis_size(axis))
    route = [(i - distance, i) for i in devices if i - distance in devices]
    return lax.ppermute(block, axis, route)


def entering(value, axis, combine, identity):
    size, index = (lax.axis_size(axis), lax.axis_index(axis))
    everything = jax.tree.map(lambda part: lax.all_gather(part, axis), value)
    start = jax.tree.map(
        lambda part, zero: jnp.broadcast_to(jnp.asarray(zero, part.dtype), part.shape),
        value,
        identity,
    )

    def lap(k, before):
        reached = k < index
        new = combine(before, jax.tree.map(lambda part: part[k], everything))
        return jax.tree.map(lambda a, b: jnp.where(reached, a, b), new, before)

    return lax.fori_loop(0, size, lap, start)


def prefix(value, axis, join, neutral):
    count = lax.axis_size(axis)
    place = lax.axis_index(axis)
    ahead = count - 1 - place
    gathered = jax.tree.map(
        lambda a, kind: lax.all_gather(a.astype(kind), axis),
        value,
        jax.tree.map(lambda a: jnp.bfloat16 if a.dtype == jnp.float32 else a.dtype, value),
    )
    state = jax.tree.map(lambda a, e: jnp.zeros_like(a) + jnp.asarray(e, a.dtype), value, neutral)

    def one(lap, state):
        source = count - 1 - lap
        return join(
            state,
            jax.tree.map(
                lambda a, own: lax.dynamic_index_in_dim(a, source, 0, False).astype(own.dtype),
                gathered,
                value,
            ),
        )

    return lax.fori_loop(0, ahead, one, state)


def silu(values):
    return values * jax.nn.sigmoid(values)


def matmul(first_op, second_op):
    return jnp.dot(first_op, second_op, preferred_element_type=jnp.float32)


def matmul_left_t(first_op, second_op):
    return lax.dot_general(
        first_op, second_op, (((0,), (0,)), ((), ())), preferred_element_type=jnp.float32
    )


def matmul_right_t(first_op, second_op):
    return lax.dot_general(
        first_op, second_op, (((1,), (1,)), ((), ())), preferred_element_type=jnp.float32
    )


def combine(earlier, latter):
    return (earlier[0] * latter[0], latter[0][:, None, None] * earlier[1] + latter[1])


def conv_local(extended, kernel, offset):
    length = extended.shape[0] - kernel.shape[0] + 1
    summed = jnp.broadcast_to(offset[None, :], (length, offset.shape[0]))
    for lagged in range(kernel.shape[0]):
        summed = summed + kernel[lagged][None, :] * extended[lagged : lagged + length]
    return silu(summed)


def part_state(extended, dt_raw, kernel_x, kernel_bc, offset_x, offset_bc, dt_bias, a_log):
    local_width = kernel_x.shape[1]
    state_width = kernel_bc.shape[1] // 2
    head_count = dt_bias.shape[0]
    conv_x = conv_local(extended[:, :local_width], kernel_x, offset_x)
    conv_bc = conv_local(extended[:, local_width:], kernel_bc, offset_bc)
    tokens_here = conv_x.shape[0]
    x_heads = conv_x.reshape(tokens_here, head_count, local_width // head_count)
    b_rows = conv_bc[:, :state_width]
    c_rows = conv_bc[:, state_width:]
    step_size = jax.nn.softplus(dt_raw + dt_bias[None, :])
    cumulative = jnp.cumsum(step_size * (-jnp.exp(a_log))[None, :], axis=0)
    weighted_tail = jnp.exp(cumulative[-1][None, :] - cumulative) * step_size
    local_state = jnp.einsum("sh,shp,sn->hpn", weighted_tail, x_heads, b_rows, precision=PRECISION)
    return (x_heads, b_rows, c_rows, step_size, cumulative, local_state, cumulative[-1])


def part_output(x_heads, b_rows, c_rows, step_size, cumulative, incoming, z_val, d_skip):
    tokens_here = cumulative.shape[0]
    scores = jnp.dot(c_rows, b_rows.T, precision=PRECISION)
    causal_mask = (jnp.arange(tokens_here)[:, None] >= jnp.arange(tokens_here)[None, :])[:, :, None]
    decays = jnp.exp(jnp.where(causal_mask, cumulative[:, None, :] - cumulative[None, :, :], -1e30))
    weights = scores[:, :, None] * decays * step_size[None, :, :]
    within = jnp.einsum("tsh,shp->thp", weights, x_heads, precision=PRECISION)
    carried = jnp.exp(cumulative)[:, :, None] * jnp.einsum(
        "tn,hpn->thp", c_rows, incoming, precision=PRECISION
    )
    mixed = within + carried + d_skip[None, :, None] * x_heads
    return mixed.reshape(tokens_here, -1) * silu(z_val)


def forward_mixer(u_val, params):
    rms_scale = lax.rsqrt(jnp.mean(u_val * u_val, axis=-1, keepdims=True) + EPSILON)
    normed = (u_val * rms_scale * params["gain"][None, :]).astype(jnp.bfloat16)
    z_val = matmul(normed, params["w_z"])
    x_val = matmul(normed, params["w_x"]).astype(jnp.bfloat16)
    bc_val = matmul(normed, params["w_bc"]).astype(jnp.bfloat16)
    dt_raw = matmul(normed, params["w_dt"])
    joined = jnp.concatenate([x_val, bc_val], axis=1)
    rim_width = params["kernel_x"].shape[0] - 1
    rim_rows = from_behind(joined[joined.shape[0] - rim_width :], "seq", 1)
    extended = jnp.concatenate([rim_rows, joined], axis=0).astype(jnp.float32)
    pieces, pull_state = jax.vjp(
        part_state,
        extended,
        dt_raw,
        params["kernel_x"],
        params["kernel_bc"],
        params["offset_x"],
        params["offset_bc"],
        params["dt_bias"],
        params["a_log"],
    )
    decay_total = jnp.exp(pieces[6])
    identity = (jnp.ones_like(decay_total), jnp.zeros_like(pieces[5]))
    _, incoming = entering((decay_total, pieces[5]), "seq", combine, identity)
    gated, pull_output = jax.vjp(
        part_output,
        pieces[0],
        pieces[1],
        pieces[2],
        pieces[3],
        pieces[4],
        incoming,
        z_val,
        params["d_skip"],
    )
    square_sums = lax.psum(jnp.sum(gated * gated, axis=-1), "head")
    full_width = gated.shape[1] * lax.axis_size("head")
    gate_scale = lax.rsqrt(square_sums / full_width + EPSILON)[:, None]
    normed_gate = (gated * gate_scale * params["gate_gain"][None, :]).astype(jnp.bfloat16)
    return {
        "normed": normed,
        "rms_scale": rms_scale,
        "pull_state": pull_state,
        "pull_output": pull_output,
        "decay_total": decay_total,
        "incoming": incoming,
        "gated": gated,
        "gate_scale": gate_scale,
        "normed_gate": normed_gate,
        "full_width": full_width,
    }


def forward_layer(u_val, params):
    kept = forward_mixer(u_val, params)
    branch = lax.psum(matmul(kept["normed_gate"], params["w_out"]), "head")
    return u_val + branch


def backward_layer(u_val, grad_out, params):
    kept = forward_mixer(u_val, params)
    grad_branch = grad_out.astype(jnp.bfloat16)
    grad_w_out = matmul_left_t(kept["normed_gate"], grad_branch)
    d_normed_gate = matmul_right_t(grad_branch, params["w_out"])
    gated = kept["gated"]
    gate_scale = kept["gate_scale"]
    grad_gate_gain = jnp.sum(d_normed_gate * gated * gate_scale, axis=0)
    scaled_grad = d_normed_gate * params["gate_gain"][None, :]
    across = lax.psum(jnp.sum(scaled_grad * gated, axis=-1), "head")
    d_gated = (
        gate_scale * scaled_grad - gated * gate_scale**3 * across[:, None] / kept["full_width"]
    )
    d_pieces = kept["pull_output"](d_gated)
    decay_total = kept["decay_total"]
    identity = (jnp.ones_like(decay_total), jnp.zeros_like(d_pieces[5]))
    _, d_state = prefix((decay_total, d_pieces[5]), "seq", combine, identity)
    d_decay_log = decay_total * jnp.sum(d_state * kept["incoming"], axis=(1, 2))
    grads_state = kept["pull_state"](
        (d_pieces[0], d_pieces[1], d_pieces[2], d_pieces[3], d_pieces[4], d_state, d_decay_log)
    )
    local_width = params["w_x"].shape[1]
    rim_width = params["kernel_x"].shape[0] - 1
    d_extended = grads_state[0]
    bc_part, grad_kernel_bc, grad_offset_bc = (
        lax.psum(d_extended[:, local_width:].astype(jnp.bfloat16), "head").astype(jnp.float32),
        lax.psum(grads_state[3].astype(jnp.bfloat16), "head").astype(jnp.float32),
        lax.psum(grads_state[5].astype(jnp.bfloat16), "head").astype(jnp.float32),
    )
    d_extended = jnp.concatenate([d_extended[:, :local_width], bc_part], axis=1)
    rim_back = from_behind(d_extended[:rim_width], "seq", -1)
    tokens_here = u_val.shape[0]
    d_joined = d_extended[rim_width:] + jnp.pad(rim_back, ((tokens_here - rim_width, 0), (0, 0)))
    grad_x = d_joined[:, :local_width].astype(jnp.bfloat16)
    grad_bc = d_joined[:, local_width:].astype(jnp.bfloat16)
    grad_z = d_pieces[6].astype(jnp.bfloat16)
    grad_dt = grads_state[1].astype(jnp.bfloat16)
    normed = kept["normed"]
    partial_in = (
        matmul_right_t(grad_z, params["w_z"])
        + matmul_right_t(grad_x, params["w_x"])
        + matmul_right_t(grad_dt, params["w_dt"])
    )
    d_normed = lax.psum(partial_in.astype(jnp.bfloat16), "head").astype(
        jnp.float32
    ) + matmul_right_t(grad_bc, params["w_bc"])
    rms_scale = kept["rms_scale"]
    grad_gain = jnp.sum(d_normed * u_val * rms_scale, axis=0)
    scaled_in = d_normed * params["gain"][None, :]
    d_u = (
        grad_out
        + rms_scale * scaled_in
        - u_val * rms_scale**3 * jnp.sum(scaled_in * u_val, axis=-1, keepdims=True) / u_val.shape[1]
    )
    grads = (
        grad_gain,
        matmul_left_t(normed, grad_z),
        matmul_left_t(normed, grad_x),
        matmul_left_t(normed, grad_bc),
        matmul_left_t(normed, grad_dt),
        grads_state[2],
        grads_state[4],
        grad_kernel_bc,
        grad_offset_bc,
        grads_state[6],
        grads_state[7],
        d_pieces[7],
        grad_gate_gain,
        grad_w_out,
    )
    return (d_u, grads)


def on_device(
    inputs,
    cotangent,
    norm_gain,
    w_z,
    w_x,
    w_bc,
    w_dt,
    conv_x,
    conv_x_bias,
    conv_bc,
    conv_bc_bias,
    dt_bias,
    a_log,
    d_skip,
    gate_gain,
    w_out,
):
    params = {
        "gain": norm_gain[0],
        "w_z": w_z[0],
        "w_x": w_x[0],
        "w_bc": w_bc[0],
        "w_dt": w_dt[0],
        "kernel_x": conv_x[0],
        "offset_x": conv_x_bias[0],
        "kernel_bc": conv_bc[0],
        "offset_bc": conv_bc_bias[0],
        "dt_bias": dt_bias[0],
        "a_log": a_log[0],
        "d_skip": d_skip[0],
        "gate_gain": gate_gain[0],
        "w_out": w_out[0],
    }
    micro_count = inputs.shape[0]
    is_first = lax.axis_index("section") == 0
    received = jnp.zeros(inputs.shape[1:], jnp.bfloat16)
    kept_inputs = []
    section_outputs = []
    for step_index in range(micro_count + 1):
        if step_index < micro_count:
            source = inputs[step_index]
        else:
            source = jnp.zeros(inputs.shape[1:], jnp.bfloat16)
        layer_input = jnp.where(is_first, source, received)
        kept_inputs.append(layer_input)
        result = forward_layer(layer_input.astype(jnp.float32), params)
        rounded = result.astype(jnp.bfloat16)
        section_outputs.append(rounded)
        if step_index < micro_count:
            received = from_behind(rounded, "section", 1)
    mailbox = jnp.zeros(inputs.shape[1:], jnp.float32)
    input_parts = []
    totals = None
    for step_index in range(micro_count + 1):
        if step_index < micro_count:
            upstream = cotangent[micro_count - 1 - step_index].astype(jnp.float32)
        else:
            upstream = jnp.zeros(inputs.shape[1:], jnp.float32)
        grad_out = jnp.where(is_first, mailbox, upstream)
        layer_input = kept_inputs[micro_count - step_index].astype(jnp.float32)
        d_u, tick_grads = backward_layer(layer_input, grad_out, params)
        input_parts.append(d_u.astype(jnp.bfloat16))
        if totals is None:
            totals = list(tick_grads)
        else:
            totals = [summand + addend for summand, addend in zip(totals, tick_grads)]
        if step_index < micro_count:
            mailbox = from_behind(d_u.astype(jnp.bfloat16), "section", -1).astype(d_u.dtype)
    summed = (
        lax.psum(totals[0].astype(jnp.bfloat16), "seq").astype(jnp.float32),
        lax.psum(totals[1].astype(jnp.bfloat16), "seq").astype(jnp.float32),
        lax.psum(totals[2].astype(jnp.bfloat16), "seq").astype(jnp.float32),
        lax.psum(totals[3].astype(jnp.bfloat16), "seq").astype(jnp.float32),
        lax.psum(totals[4].astype(jnp.bfloat16), "seq").astype(jnp.float32),
        lax.psum(totals[5].astype(jnp.bfloat16), "seq").astype(jnp.float32),
        lax.psum(totals[6].astype(jnp.bfloat16), "seq").astype(jnp.float32),
        lax.psum(totals[7].astype(jnp.bfloat16), "seq").astype(jnp.float32),
        lax.psum(totals[8].astype(jnp.bfloat16), "seq").astype(jnp.float32),
        lax.psum(totals[9].astype(jnp.bfloat16), "seq").astype(jnp.float32),
        lax.psum(totals[10].astype(jnp.bfloat16), "seq").astype(jnp.float32),
        lax.psum(totals[11].astype(jnp.bfloat16), "seq").astype(jnp.float32),
        lax.psum(totals[12].astype(jnp.bfloat16), "seq").astype(jnp.float32),
        lax.psum(totals[13].astype(jnp.bfloat16), "seq").astype(jnp.float32),
    )
    layer_outputs = jnp.stack(
        [
            jnp.where(is_first, section_outputs[batch_index], section_outputs[batch_index + 1])
            for batch_index in range(micro_count)
        ]
    )[None]
    input_grads = jnp.stack(
        [
            jnp.where(
                is_first,
                input_parts[micro_count - batch_index],
                input_parts[micro_count - 1 - batch_index],
            )
            for batch_index in range(micro_count)
        ]
    )[None]
    return (
        layer_outputs,
        input_grads,
        summed[0][None],
        summed[1][None],
        summed[2][None],
        summed[3][None],
        summed[4][None],
        summed[5][None],
        summed[6][None],
        summed[7][None],
        summed[8][None],
        summed[9][None],
        summed[10][None],
        summed[11][None],
        summed[12][None],
        summed[13][None],
    )


def solution(mesh):
    in_specs = (
        P(None, "seq", None),
        P(None, "seq", None),
        P("section", None),
        P("section", None, "head"),
        P("section", None, "head"),
        P("section", None, None),
        P("section", None, "head"),
        P("section", None, "head"),
        P("section", "head"),
        P("section", None, None),
        P("section", None),
        P("section", "head"),
        P("section", "head"),
        P("section", "head"),
        P("section", "head"),
        P("section", "head", None),
    )
    out_specs = (
        P("section", None, "seq", None),
        P("section", None, "seq", None),
        P("section", None),
        P("section", None, "head"),
        P("section", None, "head"),
        P("section", None, None),
        P("section", None, "head"),
        P("section", None, "head"),
        P("section", "head"),
        P("section", None, None),
        P("section", None),
        P("section", "head"),
        P("section", "head"),
        P("section", "head"),
        P("section", "head"),
        P("section", "head", None),
    )
    return jax.shard_map(
        on_device, mesh=mesh, in_specs=in_specs, out_specs=out_specs, check_vma=False
    )
```

profile of v0, /device:TPU:0, one launch (start us, length us, event | category | flops | bytes accessed | tf_op | source)
XLA Modules:
  0.0 2321.1 jit_solution(2029596629575149443)
XLA Ops:
  37.7 9.6 all-gather.28
  47.3 9.5 all-gather.15
  59.6 12.4 all-gather.59.cloned.1.call-done
  71.9 9.3 while.224
  91.5 18.6 all-gather.41.cloned.1.call-done
  110.1 9.2 while.215
  133.2 9.8 psum.378
  147.3 58.0 %all-reduce.140.cloned.1.call-done = f32[256,1536]{1,0:T(8,128)} async-done(((f32[256,1536]{1,0:T(8,128)}), f32[256,1536]{1,0:T(8,128)}) %all-reduce.140.cloned.1.call-update) | async-done | bytes 1572880 | tf_op jit(solution)/shard_map/psum | solution.py:177
  254.2 9.0 all-gather.26
  263.2 10.0 all-gather.16
  275.2 11.9 all-gather.57.cloned.1.call-done
  287.1 9.3 while.223
  307.0 18.2 all-gather.43.cloned.1.call-done
  325.2 9.3 while.216
  348.6 9.8 psum.380
  362.8 58.0 %all-reduce.142.cloned.1.call-done = f32[256,1536]{1,0:T(8,128)} async-done(((f32[256,1536]{1,0:T(8,128)}), f32[256,1536]{1,0:T(8,128)}) %all-reduce.142.cloned.1.call-update) | async-done | bytes 1572880 | tf_op jit(solution)/shard_map/psum | solution.py:177
  453.0 8.7 all-gather.24
  461.7 9.8 all-gather.17
  473.5 12.5 all-gather.55.cloned.1.call-done
  486.0 10.5 while.222
  506.9 17.1 all-gather.45.cloned.1.call-done
  524.1 10.5 while.217
  549.0 9.8 psum.382
  563.2 58.0 %all-reduce.144.cloned.1.call-done = f32[256,1536]{1,0:T(8,128)} async-done(((f32[256,1536]{1,0:T(8,128)}), f32[256,1536]{1,0:T(8,128)}) %all-reduce.144.cloned.1.call-update) | async-done | bytes 1572880 | tf_op jit(solution)/shard_map/psum | solution.py:177
  670.5 8.8 all-gather.22
  679.4 9.4 all-gather.18
  690.8 12.7 all-gather.53.cloned.1.call-done
  703.5 12.6 while.221
  726.7 14.4 all-gather.47.cloned.1.call-done
  741.1 12.5 while.218
  768.1 9.8 psum.384
  782.2 58.1 %all-reduce.146.cloned.1.call-done = f32[256,1536]{1,0:T(8,128)} async-done(((f32[256,1536]{1,0:T(8,128)}), f32[256,1536]{1,0:T(8,128)}) %all-reduce.146.cloned.1.call-update) | async-done | bytes 1572880 | tf_op jit(solution)/shard_map/psum | solution.py:177
  898.5 9.8 all-gather.20
  908.4 9.1 all-gather.19
  922.3 10.6 while.220
  943.4 16.3 all-gather.49.cloned.1.call-done
  959.7 10.5 while.219
  984.5 10.5 psum.388
  1021.1 16.9 all-gather.6
  1097.8 17.1 all-reduce.150.cloned.1.call-done
  1127.5 48.7 %all-reduce.152.cloned.1.call-done = bf16[256,1536]{1,0:T(8,128)(2,1)} async-done(((bf16[256,1536]{1,0:T(8,128)(2,1)}), bf16[256,1536]{1,0:T(8,128)(2,1)}) %all-reduce.152.cloned.1.call-update) | async-done | bytes 786448 | tf_op jit(solution)/shard_map/psum | solution.py:224
  1183.3 10.8 all-gather.29
  1203.2 9.5 all-gather.25
  1227.5 9.5 all-reduce.118
  1248.8 16.5 all-gather.8
  1323.5 18.2 all-reduce.154.cloned.1.call-done
  1366.0 36.9 %all-reduce.156.cloned.1.call-done = bf16[256,1536]{1,0:T(8,128)(2,1)} async-done(((bf16[256,1536]{1,0:T(8,128)(2,1)}), bf16[256,1536]{1,0:T(8,128)(2,1)}) %all-reduce.156.cloned.1.call-update) | async-done | bytes 786448 | tf_op jit(solution)/shard_map/psum | solution.py:224
  1420.3 9.5 all-reduce.117
  1441.5 19.8 all-gather.10
  1504.5 31.3 %all-reduce.158.cloned.1.call-done = bf16[259,256]{1,0:T(8,128)(2,1)} async-done(((bf16[259,256]{1,0:T(8,128)(2,1)}), bf16[259,256]{1,0:T(8,128)(2,1)}) %all-reduce.158.cloned.1.call-update) | async-done | bytes 132624 | tf_op jit(solution)/shard_map/psum | solution.py:206
  1553.9 41.3 %all-reduce.160.cloned.1.call-done = bf16[256,1536]{1,0:T(8,128)(2,1)} async-done(((bf16[256,1536]{1,0:T(8,128)(2,1)}), bf16[256,1536]{1,0:T(8,128)(2,1)}) %all-reduce.160.cloned.1.call-update) | async-done | bytes 786448 | tf_op jit(solution)/shard_map/psum | solution.py:224
  1610.5 9.5 all-reduce.116
  1630.6 19.8 all-gather.12
  1686.1 31.9 %all-reduce.162.cloned.1.call-done = bf16[259,256]{1,0:T(8,128)(2,1)} async-done(((bf16[259,256]{1,0:T(8,128)(2,1)}), bf16[259,256]{1,0:T(8,128)(2,1)}) %all-reduce.162.cloned.1.call-update) | async-done | bytes 132624 | tf_op jit(solution)/shard_map/psum | solution.py:206
  1738.4 39.1 %all-reduce.164.cloned.1.call-done = bf16[256,1536]{1,0:T(8,128)(2,1)} async-done(((bf16[256,1536]{1,0:T(8,128)(2,1)}), bf16[256,1536]{1,0:T(8,128)(2,1)}) %all-reduce.164.cloned.1.call-update) | async-done | bytes 786448 | tf_op jit(solution)/shard_map/psum | solution.py:224
  1792.2 9.5 all-reduce.115
  1812.3 19.8 all-gather.14
  1867.6 32.0 %all-reduce.166.cloned.1.call-done = bf16[259,256]{1,0:T(8,128)(2,1)} async-done(((bf16[259,256]{1,0:T(8,128)(2,1)}), bf16[259,256]{1,0:T(8,128)(2,1)}) %all-reduce.166.cloned.1.call-update) | async-done | bytes 132624 | tf_op jit(solution)/shard_map/psum | solution.py:206
  1916.0 9.9 fusion.84
  1926.0 10.3 fusion.75
  1948.8 16.8 all-reduce.120
  1971.7 18.6 all-reduce.121
  2000.5 23.3 %all-reduce.148.cloned.1.call-done = f32[256,1536]{1,0:T(8,128)} async-done(((f32[256,1536]{1,0:T(8,128)}), f32[256,1536]{1,0:T(8,128)}) %all-reduce.148.cloned.1.call-update) | async-done | bytes 1572880 | tf_op jit(solution)/shard_map/psum | solution.py:177
  2028.0 274.5 %all-reduce.170.cloned.1.call-done = (bf16[1,1536,768]{2,1,0:T(8,128)(2,1)}, bf16[1,1536,768]{2,1,0:T(8,128)(2,1)}, bf16[1,1536,256]{2,1,0:T(8,128)(2,1)}, bf16[1,768,1536]{2,1,0:T(8,128)(2,1)}) async-done(((bf16[1,1536,768]{2,1,0:T(8,128)(2,1)}, bf16[1,1536,768]{2,1,0:T(8,128)(2,1)}, bf16[1,1536,256]{2,1,0:T(8,128)(2,1)}, bf16[1,768,1536]{2,1,0:T(8,128)(2,1)}), (bf16[1,1536,768]{2,1,0:T(8,128)(2,1)}, ...) | async-done | bytes 7864336 | tf_op jit(solution)/shard_map/psum | solution.py:325
  (1811 shorter events, 1019.0 us)
Async XLA Ops:
  7.2 121.9 %copy-start = (bf16[1,1536,768]{2,1,0:T(8,128)(2,1)S(1)}, bf16[1,1536,768]{2,1,0:T(8,128)(2,1)}, u32[]{:S(2)}) copy-start(bf16[1,1536,768]{2,1,0:T(8,128)(2,1)} %param.50) | copy-start | bytes 7077892
  7.2 64.7 %all-gather.59.cloned.1.call-start = ((), (), s32[]{:S(2)}) async-start(), calls=%async_computation.24 | async-start | bytes 1966080 | tf_op jit(solution)/shard_map/all_gather | solution.py:18
  15.2 10.9 collective-permute-start
  34.4 75.7 %all-gather.41.cloned.1.call-start = ((), (), s32[]{:S(2)}) async-start(), calls=%async_computation.15 | async-start | bytes 1966080 | tf_op jit(solution)/shard_map/all_gather | solution.py:18
  36.9 168.4 %all-reduce.140.cloned.1.call-start = ((), (), s32[]{:S(2)}) async-start(), calls=%async_computation | async-start | bytes 3145728 | tf_op jit(solution)/shard_map/psum | solution.py:177
  147.3 139.9 %all-gather.57.cloned.1.call-start = ((), (), s32[]{:S(2)}) async-start(), calls=%async_computation.23 | async-start | bytes 1966080 | tf_op jit(solution)/shard_map/all_gather | solution.py:18
  207.1 3.8 collective-permute-start.1
  212.4 208.3 %copy-start.19 = (bf16[256,1536]{1,0:T(8,128)(2,1)}, bf16[256,1536]{1,0:T(8,128)(2,1)S(1)}, u32[]{:S(2)}) copy-start(bf16[256,1536]{1,0:T(8,128)(2,1)S(1)} %get-tuple-element.2026) | copy-start | bytes 2359300
  216.9 25.6 %collective-permute-start.2 = (bf16[3,1024]{1,0:T(4,128)(2,1)}, bf16[3,1024]{1,0:T(4,128)(2,1)}, u32[]{:S(2)}, u32[]{:S(2)}) collective-permute-start(bf16[3,1024]{1,0:T(4,128)(2,1)} %pad_maximum_fusion.8), channel_id=1, source_target_pairs={{0,4},{4,8},{8,12},{1,5},{5,9},{9,13},{2,6},{6,10},{10,14},{3,7},{... | collective-permute-start | bytes 18440 | tf_op jit(solution)/shard_map/ppermute | solution.py:13
  251.3 73.9 %all-gather.43.cloned.1.call-start = ((), (), s32[]{:S(2)}) async-start(), calls=%async_computation.16 | async-start | bytes 1966080 | tf_op jit(solution)/shard_map/all_gather | solution.py:18
  254.1 166.7 %all-reduce.142.cloned.1.call-start = ((), (), s32[]{:S(2)}) async-start(), calls=%async_computation.1 | async-start | bytes 3145728 | tf_op jit(solution)/shard_map/psum | solution.py:177
  362.7 123.2 %all-gather.55.cloned.1.call-start = ((), (), s32[]{:S(2)}) async-start(), calls=%async_computation.22 | async-start | bytes 1966080 | tf_op jit(solution)/shard_map/all_gather | solution.py:18
  423.6 3.5 collective-permute-start.3
  432.3 8.2 collective-permute-start.4
  450.2 73.9 %all-gather.45.cloned.1.call-start = ((), (), s32[]{:S(2)}) async-start(), calls=%async_computation.17 | async-start | bytes 1966080 | tf_op jit(solution)/shard_map/all_gather | solution.py:18
  452.9 168.3 %all-reduce.144.cloned.1.call-start = ((), (), s32[]{:S(2)}) async-start(), calls=%async_computation.2 | async-start | bytes 3145728 | tf_op jit(solution)/shard_map/psum | solution.py:177
  563.1 140.3 %all-gather.53.cloned.1.call-start = ((), (), s32[]{:S(2)}) async-start(), calls=%async_computation.21 | async-start | bytes 1966080 | tf_op jit(solution)/shard_map/all_gather | solution.py:18
  624.3 3.5 collective-permute-start.5
  633.1 26.8 %copy-start.249 = (f32[768]{0:T(1024)S(1)}, f32[768]{0:T(1024)}, u32[]{:S(2)}) copy-start(f32[768]{0:T(1024)} %copy-done.247) | copy-start | bytes 9220
  633.8 25.0 %collective-permute-start.6 = (bf16[3,1024]{1,0:T(4,128)(2,1)}, bf16[3,1024]{1,0:T(4,128)(2,1)}, u32[]{:S(2)}, u32[]{:S(2)}) collective-permute-start(bf16[3,1024]{1,0:T(4,128)(2,1)} %pad_maximum_fusion.6), channel_id=1, source_target_pairs={{0,4},{4,8},{8,12},{1,5},{5,9},{9,13},{2,6},{6,10},{10,14},{3,7},{... | collective-permute-start | bytes 18440 | tf_op jit(solution)/shard_map/ppermute | solution.py:13
  647.1 70.8 %copy-start.186 = (f32[2,8,2,128]{3,1,2,0:T(8,128)}, f32[2,8,2,128]{3,1,2,0:T(8,128)S(1)}, u32[]{:S(2)}) copy-start(f32[2,8,2,128]{3,1,2,0:T(8,128)S(1)} %copy.423) | copy-start | bytes 49156
  667.7 73.4 %all-gather.47.cloned.1.call-start = ((), (), s32[]{:S(2)}) async-start(), calls=%async_computation.18 | async-start | bytes 1966080 | tf_op jit(solution)/shard_map/all_gather | solution.py:18
  670.5 169.8 %all-reduce.146.cloned.1.call-start = ((), (), s32[]{:S(2)}) async-start(), calls=%async_computation.3 | async-start | bytes 3145728 | tf_op jit(solution)/shard_map/psum | solution.py:177
  782.1 140.2 %all-gather.51.cloned.1.call-start = ((), (), s32[]{:S(2)}) async-start(), calls=%async_computation.20 | async-start | bytes 1966080 | tf_op jit(solution)/shard_map/all_gather | solution.py:18
  843.4 3.4 collective-permute-start.7
  850.8 26.7 %collective-permute-start.8 = (bf16[3,1024]{1,0:T(4,128)(2,1)}, bf16[3,1024]{1,0:T(4,128)(2,1)}, u32[]{:S(2)}, u32[]{:S(2)}) collective-permute-start(bf16[3,1024]{1,0:T(4,128)(2,1)} %pad_maximum_fusion.5), channel_id=1, source_target_pairs={{0,4},{4,8},{8,12},{1,5},{5,9},{9,13},{2,6},{6,10},{10,14},{3,7},{... | collective-permute-start | bytes 18440 | tf_op jit(solution)/shard_map/ppermute | solution.py:13
  886.4 73.2 %all-gather.49.cloned.1.call-start = ((), (), s32[]{:S(2)}) async-start(), calls=%async_computation.19 | async-start | bytes 1966080 | tf_op jit(solution)/shard_map/all_gather | solution.py:18
  889.2 225.8 %all-reduce.150.cloned.1.call-start = ((), (), s32[]{:S(2)}) async-start(), calls=%async_computation.5 | async-start | bytes 270336 | tf_op jit(solution)/shard_map/psum | solution.py:206
  1076.0 100.2 %all-reduce.152.cloned.1.call-start = ((), (), s32[]{:S(2)}) async-start(), calls=%async_computation.6 | async-start | bytes 1572864 | tf_op jit(solution)/shard_map/psum | solution.py:224
  1116.8 5.6 collective-permute-start.9
  1126.2 50.1 %copy-start.332 = (f32[256]{0:T(256)S(1)}, f32[256]{0:T(256)}, u32[]{:S(2)}) copy-start(f32[256]{0:T(256)} %copy-done.330) | copy-start | bytes 3076
  1127.5 214.2 %all-reduce.154.cloned.1.call-start = ((), (), s32[]{:S(2)}) async-start(), calls=%async_computation.7 | async-start | bytes 270336 | tf_op jit(solution)/shard_map/psum | solution.py:206
  1181.8 41.1 %collective-permute-start.10 = (bf16[256,1536]{1,0:T(8,128)(2,1)}, bf16[256,1536]{1,0:T(8,128)(2,1)}, u32[]{:S(2)}, u32[]{:S(2)}) collective-permute-start(bf16[256,1536]{1,0:T(8,128)(2,1)} %fusion.211), channel_id=1, source_target_pairs={{16,0},{17,1},{18,2},{19,3},{20,4},{21,5},{22,6},{23,7},{24,8},{25... | collective-permute-start | bytes 2359304 | tf_op jit(solution)/shard_map/ppermute | solution.py:13
  1302.8 100.1 %all-reduce.156.cloned.1.call-start = ((), (), s32[]{:S(2)}) async-start(), calls=%async_computation.8 | async-start | bytes 1572864 | tf_op jit(solution)/shard_map/psum | solution.py:224
  1321.4 23.8 %copy-start.310 = (f32[12]{0:T(128)S(1)}, f32[12]{0:T(128)}, u32[]{:S(2)}) copy-start(f32[12]{0:T(128)} %copy-done.305) | copy-start | bytes 148
  1343.5 5.6 collective-permute-start.11
  1354.2 181.6 %all-reduce.158.cloned.1.call-start = ((), (), s32[]{:S(2)}) async-start(), calls=%async_computation.9 | async-start | bytes 270336 | tf_op jit(solution)/shard_map/psum | solution.py:206
  1362.9 40.0 %copy-start.327 = (f32[256]{0:T(256)S(1)}, f32[256]{0:T(256)}, u32[]{:S(2)}) copy-start(f32[256]{0:T(256)} %copy-done.325) | copy-start | bytes 3076
  1366.0 40.1 %copy-start.424 = (f32[256]{0:T(256)S(1)}, f32[256]{0:T(256)}, u32[]{:S(2)}) copy-start(f32[256]{0:T(256)} %get-tuple-element.2128) | copy-start | bytes 3076
  1409.0 8.8 collective-permute-start.12
  1496.9 98.3 %all-reduce.160.cloned.1.call-start = ((), (), s32[]{:S(2)}) async-start(), calls=%async_computation.10 | async-start | bytes 1572864 | tf_op jit(solution)/shard_map/psum | solution.py:224
  1536.9 5.6 collective-permute-start.13
  1546.4 171.6 %all-reduce.162.cloned.1.call-start = ((), (), s32[]{:S(2)}) async-start(), calls=%async_computation.11 | async-start | bytes 270336 | tf_op jit(solution)/shard_map/psum | solution.py:206
  1550.7 44.5 %copy-start.23 = (bf16[256,1536]{1,0:T(8,128)(2,1)S(1)}, bf16[256,1536]{1,0:T(8,128)(2,1)}, u32[]{:S(2)}) copy-start(bf16[256,1536]{1,0:T(8,128)(2,1)} %copy-done.22) | copy-start | bytes 2359300
  1550.7 44.5 %copy-start.320 = (f32[256]{0:T(256)S(1)}, f32[256]{0:T(256)}, u32[]{:S(2)}) copy-start(f32[256]{0:T(256)} %copy-done.318) | copy-start | bytes 3076
  1599.9 8.2 collective-permute-start.14
  1628.5 21.9 copy-start.469
  1679.2 98.3 %all-reduce.164.cloned.1.call-start = ((), (), s32[]{:S(2)}) async-start(), calls=%async_computation.12 | async-start | bytes 1572864 | tf_op jit(solution)/shard_map/psum | solution.py:224
  1684.9 35.7 %copy-start.311 = (f32[12]{0:T(128)S(1)}, f32[12]{0:T(128)}, u32[]{:S(2)}) copy-start(f32[12]{0:T(128)} %copy-done.305) | copy-start | bytes 148
  1684.9 35.7 %copy-start.406 = (f32[12]{0:T(128)S(1)}, f32[12]{0:T(128)}, u32[]{:S(2)}) copy-start(f32[12]{0:T(128)} %get-tuple-element.1747) | copy-start | bytes 148
  1719.2 5.6 collective-permute-start.15
  1728.7 170.9 %all-reduce.166.cloned.1.call-start = ((), (), s32[]{:S(2)}) async-start(), calls=%async_computation.13 | async-start | bytes 270336 | tf_op jit(solution)/shard_map/psum | solution.py:206
  1738.4 42.0 %copy-start.316 = (f32[256]{0:T(256)S(1)}, f32[256]{0:T(256)}, u32[]{:S(2)}) copy-start(f32[256]{0:T(256)} %copy-done.313) | copy-start | bytes 3076
  1738.4 42.0 %copy-start.418 = (f32[256]{0:T(256)S(1)}, f32[256]{0:T(256)}, u32[]{:S(2)}) copy-start(f32[256]{0:T(256)} %get-tuple-element.2120) | copy-start | bytes 3076
  1782.2 7.6 collective-permute-start.16
  1810.2 21.9 copy-start.468
  1860.7 107.0 %all-reduce.168.cloned.1.call-start = ((), (), s32[]{:S(2)}) async-start(), calls=%async_computation.14 | async-start | bytes 1572864 | tf_op jit(solution)/shard_map/psum | solution.py:224
  1866.4 36.0 %copy-start.312 = (f32[12]{0:T(128)S(1)}, f32[12]{0:T(128)}, u32[]{:S(2)}) copy-start(f32[12]{0:T(128)} %copy-done.305) | copy-start | bytes 148
  1900.7 5.6 collective-permute-start.17
  1910.3 113.5 %all-reduce.148.cloned.1.call-start = ((), (), s32[]{:S(2)}) async-start(), calls=%async_computation.4 | async-start | bytes 3145728 | tf_op jit(solution)/shard_map/psum | solution.py:177
  1915.9 386.6 %all-reduce.170.cloned.1.call-start = ((), (), s32[]{:S(2)}) async-start(), calls=%async_computation.25 | async-start | bytes 15728640 | tf_op jit(solution)/shard_map/psum | solution.py:325
  1967.7 28.3 %copy-start.109 = (bf16[256,1536]{1,0:T(8,128)(2,1)S(1)}, bf16[256,1536]{1,0:T(8,128)(2,1)}, u32[]{:S(2)}) copy-start(bf16[256,1536]{1,0:T(8,128)(2,1)} %copy-done.108) | copy-start | bytes 2359300
  1967.7 28.3 %copy-start.447 = (f32[256]{0:T(256)S(1)}, f32[256]{0:T(256)}, u32[]{:S(2)}) copy-start(f32[256]{0:T(256)} %get-tuple-element.2116) | copy-start | bytes 3076
  1998.6 25.2 %copy-start.34 = (bf16[256,1536]{1,0:T(8,128)(2,1)S(1)}, bf16[256,1536]{1,0:T(8,128)(2,1)}, u32[]{:S(2)}) copy-start(bf16[256,1536]{1,0:T(8,128)(2,1)} %copy-done.30) | copy-start | bytes 2359300
  (486 other events, 2104.1 us)
Sparse Core Ops, SparseCore 0:
  34.5 37.3 all-gather.58
  74.1 35.9 all-gather.40
  147.4 57.8 all-reduce.139
  251.5 35.6 all-gather.56
  289.2 35.9 all-gather.42
  362.8 57.8 all-reduce.141
  450.3 35.6 all-gather.54
  488.1 35.9 all-gather.44
  563.3 57.8 all-reduce.143
  667.8 35.6 all-gather.52
  705.1 35.9 all-gather.46
  782.2 57.9 all-reduce.145
  886.6 35.6 all-gather.50
  923.7 35.9 all-gather.48
  1076.1 38.8 all-reduce.149
  1127.6 48.5 all-reduce.151
  1302.9 38.6 all-reduce.153
  1354.3 48.5 all-reduce.155
  1497.1 38.6 all-reduce.157
  1546.6 48.5 all-reduce.159
  1679.3 38.6 all-reduce.161
  1728.9 48.5 all-reduce.163
  1860.9 38.7 all-reduce.165
  1910.4 48.7 all-reduce.167
  1962.9 60.8 all-reduce.147
  2027.6 274.7 all-reduce.169
where the time goes:
time: 2340 us; the launch traced here: 2320 us
  waiting for transfers between devices  983 us (42%)
  matrix products  411 us (18%)
  blocking collectives  362 us (15%)
  other arithmetic  320 us (14%)
  local copies, waits for them, and re-layouts  180 us (8%)
  starting transfers between devices  42.6 us (2%)
    psum x1, waiting for transfers between devices, on_device(): lax.psum(totals[1].astype(jnp.bfloat16), 'seq').astype(jnp.float32)  274 us
    psum x5, waiting for transfers between devices, forward_layer(): branch = lax.psum(matmul(kept['normed_gate'], params['w_out']), 'head')  255 us
    psum x5, waiting for transfers between devices, backward_layer(): lax.psum(partial_in.astype(jnp.bfloat16), 'head').astype(jnp.float32)  166 us
    all_gather x10, waiting for transfers between devices, entering(): everything = jax.tree.map(lambda part: lax.all_gather(part, axis), value)  137 us
    all_gather x10, blocking collectives, prefix(): lax.all_gather(a.astype(kind), axis)  137 us
    psum x5, waiting for transfers between devices, backward_layer(): lax.psum(d_extended[:, local_width:].astype(jnp.bfloat16), 'head')  131 us
    dot_general x20, matrix products, part_output(): within = jnp.einsum('tsh,shp->thp', weights, x_heads, precision=PRECISION)  108 us
    all_gather x10, blocking collectives, entering(): everything = jax.tree.map(lambda part: lax.all_gather(part, axis), value)  93.7 us
  transfers between devices with their start and end apart: 44, of which 34 were waited for; matrix products, arithmetic and copies ran while one was open for 17% of the time, Pallas kernels for 0%

commit v1 on v0

v1 whole, which is shorter than its diff:
```python
import functools

import jax
import jax.numpy as jnp
from jax import lax
from jax.experimental import pallas as pl
from jax.experimental.pallas import tpu as pltpu
from jax.sharding import PartitionSpec as P

EPSILON = 1e-05
MESH = pl.DeviceIdType.MESH
HIGH = lax.Precision.HIGHEST
BF = jnp.bfloat16
F32 = jnp.float32
LANES = 128
VMEM_LIMIT = 56 * 2**20


def shape(dims, kind):
    return jax.ShapeDtypeStruct(dims, kind)


def dot(a, b, dims=((1,), (0,)), precision=None):
    return lax.dot_general(a, b, (dims, ((), ())), precision=precision, preferred_element_type=F32)


NT = ((1,), (1,))
TN = ((0,), (0,))


def head_mask(width, heads):
    size = width // heads
    return (
        lax.broadcasted_iota(jnp.int32, (LANES, width), 0)
        == lax.broadcasted_iota(jnp.int32, (LANES, width), 1) // size
    ).astype(F32)


def order_mask(n, lower):
    rows = lax.broadcasted_iota(jnp.int32, (n, n), 0)
    columns = lax.broadcasted_iota(jnp.int32, (n, n), 1)
    return (rows >= columns) if lower else (rows <= columns)


def sigmoid(v):
    return 1.0 / (1.0 + jnp.exp(-v))


def softplus(v):
    return jnp.maximum(v, 0.0) + jnp.log1p(jnp.exp(-jnp.abs(v)))


def column(row_block):
    n = row_block.shape[1]
    return [
        jnp.transpose(jnp.broadcast_to(row_block[i : i + 1, :], (LANES, n))) for i in range(2)
    ]


def rows_of(columns):
    n = columns[0].shape[0]
    rows = [jnp.transpose(jnp.broadcast_to(c, (n, LANES)))[0:1] for c in columns]
    return jnp.concatenate(rows + [jnp.zeros((8 - len(rows), n), F32)], axis=0)


def conv_pre(ext, proj_xbc, halo, taps, bias):
    n = proj_xbc.shape[0]
    ext[0:8, :] = halo
    ext[8 : 8 + n, :] = proj_xbc
    pre = bias + taps[3:4, :] * proj_xbc
    for k in range(3):
        pre = pre + taps[k : k + 1, :] * ext[5 + k : 5 + k + n, :]
    return pre


def ssd_fwd1_kernel(dims, proj, halo, taps, bias, dt_bias, a_neg, cx, dt_o, cum_o, state, decay, ext):
    heads, inner, states = dims
    n = proj.shape[1]
    wide = inner + 2 * states
    xbc = proj[0, :, inner : inner + wide].astype(BF).astype(F32)
    pre = conv_pre(ext, xbc, halo[0].astype(F32), taps[...], bias[...])
    act = pre * sigmoid(pre)
    cx[0] = act
    dt = softplus(proj[0, :, inner + wide :] + dt_bias[...])
    cum = dot(order_mask(n, True).astype(F32), dt * a_neg[...], precision=HIGH)
    dt_o[0] = dt
    cum_o[0] = cum
    last = cum[n - 1 : n, :]
    expand = head_mask(inner, heads)
    weight = dot(jnp.exp(last - cum) * dt, expand, precision=HIGH)
    state[0] = dot(act[:, inner : inner + states].astype(BF), (act[:, :inner] * weight).astype(BF), TN)
    decay[0] = dot(jnp.broadcast_to(jnp.exp(last), (8, LANES)), expand, precision=HIGH)


def ssd_fwd1(proj, halo, taps, bias, dt_bias, a_neg, dims):
    heads, inner, states = dims
    batch, n, _ = proj.shape
    wide = inner + 2 * states
    block = lambda *s: pl.BlockSpec((1,) + s, lambda i: (i, 0, 0))
    whole = lambda a: pl.BlockSpec(a.shape, lambda i: (0, 0))
    return pl.pallas_call(
        functools.partial(ssd_fwd1_kernel, dims),
        grid=(batch,),
        out_shape=(
            shape((batch, n, wide), F32),
            shape((batch, n, LANES), F32),
            shape((batch, n, LANES), F32),
            shape((batch, states, inner), F32),
            shape((batch, 8, inner), F32),
        ),
        in_specs=[
            block(n, proj.shape[2]),
            block(8, wide),
            whole(taps),
            whole(bias),
            whole(dt_bias),
            whole(a_neg),
        ],
        out_specs=(
            block(n, wide),
            block(n, LANES),
            block(n, LANES),
            block(states, inner),
            block(8, inner),
        ),
        scratch_shapes=[pltpu.VMEM((n + 8, wide), F32)],
        compiler_params=pltpu.CompilerParams(vmem_limit_bytes=VMEM_LIMIT),
        name="ssd_fwd1",
    )(proj, halo, taps, bias, dt_bias, a_neg)


def ssd_fwd2_kernel(dims, cx, dt, cum, state, proj, skip, gain, dyn, y_o, gg_o, ssq_o):
    heads, inner, states = dims
    n = cx.shape[1]
    size = inner // heads
    expand = head_mask(inner, heads)
    x = cx[0, :, :inner]
    b = cx[0, :, inner : inner + states].astype(BF)
    c = cx[0, :, inner + states :].astype(BF)
    scores = dot(c, b, NT)
    cums = cum[0]
    cums_t = jnp.transpose(cums)
    dtx = (x * dot(dt[0], expand, precision=HIGH)).astype(BF)
    carried = dot(jnp.exp(cums), expand, precision=HIGH) * dot(c, state[0].astype(BF))
    base = carried + skip[...] * x
    keep = order_mask(n, True)
    first = lax.broadcasted_iota(jnp.int32, (n, LANES), 1) < size
    total = jnp.zeros((n, LANES), F32)
    across = jnp.zeros((n, LANES), F32)
    for p in range(heads // 2):
        lanes = slice(p * LANES, (p + 1) * LANES)
        both = []
        for h in (2 * p, 2 * p + 1):
            lag = jnp.where(keep, cums[:, h : h + 1] - cums_t[h : h + 1, :], -1e30)
            both.append(dot((scores * jnp.exp(lag)).astype(BF), dtx[:, lanes]))
        y = base[:, lanes] + jnp.where(first, both[0], both[1])
        y_o[0, :, lanes] = y
        z = proj[0, :, lanes]
        gated = y * z * sigmoid(z)
        scaled = gated * gain[:, lanes]
        gg_o[0, :, lanes] = scaled.astype(BF)
        total = total + gated * gated
        if dyn is not None:
            across = across + scaled * dyn[0, :, lanes]
    ssq_o[0] = rows_of([jnp.sum(total, axis=1, keepdims=True), jnp.sum(across, axis=1, keepdims=True)])


def ssd_fwd2(cx, dt, cum, state, proj, skip, gain, dyn, dims):
    heads, inner, states = dims
    batch, n, wide = cx.shape
    block = lambda *s: pl.BlockSpec((1,) + s, lambda i: (i, 0, 0))
    whole = lambda a: pl.BlockSpec(a.shape, lambda i: (0, 0))
    return pl.pallas_call(
        functools.partial(ssd_fwd2_kernel, dims)
        if dyn is not None
        else lambda *refs: ssd_fwd2_kernel(dims, *refs[:7], None, *refs[7:]),
        grid=(batch,),
        out_shape=(
            shape((batch, n, inner), F32),
            shape((batch, n, inner), BF),
            shape((batch, 8, n), F32),
        ),
        in_specs=[
            block(n, wide),
            block(n, LANES),
            block(n, LANES),
            block(states, inner),
            block(n, inner),
            whole(skip),
            whole(gain),
        ]
        + ([block(n, inner)] if dyn is not None else []),
        out_specs=(block(n, inner), block(n, inner), block(8, n)),
        compiler_params=pltpu.CompilerParams(vmem_limit_bytes=VMEM_LIMIT),
        name="ssd_fwd2",
    )(cx, dt, cum, state, proj, skip, gain, *([dyn] if dyn is not None else []))


def ssd_bwd1_kernel(dims, full, dyn, y, proj, cx, cum, gs, across, gain, dy_o, dz_o, yn_o, ggg_o, state_o):
    heads, inner, states = dims
    n = dyn.shape[1]
    expand = head_mask(inner, heads)
    gs_c = jnp.concatenate([column(gs[i])[0] for i in range(gs.shape[0])], axis=0)[:, 0:1]
    ac_c = jnp.concatenate([column(across[i])[1] for i in range(gs.shape[0])], axis=0)[:, 0:1]
    z = proj[0]
    sig = sigmoid(z)
    yv = y[0]
    gated = yv * z * sig
    dynv = dyn[0]
    scaled = gated * gs_c
    ggg_o[0] = jnp.broadcast_to(jnp.sum(dynv * scaled, axis=0, keepdims=True), (8, inner))
    yn_o[0] = (scaled * gain[...]).astype(BF)
    dgated = gs_c * gain[...] * dynv - gated * (gs_c * gs_c * gs_c * ac_c / full)
    dy = dgated * z * sig
    dy_o[0] = dy
    dz_o[0] = (dgated * yv * sig * (1.0 + z * (1.0 - sig))).astype(BF)
    moved = dot(jnp.exp(cum[0]), expand, precision=HIGH) * dy
    state_o[0] = dot(cx[0, :, inner + states :].astype(BF), moved.astype(BF), TN)


def ssd_bwd1(dyn, y, proj, cx, cum, stats_gs, stats_across, gain, dims, full):
    heads, inner, states = dims
    batch, n, wide = cx.shape
    per = stats_gs.shape[0] // batch
    block = lambda *s: pl.BlockSpec((1,) + s, lambda i: (i, 0, 0))
    whole = lambda a: pl.BlockSpec(a.shape, lambda i: (0, 0))
    chunk = pl.BlockSpec((per,) + stats_gs.shape[1:], lambda i: (i, 0, 0))
    return pl.pallas_call(
        functools.partial(ssd_bwd1_kernel, dims, full),
        grid=(batch,),
        out_shape=(
            shape((batch, n, inner), F32),
            shape((batch, n, inner), BF),
            shape((batch, n, inner), BF),
            shape((batch, 8, inner), F32),
            shape((batch, states, inner), F32),
        ),
        in_specs=[
            block(n, inner),
            block(n, inner),
            block(n, inner),
            block(n, wide),
            block(n, LANES),
            chunk,
            chunk,
            whole(gain),
        ],
        out_specs=(block(n, inner), block(n, inner), block(n, inner), block(8, inner), block(states, inner)),
        compiler_params=pltpu.CompilerParams(vmem_limit_bytes=VMEM_LIMIT),
        name="ssd_bwd1",
    )(dyn, y, proj, cx, cum, stats_gs, stats_across, gain)


def ssd_bwd2_kernel(
    dims, dy, proj, halo, cx, dt, cum, state, later, taps, bias, dt_bias, a_neg, skip,
    dpre_o, gdt_o, conv_o, small_o, ext, rowq,
):
    heads, inner, states = dims
    n = dy.shape[1]
    size = inner // heads
    wide = inner + 2 * states
    expand = head_mask(inner, heads)
    x = cx[0, :, :inner]
    b = cx[0, :, inner : inner + states].astype(BF)
    c = cx[0, :, inner + states :].astype(BF)
    dyv = dy[0]
    dyb = dyv.astype(BF)
    dtv = dt[0]
    cums = cum[0]
    cums_t = jnp.transpose(cums)
    last = cums[n - 1 : n, :]
    dt_wide = dot(dtv, expand, precision=HIGH)
    dtx = (x * dt_wide).astype(BF)
    scores_t = dot(b, c, NT)
    keep = order_mask(n, False)
    lane = lax.broadcasted_iota(jnp.int32, (n, LANES), 1)
    first = lane < size
    rowq[...] = jnp.zeros_like(rowq)
    colq = jnp.zeros((n, LANES), F32)
    d_scores = jnp.zeros((n, n), F32)
    pieces = []
    for p in range(heads // 2):
        lanes = slice(p * LANES, (p + 1) * LANES)
        both = []
        for j, h in enumerate((2 * p, 2 * p + 1)):
            lag = jnp.where(keep, cums_t[h : h + 1, :] - cums[:, h : h + 1], -1e30)
            decays = jnp.exp(lag)
            weights = scores_t * decays
            mine = jnp.where(first if j == 0 else jnp.logical_not(first), dtx[:, lanes], jnp.zeros((), BF))
            d_weights = dot(mine, dyb[:, lanes], NT)
            q = d_weights * weights
            d_scores = d_scores + d_weights * decays
            rowq[h : h + 1, :] = jnp.sum(q, axis=0, keepdims=True)
            colq = colq + jnp.where(lane == h, jnp.sum(q, axis=1, keepdims=True), 0.0)
            both.append(dot(weights.astype(BF), dyb[:, lanes]))
        pieces.append(jnp.where(first, both[0], both[1]))
    dxw = jnp.concatenate(pieces, axis=1)
    state_b = state[0].astype(BF)
    later_b = later[0].astype(BF)
    ecum = dot(jnp.exp(cums), expand, precision=HIGH)
    moved = ecum * dyv
    carried = dot(c, state_b)
    tail = jnp.exp(last - cums)
    weight = tail * dtv
    weight_wide = dot(weight, expand, precision=HIGH)
    pulled = dot(b, later_b)
    dx = dt_wide * dxw + weight_wide * pulled + skip[...] * dyv
    fold = lambda v: dot(v, expand, NT, precision=HIGH)
    ddt = fold(x * dxw)
    dw = fold(x * pulled)
    wdw = weight * dw
    change = jnp.transpose(rowq[...]) + fold(carried * moved) - colq - wdw
    ends = jnp.sum(wdw, axis=0, keepdims=True) + jnp.exp(last) * fold(
        jnp.broadcast_to(
            jnp.sum(state_b.astype(F32) * later_b.astype(F32), axis=0, keepdims=True), (8, inner)
        )
    )[0:1]
    log_grad = dot(order_mask(n, False).astype(F32), change, precision=HIGH) + ends
    ddt = ddt + tail * dw + a_neg[...] * log_grad
    ddt_raw = ddt * sigmoid(proj[0, :, inner + wide :] + dt_bias[...])
    gdt_o[0] = ddt_raw.astype(BF)
    small_o[0] = jnp.concatenate(
        [
            jnp.sum(ddt_raw, axis=0, keepdims=True),
            jnp.sum(dtv * log_grad, axis=0, keepdims=True) * a_neg[...],
            jnp.sum(fold(x * dyv), axis=0, keepdims=True),
            jnp.zeros((5, LANES), F32),
        ],
        axis=0,
    )
    d_scores_b = d_scores.astype(BF)
    dc = dot(d_scores_b, b, TN) + dot(moved.astype(BF), state_b, NT)
    db = dot(d_scores_b, c) + dot((x * weight_wide).astype(BF), later_b, NT)
    xbc = proj[0, :, inner : inner + wide].astype(BF).astype(F32)
    pre = conv_pre(ext, xbc, halo[0].astype(F32), taps[...], bias[...])
    sig = sigmoid(pre)
    dpre = jnp.concatenate([dx, db, dc], axis=1) * sig * (1.0 + pre * (1.0 - sig))
    dpre_o[0] = dpre
    rows = [jnp.sum(dpre * ext[5 + k : 5 + k + n, :], axis=0, keepdims=True) for k in range(4)]
    rows.append(jnp.sum(dpre, axis=0, keepdims=True))
    conv_o[0] = jnp.concatenate(rows + [jnp.zeros((3, wide), F32)], axis=0)


def ssd_bwd2(dy, proj, halo, cx, dt, cum, state, later, taps, bias, dt_bias, a_neg, skip, dims):
    heads, inner, states = dims
    batch, n, wide = cx.shape
    block = lambda *s: pl.BlockSpec((1,) + s, lambda i: (i, 0, 0))
    whole = lambda a: pl.BlockSpec(a.shape, lambda i: (0, 0))
    return pl.pallas_call(
        functools.partial(ssd_bwd2_kernel, dims),
        grid=(batch,),
        out_shape=(
            shape((batch, n, wide), F32),
            shape((batch, n, LANES), BF),
            shape((batch, 8, wide), F32),
            shape((batch, 8, LANES), F32),
        ),
        in_specs=[
            block(n, inner),
            block(n, proj.shape[2]),
            block(8, wide),
            block(n, wide),
            block(n, LANES),
            block(n, LANES),
            block(states, inner),
            block(states, inner),
            whole(taps),
            whole(bias),
            whole(dt_bias),
            whole(a_neg),
            whole(skip),
        ],
        out_specs=(block(n, wide), block(n, LANES), block(8, wide), block(8, LANES)),
        scratch_shapes=[pltpu.VMEM((n + 8, wide), F32), pltpu.VMEM((LANES, n), F32)],
        compiler_params=pltpu.CompilerParams(vmem_limit_bytes=VMEM_LIMIT),
        name="ssd_bwd2",
    )(dy, proj, halo, cx, dt, cum, state, later, taps, bias, dt_bias, a_neg, skip)


def conv_bwd_kernel(dims, dpre, halo, dz, gdt, taps, out, ext):
    heads, inner, states = dims
    n = dpre.shape[1]
    wide = inner + 2 * states
    ext[0:n, :] = dpre[0]
    ext[n : n + 8, :] = halo[0]
    total = taps[3:4, :] * dpre[0]
    for k in range(3):
        total = total + taps[k : k + 1, :] * ext[3 - k : 3 - k + n, :]
    out[0, :, :inner] = dz[0]
    out[0, :, inner : inner + wide] = total.astype(BF)
    out[0, :, inner + wide :] = gdt[0]


def conv_bwd(dpre, halo, dz, gdt, taps, dims):
    heads, inner, states = dims
    batch, n, wide = dpre.shape
    block = lambda *s: pl.BlockSpec((1,) + s, lambda i: (i, 0, 0))
    return pl.pallas_call(
        functools.partial(conv_bwd_kernel, dims),
        grid=(batch,),
        out_shape=shape((batch, n, inner + wide + LANES), BF),
        in_specs=[
            block(n, wide),
            block(8, wide),
            block(n, inner),
            block(n, LANES),
            pl.BlockSpec(taps.shape, lambda i: (0, 0)),
        ],
        out_specs=block(n, inner + wide + LANES),
        scratch_shapes=[pltpu.VMEM((n + 8, wide), F32)],
        compiler_params=pltpu.CompilerParams(vmem_limit_bytes=VMEM_LIMIT),
        name="conv_bwd",
    )(dpre, halo, dz, gdt, taps)


def push(src, dst, send, recv, device):
    copy = pltpu.make_async_remote_copy(
        src_ref=src, dst_ref=dst, send_sem=send, recv_sem=recv, device_id=device, device_id_type=MESH
    )
    copy.start()
    return copy


def both_layers_kernel(places, *refs):
    count = len(places)
    ins, outs = refs[:count], refs[count:-3]
    send, recv, local = refs[-3:]
    me = lax.axis_index("section")
    other = {"section": 1 - me}
    barrier = pltpu.get_barrier_semaphore()
    pl.semaphore_signal(barrier, inc=1, device_id=other, device_id_type=MESH)
    pl.semaphore_wait(barrier, 1)
    copies = []
    for i, (which, start) in enumerate(places):
        target = outs[which].at[me, :, pl.ds(start, ins[i].shape[1])]
        copies.append(push(ins[i], target, send.at[i], recv.at[i], other))
        own = pltpu.make_async_copy(ins[i], target, local.at[i])
        own.start()
        copies.append(own)
    for copy in copies:
        copy.wait()


def both_layers(groups):
    places, flat, outs = [], [], []
    for i, group in enumerate(groups):
        start = 0
        for a in group:
            places.append((i, start))
            flat.append(a)
            start += a.shape[1]
        outs.append(shape((2, group[0].shape[0], start), group[0].dtype))
    count = len(flat)
    vm = pl.BlockSpec(memory_space=pltpu.VMEM)
    anywhere = pl.BlockSpec(memory_space=pl.ANY)
    return pl.pallas_call(
        functools.partial(both_layers_kernel, places),
        out_shape=tuple(outs),
        in_specs=[vm] * count,
        out_specs=(anywhere,) * len(outs),
        scratch_shapes=[pltpu.SemaphoreType.DMA((count,)) for _ in range(3)],
        compiler_params=pltpu.CompilerParams(
            collective_id=0, has_side_effects=True, vmem_limit_bytes=VMEM_LIMIT
        ),
        name="both_layers",
    )(*flat)


def chain_kernel(forward, size, parts, own, decay, out, outgoing, incoming, send, recv):
    me = lax.axis_index("seq")
    batch = own.shape[0]
    step = 1 if forward else -1
    width = own.shape[2] // parts
    has_from = (me > 0) if forward else (me < size - 1)
    has_to = (me < size - 1) if forward else (me > 0)
    target = {"seq": me + step}
    barrier = pltpu.get_barrier_semaphore()

    @pl.when(has_from)
    def _():
        pl.semaphore_signal(barrier, inc=1, device_id={"seq": me - step}, device_id_type=MESH)

    @pl.when(has_to)
    def _():
        pl.semaphore_wait(barrier, 1)

    def copy(m, p):
        at = pl.ds(p * width, width)
        return pltpu.make_async_remote_copy(
            src_ref=outgoing.at[m, :, at],
            dst_ref=incoming.at[m, :, at],
            send_sem=send.at[m * parts + p],
            recv_sem=recv.at[m * parts + p],
            device_id=target,
            device_id_type=MESH,
        )

    for m in range(batch):
        for p in range(parts):
            at = slice(p * width, (p + 1) * width)

            @pl.when(has_from)
            def _():
                copy(m, p).wait_recv()
                out[m, :, at] = incoming[m, :, at].astype(F32)

            @pl.when(jnp.logical_not(has_from))
            def _():
                out[m, :, at] = jnp.zeros_like(out[m, :, at])

            @pl.when(has_to)
            def _():
                outgoing[m, :, at] = (decay[m, 0:1, at] * out[m, :, at] + own[m, :, at]).astype(BF)
                copy(m, p).start()

    @pl.when(has_to)
    def _():
        for m in range(batch):
            for p in range(parts):
                copy(m, p).wait_send()


def chain(own, decay, forward, size, parts=3):
    batch = own.shape[0]
    vm = pl.BlockSpec(memory_space=pltpu.VMEM)
    return pl.pallas_call(
        functools.partial(chain_kernel, forward, size, parts),
        out_shape=shape(own.shape, F32),
        in_specs=[vm, vm],
        out_specs=vm,
        scratch_shapes=[
            pltpu.VMEM(own.shape, BF),
            pltpu.VMEM(own.shape, BF),
            pltpu.SemaphoreType.DMA((batch * parts,)),
            pltpu.SemaphoreType.DMA((batch * parts,)),
        ],
        compiler_params=pltpu.CompilerParams(
            collective_id=1 if forward else 2, has_side_effects=True, vmem_limit_bytes=VMEM_LIMIT
        ),
        name="chain_fwd" if forward else "chain_bwd",
    )(own, decay)


def greet(size):
    me = lax.axis_index("head")
    barrier = pltpu.get_barrier_semaphore()
    peers = [{"head": lax.rem(me + d, size)} for d in range(1, size)]
    for peer in peers:
        pl.semaphore_signal(barrier, inc=1, device_id=peer, device_id_type=MESH)
    pl.semaphore_wait(barrier, size - 1)
    return me, peers


def head_fwd_kernel(size, full, partial, ssq, u, h_o, stats_o, got, got_ssq, send, recv):
    rows = partial.shape[0] // size
    me, peers = greet(size)
    copies = []
    for d, peer in enumerate(peers):
        to = lax.rem(me + d + 1, size)
        at = pl.ds(pl.multiple_of(to * rows, rows), rows)
        copies.append(push(partial.at[at], got.at[d], send.at[0, d], recv.at[0, d], peer))
        copies.append(push(ssq.at[to], got_ssq.at[d], send.at[1, d], recv.at[1, d], peer))
    mine = pl.ds(pl.multiple_of(me * rows, rows), rows)
    for copy in copies:
        copy.wait()
    squares = ssq[me]
    for d in range(size - 1):
        squares = squares + got_ssq[d]
    gs = lax.rsqrt(column(squares)[0] / full + EPSILON)[:, 0:1]
    total = partial[mine, :].astype(F32)
    for d in range(size - 1):
        total = total + got[d].astype(F32)
    h_o[mine, :] = (u[mine, :].astype(F32) + gs * total).astype(BF)
    stats_o[me] = jnp.concatenate([rows_of([gs])[0:1], squares[1:]], axis=0)
    copies = []
    for d, peer in enumerate(peers):
        copies.append(push(h_o.at[mine], h_o.at[mine], send.at[2, d], recv.at[2, d], peer))
        copies.append(push(stats_o.at[me], stats_o.at[me], send.at[3, d], recv.at[3, d], peer))
    for copy in copies:
        copy.wait()


def head_fwd(partial, ssq, u, size, full):
    n, d_model = partial.shape
    rows = n // size
    vm = pl.BlockSpec(memory_space=pltpu.VMEM)
    return pl.pallas_call(
        functools.partial(head_fwd_kernel, size, full),
        out_shape=(shape((n, d_model), BF), shape((size, 8, rows), F32)),
        in_specs=[vm] * 3,
        out_specs=(vm,) * 2,
        scratch_shapes=[
            pltpu.VMEM((size - 1, rows, d_model), BF),
            pltpu.VMEM((size - 1, 8, rows), F32),
            pltpu.SemaphoreType.DMA((4, size - 1)),
            pltpu.SemaphoreType.DMA((4, size - 1)),
        ],
        compiler_params=pltpu.CompilerParams(
            collective_id=3, has_side_effects=True, vmem_limit_bytes=VMEM_LIMIT
        ),
        name="head_fwd",
    )(partial, ssq, u)


def head_bwd_kernel(size, last, partial, upper, u, gain, du_o, mine_o, grad_o, got, send, recv):
    rows = partial.shape[0] // size
    me, peers = greet(size)
    copies = []
    for d, peer in enumerate(peers):
        to = lax.rem(me + d + 1, size)
        at = pl.ds(pl.multiple_of(to * rows, rows), rows)
        copies.append(push(partial.at[at], got.at[d], send.at[0, d], recv.at[0, d], peer))
    mine = pl.ds(pl.multiple_of(me * rows, rows), rows)
    for copy in copies:
        copy.wait()
    dn = partial[mine, :].astype(F32)
    for d in range(size - 1):
        dn = dn + got[d].astype(F32)
    uv = u[mine, :].astype(F32)
    width = uv.shape[1]
    s = lax.rsqrt(jnp.sum(uv * uv, axis=1, keepdims=True) / width + EPSILON)
    grad_o[...] = jnp.broadcast_to(jnp.sum(dn * uv * s, axis=0, keepdims=True), grad_o.shape)
    scaled = dn * gain[...]
    inner = jnp.sum(scaled * uv, axis=1, keepdims=True)
    above = upper[mine, :].astype(F32) if last else upper[...]
    du = above + s * scaled - uv * (s * s * s * inner / width)
    mine_o[...] = du
    du_o[mine, :] = du.astype(BF)
    copies = []
    for d, peer in enumerate(peers):
        copies.append(push(du_o.at[mine], du_o.at[mine], send.at[1, d], recv.at[1, d], peer))
    for copy in copies:
        copy.wait()


def head_bwd(partial, upper, u, gain, size, last):
    n, d_model = partial.shape
    rows = n // size
    vm = pl.BlockSpec(memory_space=pltpu.VMEM)
    return pl.pallas_call(
        functools.partial(head_bwd_kernel, size, last),
        out_shape=(
            shape((n, d_model), BF),
            shape((rows, d_model), F32),
            shape((8, d_model), F32),
        ),
        in_specs=[vm] * 4,
        out_specs=(vm,) * 3,
        scratch_shapes=[
            pltpu.VMEM((size - 1, rows, d_model), BF),
            pltpu.SemaphoreType.DMA((2, size - 1)),
            pltpu.SemaphoreType.DMA((2, size - 1)),
        ],
        compiler_params=pltpu.CompilerParams(
            collective_id=6 if last else 5, has_side_effects=True, vmem_limit_bytes=VMEM_LIMIT
        ),
        name="head_bwd",
    )(partial, upper, u, gain)


def swap_kernel(mine, got, send, recv):
    me = lax.axis_index("section")
    other = {"section": 1 - me}
    barrier = pltpu.get_barrier_semaphore()
    pl.semaphore_signal(barrier, inc=1, device_id=other, device_id_type=MESH)
    pl.semaphore_wait(barrier, 1)
    push(mine.at[1 - me], got, send, recv, other).wait()


def swap(pair, which):
    anywhere = pl.BlockSpec(memory_space=pl.ANY)
    return pl.pallas_call(
        swap_kernel,
        out_shape=shape(pair.shape[1:], pair.dtype),
        in_specs=[anywhere],
        out_specs=anywhere,
        scratch_shapes=[pltpu.SemaphoreType.DMA, pltpu.SemaphoreType.DMA],
        compiler_params=pltpu.CompilerParams(collective_id=which, has_side_effects=True),
        name="swap",
    )(pair)


OWN = 16
SHARED = 80
PIECE = 48
TAIL = (OWN + SHARED) // PIECE


def grad_pack_kernel(dims, heads_axis, normed, g_in, yn, go, conv, scalars, gate, gain, out, few, few_shared):
    heads, inner, states = dims
    width = normed.shape[1]
    tile = 256

    def in_rows(i, _):
        at = pl.ds(pl.multiple_of(i * tile, tile), tile)
        out[at, :] = dot(normed[:, at], g_in[:, : 2 * inner], TN).astype(BF)
        return 0

    lax.fori_loop(0, width // tile, in_rows, 0)

    def out_rows(i, _):
        at = pl.ds(pl.multiple_of(i * tile, tile), tile)
        to = pl.ds(pl.multiple_of(width + i * tile, tile), tile)
        out[to, :] = dot(yn[:, at], go[...], TN).astype(BF)
        return 0

    lax.fori_loop(0, inner // tile, out_rows, 0)
    plain = width + inner + OWN
    split = 2 * inner + 2 * states
    out[plain : plain + 2 * states, :] = dot(g_in[:, 2 * inner : split], normed[...], TN).astype(BF)
    conv_sum = conv[0]
    scalar_sum = scalars[0]
    gate_sum = gate[0]
    for i in range(1, conv.shape[0]):
        conv_sum, scalar_sum, gate_sum = conv_sum + conv[i], scalar_sum + scalars[i], gate_sum + gate[i]
    few[...] = jnp.zeros_like(few)
    few[0:heads, :] = dot(g_in[:, split:], normed[...], TN)[0:heads]
    few[heads : heads + 4, 0:inner] = conv_sum[0:4, :inner]
    few[heads : heads + 1, inner : 2 * inner] = conv_sum[4:5, :inner]
    few[heads + 1 : heads + 2, inner : 2 * inner] = gate_sum[0:1]
    for i in range(3):
        few[heads + 2 : heads + 3, inner + i * LANES : inner + (i + 1) * LANES] = scalar_sum[i : i + 1]
    out[plain - OWN : plain, :] = few[...].astype(BF)
    few_shared[...] = jnp.zeros_like(few_shared)
    few_shared[0:1, :] = gain[0:1, :]
    few_shared[1:6, 0 : 2 * states] = conv_sum[0:5, inner:]
    out[plain + 2 * states :, :] = few_shared[...].astype(BF)


def grad_pack(normed, g_in, yn, go, conv, scalars, gate, gain, dims, heads_axis):
    heads, inner, states = dims
    width = normed.shape[1]
    rows = width + inner + OWN + heads_axis * SHARED
    vm = pl.BlockSpec(memory_space=pltpu.VMEM)
    return pl.pallas_call(
        functools.partial(grad_pack_kernel, dims, heads_axis),
        out_shape=shape((rows, width), BF),
        in_specs=[vm] * 8,
        out_specs=vm,
        scratch_shapes=[
            pltpu.VMEM((OWN, width), F32),
            pltpu.VMEM((heads_axis * SHARED - 2 * states, width), F32),
        ],
        compiler_params=pltpu.CompilerParams(vmem_limit_bytes=VMEM_LIMIT),
        name="grad_pack",
    )(normed, g_in, yn, go, conv, scalars, gate, gain)


def grad_sum_kernel(size, heads, skew, pack0, pack1, out, shared_o, own, core, got, shared, shared_core, shared_got,
                    ls, cs, cr, rs, rr, bs, br, hs, hr, xs):
    me, layer, head = lax.axis_index("seq"), lax.axis_index("section"), lax.axis_index("head")
    rows = pack0.shape[0] - heads * SHARED + SHARED
    plain = rows - SHARED
    half = rows // 2
    parts = half // PIECE
    up, down, other = {"seq": me + 1}, {"seq": me - 1}, {"section": 1 - layer}
    peers = [{"head": lax.rem(head + d, heads)} for d in range(1, heads)]
    low_end, high_end = me == 0, me == size - 1
    barrier = pltpu.get_barrier_semaphore()
    pl.semaphore_signal(barrier, inc=1, device_id=other, device_id_type=MESH)
    for peer in peers:
        pl.semaphore_signal(barrier, inc=1, device_id=peer, device_id_type=MESH)

    @pl.when(jnp.logical_not(low_end))
    def _():
        pl.semaphore_signal(barrier, inc=1, device_id=down, device_id_type=MESH)

    @pl.when(jnp.logical_not(high_end))
    def _():
        pl.semaphore_signal(barrier, inc=1, device_id=up, device_id_type=MESH)

    @pl.when(jnp.logical_not(jnp.logical_or(low_end, high_end)))
    def _():
        pl.semaphore_wait(barrier, heads + 2)

    @pl.when(jnp.logical_or(low_end, high_end))
    def _():
        pl.semaphore_wait(barrier, heads + 1)

    part = pl.ds(plain - OWN, OWN + heads * SHARED)
    def fetch_shared(ours, others):
        return (
            pltpu.make_async_copy(ours.at[part], shared, xs.at[0]),
            pltpu.make_async_remote_copy(
                src_ref=others.at[part], dst_ref=shared_core, send_sem=xs.at[1], recv_sem=xs.at[2],
                device_id=other, device_id_type=MESH,
            ),
        )

    def by_layer(act):
        pl.when(layer == 0)(lambda: act(pack0, pack1))
        pl.when(layer == 1)(lambda: act(pack1, pack0))

    def start_all(copies):
        for copy in copies:
            copy.start()

    by_layer(lambda a, b: start_all(fetch_shared(a, b)))

    shift = parts * 3 // 5

    def order(side, p):
        return lax.rem(p + (shift if side else 0), parts)

    def place(side, p):
        return pl.ds(pl.multiple_of(side * half + order(side, p) * PIECE, PIECE), PIECE)

    def unless_tail(side, p, act):
        if side:
            pl.when(order(side, p) < parts - TAIL)(act)
        else:
            act()

    def fetch(side, p, ours, others):
        at = place(side, p)
        return (
            pltpu.make_async_copy(ours.at[at], own.at[at], ls.at[side, p]),
            pltpu.make_async_remote_copy(
                src_ref=others.at[at], dst_ref=core.at[at], send_sem=cs.at[side, p],
                recv_sem=cr.at[side, p], device_id=other, device_id_type=MESH,
            ),
        )

    def start_fetch(p, _):
        for side in range(2):

            unless_tail(side, p, lambda: by_layer(lambda a, b: start_all(fetch(side, p, a, b))))
        return 0

    lax.fori_loop(0, parts, start_fetch, 0)
    for copy in fetch_shared(pack0, pack1):
        copy.wait()
    shared[...] = (shared[...].astype(F32) + shared_core[...].astype(F32)).astype(BF)
    block = lambda i: pl.ds(pl.multiple_of(OWN + i * SHARED, 16), SHARED)
    scatter = lambda d: pltpu.make_async_remote_copy(
        src_ref=shared.at[block(lax.rem(head + d + 1, heads))], dst_ref=shared_got.at[d],
        send_sem=hs.at[0, d], recv_sem=hr.at[0, d], device_id=peers[d], device_id_type=MESH,
    )
    gather = lambda d: pltpu.make_async_remote_copy(
        src_ref=shared_o.at[head], dst_ref=shared_o.at[head],
        send_sem=hs.at[1, d], recv_sem=hr.at[1, d], device_id=peers[d], device_id_type=MESH,
    )
    for d in range(heads - 1):
        scatter(d).start()

    def sending(side, p, back, source):
        at = place(side, p)
        towards = down if (side == 0) != back else up
        target, send, recv = (out, bs, br) if back else (got, rs, rr)
        return pltpu.make_async_remote_copy(
            src_ref=source.at[at], dst_ref=target.at[at], send_sem=send.at[side, p],
            recv_sem=recv.at[side, p], device_id=towards, device_id_type=MESH,
        )

    def reduce(side, p):
        start, end = (high_end, low_end) if side == 0 else (low_end, high_end)
        at = place(side, p)

        def collect():
            local, remote = fetch(side, p, pack0, pack1)
            local.wait()
            remote.wait()
            own[at, :] = (own[at, :].astype(F32) + core[at, :].astype(F32)).astype(BF)

        unless_tail(side, p, collect)

        @pl.when(start)
        def _():
            sending(side, p, False, own).start()

        @pl.when(jnp.logical_not(start))
        def _():
            sending(side, p, False, got).wait_recv()
            summed = (own[at, :].astype(F32) + got[at, :].astype(F32)).astype(BF)

            @pl.when(end)
            def _():
                out[at, :] = summed
                sending(side, p, True, out).start()

            @pl.when(jnp.logical_not(end))
            def _():
                got[at, :] = summed
                sending(side, p, False, got).start()

    def back(side, p):
        start, end = (high_end, low_end) if side == 0 else (low_end, high_end)

        @pl.when(jnp.logical_not(end))
        def _():
            sending(side, p, True, out).wait_recv()

            @pl.when(jnp.logical_not(start))
            def _():
                sending(side, p, True, out).start()

    def guarded(act, side, p):
        @pl.when(jnp.logical_and(p >= 0, p < parts))
        def _():
            act(side, p)

    far = size - 1
    ready = parts - shift - TAIL - 1
    finished = parts - shift + skew * (2 * far - me)

    def step(t, _):
        @pl.when(t == ready)
        def _():
            total = shared[block(head), :].astype(F32)
            for d in range(heads - 1):
                scatter(d).wait()
                total = total + shared_got[d].astype(F32)
            own[plain : plain + SHARED, :] = total.astype(BF)
            own[plain - OWN : plain, :] = shared[0:OWN, :]

        guarded(reduce, 0, t - skew * (far - me))
        guarded(reduce, 1, t - skew * me)
        guarded(back, 0, t - skew * (far + me))
        guarded(back, 1, t - skew * (2 * far - me))

        @pl.when(t == finished)
        def _():
            shared_o[head] = out[plain:rows, :]
            for d in range(heads - 1):
                gather(d).start()

        return 0

    lax.fori_loop(0, parts + 2 * skew * far, step, 0)

    def drain(p, _):
        for side in range(2):
            start, end = (high_end, low_end) if side == 0 else (low_end, high_end)

            @pl.when(jnp.logical_not(end))
            def _():
                sending(side, p, False, got).wait_send()

            @pl.when(jnp.logical_not(start))
            def _():
                sending(side, p, True, out).wait_send()

        return 0

    lax.fori_loop(0, parts, drain, 0)
    for d in range(heads - 1):
        gather(d).wait()


def grad_sum(pack0, pack1, size, heads, skew=2):
    rows = pack0.shape[0] - (heads - 1) * SHARED
    width = pack0.shape[1]
    parts = rows // 2 // PIECE
    vm = pl.BlockSpec(memory_space=pltpu.VMEM)
    pair = pltpu.SemaphoreType.DMA((2, parts))
    return pl.pallas_call(
        functools.partial(grad_sum_kernel, size, heads, skew),
        out_shape=(shape((rows, width), BF), shape((heads, SHARED, width), BF)),
        in_specs=[pl.BlockSpec(memory_space=pl.ANY)] * 2,
        out_specs=(vm, vm),
        scratch_shapes=[pltpu.VMEM((rows, width), BF) for _ in range(3)]
        + [pltpu.VMEM((OWN + heads * SHARED, width), BF) for _ in range(2)]
        + [pltpu.VMEM((heads - 1, SHARED, width), BF)]
        + [pair] * 7
        + [pltpu.SemaphoreType.DMA((2, heads - 1)) for _ in range(2)]
        + [pltpu.SemaphoreType.DMA((3,))],
        compiler_params=pltpu.CompilerParams(
            collective_id=8, has_side_effects=True, vmem_limit_bytes=VMEM_LIMIT
        ),
        name="grad_sum",
    )(pack0, pack1)


def over_seq(block, distance):
    size = lax.axis_size("seq")
    route = [(i - distance, i) for i in range(size) if 0 <= i - distance < size]
    return lax.ppermute(block, "seq", route)


def normalise(u, gain):
    uv = u.astype(F32)
    s = lax.rsqrt(jnp.mean(uv * uv, axis=-1, keepdims=True) + EPSILON)
    return (uv * s * gain).astype(BF)


def on_device(
    inputs, cotangent, norm_gain, w_z, w_x, w_bc, w_dt, conv_x, conv_x_bias, conv_bc, conv_bc_bias,
    dt_bias, a_log, d_skip, gate_gain, w_out,
):
    me = lax.axis_index("section")
    seq_size, head_size = lax.axis_size("seq"), lax.axis_size("head")
    micro, n, d_model = inputs.shape
    batch = micro // 2
    tokens = batch * n
    inner, heads, states = w_z.shape[2], w_dt.shape[2], w_bc.shape[2] // 2
    wide = inner + 2 * states
    full = inner * head_size
    dims = (heads, inner, states)
    pad_heads = lambda a: jnp.pad(a, ((0, 0),) * (a.ndim - 1) + ((0, LANES - heads),))

    taps_x = jnp.concatenate([conv_x[0], conv_x_bias, jnp.zeros((3, inner), F32)], axis=0)
    taps_bc = jnp.concatenate([conv_bc[0], conv_bc_bias, jnp.zeros((3, 2 * states), F32)], axis=0)
    taps = jnp.concatenate([taps_x, taps_bc], axis=1)
    scalars = pad_heads(jnp.concatenate([dt_bias, -jnp.exp(a_log)], axis=0)).reshape(1, -1)
    vectors = jnp.concatenate(
        [
            jnp.repeat(d_skip[0], inner // heads)[None],
            gate_gain,
            jnp.pad(scalars, ((0, 0), (0, inner - 2 * LANES))),
            jnp.zeros((5, inner), F32),
        ],
        axis=0,
    )
    gains = jnp.broadcast_to(norm_gain, (8, d_model))
    w_in2, w_out2, vectors2 = both_layers(
        [[w_z[0], w_x[0], w_bc[0], pad_heads(w_dt[0])], [w_out[0]], [taps, vectors, gains]]
    )
    gains2 = vectors2[:, :, wide + inner :]
    taps2, vectors2 = vectors2[:, :, :wide], vectors2[:, :, wide : wide + inner]

    u = lax.dynamic_slice_in_dim(inputs, me * batch, batch, 0).reshape(tokens, d_model)
    cot = lax.dynamic_slice_in_dim(cotangent, me * batch, batch, 0).reshape(tokens, d_model)

    kept = []
    layers = 2
    for l in range(layers):
        gain = gains2[l, 0:1]
        kernel, bias = taps2[l, 0:4], taps2[l, 4:5]
        skip, gate = vectors2[l, 0:1], vectors2[l, 1:2]
        dt_b, a_neg = vectors2[l, 2:3, :LANES], vectors2[l, 2:3, LANES : 2 * LANES]
        normed = normalise(u, gain)
        proj = dot(normed, w_in2[l]).reshape(batch, n, -1)
        rim = over_seq(proj[:, n - 3 :, inner : inner + wide].astype(BF), 1)
        halo = jnp.pad(rim, ((0, 0), (5, 0), (0, 0)))
        cx, dt, cum, own, decay = ssd_fwd1(proj, halo, kernel, bias, dt_b, a_neg, dims)
        state = chain(own, decay, True, seq_size)
        dyn = dot(cot, w_out2[l], NT).reshape(batch, n, inner) if l == layers - 1 else None
        y, gg, ssq = ssd_fwd2(cx, dt, cum, state, proj, skip, gate, dyn, dims)
        partial = dot(gg.reshape(tokens, inner), w_out2[l]).astype(BF)
        per = head_size // batch
        ssq = ssq.reshape(batch, 8, per, n // per).transpose(0, 2, 1, 3).reshape(head_size, 8, n // per)
        h, stats = head_fwd(partial, ssq, u, head_size, full)
        kept.append((u, gain, kernel, bias, skip, gate, dt_b, a_neg, normed, proj, halo, cx, dt, cum, decay, state, y, stats, dyn, h))
        u = h
    go, upper = cot, cot
    results = []
    for l in reversed(range(layers)):
        (u, gain, kernel, bias, skip, gate, dt_b, a_neg, normed, proj, halo, cx, dt, cum, decay, state, y, stats, dyn, h) = kept[l]
        last = l == layers - 1
        across = stats
        if not last:
            dyn = dot(go, w_out2[l], NT).reshape(batch, n, inner)
            z = proj[..., :inner]
            across = lax.psum(jnp.sum(dyn * gate * y * z * sigmoid(z), axis=-1), "head")
            across = jnp.broadcast_to(across.reshape(head_size, 1, -1), stats.shape)
        dy, dz, yn, ggg, d_state = ssd_bwd1(dyn, y, proj, cx, cum, stats, across, gate, dims, full)
        later = chain(d_state, decay, False, seq_size)
        dpre, gdt, conv_grads, small = ssd_bwd2(
            dy, proj, halo, cx, dt, cum, state, later, kernel, bias, dt_b, a_neg, skip, dims
        )
        rim = jnp.pad(over_seq(dpre[:, :3], -1), ((0, 0), (0, 5), (0, 0)))
        g_in = conv_bwd(dpre, rim, dz, gdt, kernel, dims).reshape(tokens, -1)
        partial = dot(g_in, w_in2[l], NT).astype(BF)
        du, upper_new, grad_gain = head_bwd(partial, upper, u, gain, head_size, last)
        pack = grad_pack(normed, g_in, yn.reshape(tokens, inner), go, conv_grads, small, ggg, grad_gain, dims, head_size)
        results.append((du, pack))
        go, upper = du, upper_new
    results = results[::-1]

    grads, shared = grad_sum(results[0][1], results[1][1], seq_size, head_size)
    plain = d_model + inner
    small = grads[plain : plain + OWN].astype(F32)
    shared = shared.reshape(-1, d_model)
    grad_bc = shared[: 2 * states].T.astype(F32)
    grad_gain = shared[2 * states].astype(F32)
    conv_b = shared[2 * states + 1 : 2 * states + 6, : 2 * states].astype(F32)

    def gather(first, second):
        pair = jnp.stack([first, second]).reshape(2, batch, n, d_model)
        got = swap(pair, 9)
        own = lax.dynamic_index_in_dim(pair, me, 0, False)
        out = jnp.zeros((micro, n, d_model), BF)
        out = lax.dynamic_update_slice_in_dim(out, own, me * batch, 0)
        return lax.dynamic_update_slice_in_dim(out, got, (1 - me) * batch, 0)[None]

    layer_outputs = gather(kept[0][19], kept[1][19])
    input_grads = gather(results[0][0], results[1][0])
    return (
        layer_outputs,
        input_grads,
        grad_gain[None],
        grads[None, :d_model, :inner].astype(F32),
        grads[None, :d_model, inner:].astype(F32),
        grad_bc[None],
        small[None, :heads].transpose(0, 2, 1),
        small[None, heads : heads + 4, :inner],
        small[None, heads, inner:],
        conv_b[None, :4],
        conv_b[None, 4],
        small[None, heads + 2, inner : inner + heads],
        small[None, heads + 2, inner + LANES : inner + LANES + heads],
        small[None, heads + 2, inner + 2 * LANES : inner + 2 * LANES + heads],
        small[None, heads + 1, inner:],
        grads[None, d_model:plain].astype(F32),
    )


def solution(mesh):
    in_specs = (
        P(None, "seq", None),
        P(None, "seq", None),
        P("section", None),
        P("section", None, "head"),
        P("section", None, "head"),
        P("section", None, None),
        P("section", None, "head"),
        P("section", None, "head"),
        P("section", "head"),
        P("section", None, None),
        P("section", None),
        P("section", "head"),
        P("section", "head"),
        P("section", "head"),
        P("section", "head"),
        P("section", "head", None),
    )
    out_specs = (
        P("section", None, "seq", None),
        P("section", None, "seq", None),
        P("section", None),
        P("section", None, "head"),
        P("section", None, "head"),
        P("section", None, None),
        P("section", None, "head"),
        P("section", None, "head"),
        P("section", "head"),
        P("section", None, None),
        P("section", None),
        P("section", "head"),
        P("section", "head"),
        P("section", "head"),
        P("section", "head"),
        P("section", "head", None),
    )
    return jax.shard_map(
        on_device, mesh=mesh, in_specs=in_specs, out_specs=out_specs, check_vma=False
    )
```

time: 2340 us -> 720 us (0.31)
  waiting for transfers between devices: 983 us -> 2.35 us
  Pallas kernels: 0 us -> 568 us
  matrix products: 411 us -> 42.9 us
  blocking collectives: 362 us -> 12.3 us
  other arithmetic: 320 us -> 36.7 us
  local copies, waits for them, and re-layouts: 180 us -> 32.9 us
  starting transfers between devices: 42.6 us -> 14.6 us
    psum x16 -> x0, waiting for transfers between devices: 826 us -> none  [the longest x1 274 us: on_device(): lax.psum(totals[1].astype(jnp.bfloat16), 'seq').astype(jnp.float32)]
    pallas_call x0 -> x24, Pallas kernels: none -> 568 us  [the longest x1 190 us: grad_sum(): pl.pallas_call(functools.partial(grad_sum_kernel, size, heads, skew), out...]
    dot_general x150 -> x8, matrix products: 411 us -> 42.9 us  [dot(): lax.dot_general(a, b, (dims, ((), ())), precision=precision, preferred_el...]
    all_gather x20 -> x0, blocking collectives: 230 us -> none  [the longest x10 137 us: prefix(): lax.all_gather(a.astype(kind), axis)]
    all_gather x10 -> x0, waiting for transfers between devices: 137 us -> none  [entering(): everything = jax.tree.map(lambda part: lax.all_gather(part, axis), value)]
    psum x12 -> x1, blocking collectives: 132 us -> 12.3 us  [on_device(): across = lax.psum(jnp.sum(dyn * gate * y * z * sigmoid(z), axis=-1), 'head')]
    another operation x72 -> x3, other arithmetic: 76.2 us -> 4.48 us  [the longest x2 3.87 us: gather(): pair = jnp.stack([first, second]).reshape(2, batch, n, d_model)]
    select_n x40 -> x0, other arithmetic: 64.7 us -> none  [lap(): return jax.tree.map(lambda a, b: jnp.where(reached, a, b), new, before)]
  transfers between devices with their start and end apart: 44 -> 4, of which waited for: 34 -> 1; matrix products, arithmetic and copies ran while one was open for 17% -> 2% of each run, Pallas kernels for 0% -> 2%
where the time goes in v1:
time: 720 us; the launch traced here: 711 us
  Pallas kernels  568 us (79%)
  matrix products  42.9 us (6%)
  other arithmetic  36.7 us (5%)
  local copies, waits for them, and re-layouts  32.9 us (5%)
  starting transfers between devices  14.6 us (2%)
  blocking collectives  12.3 us (2%)
    pallas_call x1, Pallas kernels, grad_sum(): pl.pallas_call(functools.partial(grad_sum_kernel, size, heads, skew), out...  190 us
    pallas_call x2, Pallas kernels, head_fwd(): pl.pallas_call(functools.partial(head_fwd_kernel, size, full), out_shape=...  82.7 us
    pallas_call x2, Pallas kernels, head_bwd(): pl.pallas_call(functools.partial(head_bwd_kernel, size, last), out_shape=...  82.3 us
    pallas_call x4, Pallas kernels, chain(): pl.pallas_call(functools.partial(chain_kernel, forward, size, parts), out...  68.2 us
    pallas_call x2, Pallas kernels, ssd_bwd2(): pl.pallas_call(functools.partial(ssd_bwd2_kernel, dims), grid=(batch,), o...  46.7 us
    dot_general x8, matrix products, dot(): lax.dot_general(a, b, (dims, ((), ())), precision=precision, preferred_el...  42.9 us
    pallas_call x2, Pallas kernels, grad_pack(): pl.pallas_call(functools.partial(grad_pack_kernel, dims, heads_axis), out...  24 us
    pallas_call x1, Pallas kernels, both_layers(): pl.pallas_call(functools.partial(both_layers_kernel, places), out_shape=t...  17.1 us
  transfers between devices with their start and end apart: 4, of which 1 were waited for; matrix products, arithmetic and copies ran while one was open for 2% of the time, Pallas kernels for 2%

profile of v1, /device:TPU:0, one launch (start us, length us, event | category | flops | bytes accessed | tf_op | source)
XLA Modules:
  0.0 711.3 jit_solution(16849941551575888517)
XLA Ops:
  0.7 3.0 fusion.12
  4.3 1.0 copy.34
  8.4 1.4 fusion.41.refs_6_
  9.8 1.4 maximum_maximum_fusion.refs_5_
  11.8 17.1 %both_layers.1 = (bf16[2,1536,1920]{2,1,0:T(8,128)(2,1)}, bf16[2,768,1536]{2,1,0:T(8,128)(2,1)}, f32[2,8,3328]{2,1,0:T(8,128)}) custom-call(bf16[1536,768]{1,0:T(8,128)(2,1)} %bitcast.138, bf16[1536,768]{1,0:T(8,128)(2,1)} %bitcast.139, bf16[1536,256]{1,0:T(8,128)(2,1)} %bitcast.142, bf16[1536,128]{1,0:T(8,128)(2,1)} %pad.26.refs_3_, ...), custom_call_target="tpu_custom_call" | custom-call | tf_op jit(solution)/shard_map/both_layers/pallas_call | solution.py:456
  28.9 1.4 slice_bitcast_fusion.8
  30.4 5.7 fusion.4.proj.refs_4_
  36.1 4.8 collective-permute-start
  40.9 1.2 slice_bitcast_fusion.13
  42.2 1.4 slice_bitcast_fusion.1
  43.5 1.4 slice_bitcast_fusion.5
  45.0 1.7 multiply_convert_fusion.normed
  46.7 1.4 slice_reduce_fusion.2
  48.8 6.8 ssd_fwd1.2
  55.6 12.2 %chain_fwd.2.refs_3_.state = f32[2,128,768]{2,1,0:T(8,128)} custom-call(f32[2,128,768]{2,1,0:T(8,128)} %get-tuple-element.69.own, f32[2,8,768]{2,1,0:T(8,128)} %get-tuple-element.70.decay), custom_call_target="tpu_custom_call" | custom-call | tf_op jit(solution)/shard_map/chain_fwd/pallas_call | solution.py:526
  67.8 6.9 ssd_fwd2.2
  76.0 4.4 convolution_convert_fusion.1.partial
  80.4 41.6 %head_fwd.2 = (bf16[512,1536]{1,0:T(8,128)(2,1)}, f32[4,8,128]{2,1,0:T(8,128)}) custom-call(bf16[512,1536]{1,0:T(8,128)(2,1)} %convolution_convert_fusion.1.partial, f32[4,8,128]{2,1,0:T(8,128)} %bitcast.148, bf16[512,1536]{1,0:T(8,128)(2,1)} %bitcast.122), custom_call_target="tpu_custom_call" | custom-call | tf_op jit(solution)/shard_map/head_fwd/pallas_call | solution.py:587
  122.0 1.8 fusion.15
  123.8 2.0 fusion.17.normed
  125.8 6.1 fusion.proj
  132.0 1.9 copy-done.3
  133.9 6.6 collective-permute-start.1
  140.5 2.6 fusion.26.dyn
  143.7 6.8 ssd_fwd1.3
  150.5 13.9 %chain_fwd.3.state = f32[2,128,768]{2,1,0:T(8,128)} custom-call(f32[2,128,768]{2,1,0:T(8,128)} %get-tuple-element.78.own, f32[2,8,768]{2,1,0:T(8,128)} %get-tuple-element.79.decay), custom_call_target="tpu_custom_call" | custom-call | tf_op jit(solution)/shard_map/chain_fwd/pallas_call | solution.py:526
  164.4 7.6 %ssd_fwd2.3 = (f32[2,256,768]{2,1,0:T(8,128)}, bf16[2,256,768]{2,1,0:T(8,128)(2,1)}, f32[2,8,256]{2,1,0:T(8,128)}) custom-call(f32[2,256,1024]{2,1,0:T(8,128)} %get-tuple-element.75.cx, f32[2,256,128]{2,1,0:T(8,128)} %get-tuple-element.76.dt, f32[2,256,128]{2,1,0:T(8,128)} %get-tuple-element.77.cum, f32[2,128,768]{2,1,0:T(8,128)} %chain_fwd.3.state, ...), custom_call_target="tpu_custom_call" | custom-call | tf_op jit(solution)/shard_map/ssd_fwd2/pallas_call | solution.py:173
  172.7 3.8 convolution_convert_fusion.partial
  177.1 41.1 %head_fwd.3 = (bf16[512,1536]{1,0:T(8,128)(2,1)}, f32[4,8,128]{2,1,0:T(8,128)}) custom-call(bf16[512,1536]{1,0:T(8,128)(2,1)} %convolution_convert_fusion.partial, f32[4,8,128]{2,1,0:T(8,128)} %bitcast.149, bf16[512,1536]{1,0:T(8,128)(2,1)} %get-tuple-element.74.u), custom_call_target="tpu_custom_call" | custom-call | tf_op jit(solution)/shard_map/head_fwd/pallas_call | solution.py:587
  218.3 6.6 ssd_bwd1.2
  224.8 27.0 %chain_bwd.2.later = f32[2,128,768]{2,1,0:T(8,128)} custom-call(f32[2,128,768]{2,1,0:T(8,128)} %get-tuple-element.86.own, f32[2,8,768]{2,1,0:T(8,128)} %get-tuple-element.79.decay), custom_call_target="tpu_custom_call" | custom-call | tf_op jit(solution)/shard_map/chain_bwd/pallas_call | solution.py:526
  251.8 23.4 %ssd_bwd2.2 = (f32[2,256,1024]{2,1,0:T(8,128)}, bf16[2,256,128]{2,1,0:T(8,128)(2,1)}, f32[2,8,1024]{2,1,0:T(8,128)}, f32[2,8,128]{2,1,0:T(8,128)}) custom-call(f32[2,256,768]{2,1,0:T(8,128)} %get-tuple-element.85.dy, f32[2,256,1920]{2,1,0:T(8,128)} %copy-done.3, bf16[2,8,1024]{2,1,0:T(8,128)(2,1)} %pad.30.halo, f32[2,256,1024]{2,1,0:T(8,128)} %get-tuple-element.75.cx, ...), custom_call_target="tpu_custom_call" | custom-call | tf_op jit(solution)/shard_map/ssd_bwd2/pallas_call | solution.py:349
  276.0 1.5 collective-permute-start.2
  277.6 1.9 pad_maximum_fusion.mine
  279.5 2.3 collective-permute-done.2
  282.5 4.2 conv_bwd.2
  286.7 7.9 %fusion.21.partial = bf16[512,1536]{1,0:T(8,128)(2,1)} fusion(bf16[512,1920]{1,0:T(8,128)(2,1)} %bitcast.129, bf16[2,1536,1920]{2,1,0:T(8,128)(2,1)} %get-tuple-element.65), kind=kOutput, calls=%fused_computation.30 | convolution fusion | flops 3020685312 | bytes 9437184 | tf_op jit(solution)/shard_map/dot_general | solution.py:24
  294.5 39.7 %head_bwd.2 = (bf16[512,1536]{1,0:T(8,128)(2,1)}, f32[128,1536]{1,0:T(8,128)}, f32[8,1536]{1,0:T(8,128)}) custom-call(bf16[512,1536]{1,0:T(8,128)(2,1)} %fusion.21.partial, bf16[512,1536]{1,0:T(8,128)(2,1)} %bitcast.124, bf16[512,1536]{1,0:T(8,128)(2,1)} %get-tuple-element.74.u, f32[1,1536]{1,0:T(1,128)} %get-tuple-element.151.gain), custom_call_target="tpu_custom_call" | custom-call | tf_op jit(solution)/shard_map/head_bwd/pallas_call | solution.py:640
  334.2 4.6 multiply_reduce_fusion
  338.8 12.3 %psum.7 = f32[4,128]{1,0:T(4,128)S(1)} all-reduce(f32[4,128]{1,0:T(4,128)S(1)} %broadcast_in_dim.63), channel_id=1, replica_groups=mesh['section'=2,'seq'=4,'head'=4] {'head'}, use_global_device_ids=true, to_apply=%region_3.4 | all-reduce | flops 512 | bytes 4096 | tf_op jit(solution)/shard_map/psum | solution.py:1054
  351.8 6.3 ssd_bwd1.3
  358.0 15.2 %chain_bwd.3.later = f32[2,128,768]{2,1,0:T(8,128)} custom-call(f32[2,128,768]{2,1,0:T(8,128)} %get-tuple-element.94.own, f32[2,8,768]{2,1,0:T(8,128)} %get-tuple-element.70.decay), custom_call_target="tpu_custom_call" | custom-call | tf_op jit(solution)/shard_map/chain_bwd/pallas_call | solution.py:526
  373.2 23.3 %ssd_bwd2.3 = (f32[2,256,1024]{2,1,0:T(8,128)}, bf16[2,256,128]{2,1,0:T(8,128)(2,1)}, f32[2,8,1024]{2,1,0:T(8,128)}, f32[2,8,128]{2,1,0:T(8,128)}) custom-call(f32[2,256,768]{2,1,0:T(8,128)} %get-tuple-element.93.dy, f32[2,256,1920]{2,1,0:T(8,128)} %copy-done.2, bf16[2,8,1024]{2,1,0:T(8,128)(2,1)} %pad.29.halo, ...), custom_call_target="tpu_custom_call" | custom-call | tf_op jit(solution)/shard_map/ssd_bwd2/pallas_call | solution.py:349
  396.5 1.0 slice.178
  397.5 1.7 collective-permute-start.3
  399.3 1.9 broadcast_in_dim.55.clone.1
  401.2 1.7 fusion.38
  402.9 3.8 swap.2
  406.6 12.0 %grad_pack.3.pack1 = bf16[2640,1536]{1,0:T(8,128)(2,1)} custom-call(bf16[512,1536]{1,0:T(8,128)(2,1)} %copy-done.15, bf16[512,1920]{1,0:T(8,128)(2,1)} %bitcast.130, bf16[512,768]{1,0:T(8,128)(2,1)} %bitcast.143, bf16[512,1536]{1,0:T(8,128)(2,1)} %bitcast.125, f32[2,8,1024]{2,1,0:T(8,128)} %get-tuple-element.106.conv, ...), custom_call_target="tpu_custom_call" | custom-call | tf_op jit(solution)/shard_map/grad_pack/pallas_call | solution.py:735
  419.3 4.1 conv_bwd.3
  423.4 7.9 %fusion.18.partial = bf16[512,1536]{1,0:T(8,128)(2,1)} fusion(bf16[512,1920]{1,0:T(8,128)(2,1)} %bitcast.131, bf16[2,1536,1920]{2,1,0:T(8,128)(2,1)} %get-tuple-element.65), kind=kOutput, calls=%fused_computation.29 | convolution fusion | flops 3020685312 | bytes 9437184 | tf_op jit(solution)/shard_map/dot_general | solution.py:24
  431.3 42.6 %head_bwd.3 = (bf16[512,1536]{1,0:T(8,128)(2,1)}, f32[128,1536]{1,0:T(8,128)}, f32[8,1536]{1,0:T(8,128)}) custom-call(bf16[512,1536]{1,0:T(8,128)(2,1)} %fusion.18.partial, f32[128,1536]{1,0:T(8,128)} %get-tuple-element.98.upper, bf16[512,1536]{1,0:T(8,128)(2,1)} %bitcast.123, f32[1,1536]{1,0:T(1,128)} %get-tuple-element.150.gain), custom_call_target="tpu_custom_call" | custom-call | tf_op jit(solution)/shard_map/head_bwd/pallas_call | solution.py:640
  473.9 12.0 %grad_pack.2.pack0 = bf16[2640,1536]{1,0:T(8,128)(2,1)} custom-call(bf16[512,1536]{1,0:T(8,128)(2,1)} %multiply_convert_fusion.normed, bf16[512,1920]{1,0:T(8,128)(2,1)} %bitcast.132, bf16[512,768]{1,0:T(8,128)(2,1)} %bitcast.144, bf16[512,1536]{1,0:T(8,128)(2,1)} %get-tuple-element.90.go, f32[2,8,1024]{2,1,0:T(8,128)} %get-tuple-element.101.conv, ...), custom_call_target="tpu_custom_call" | custom-call | tf_op jit(solution)/shard_map/grad_pack/pallas_call | solution.py:735
  485.9 190.3 %grad_sum.1 = (bf16[2400,1536]{1,0:T(8,128)(2,1)}, bf16[4,80,1536]{2,1,0:T(8,128)(2,1)}) custom-call(bf16[2640,1536]{1,0:T(8,128)(2,1)} %grad_pack.2.pack0, bf16[2640,1536]{1,0:T(8,128)(2,1)} %grad_pack.3.pack1), custom_call_target="tpu_custom_call" | custom-call | tf_op jit(solution)/shard_map/grad_sum/pallas_call | solution.py:956
  676.3 6.9 bitcast_convert_fusion.1
  683.1 4.6 bitcast_convert_fusion
  687.7 1.0 slice_convert_fusion
  693.1 2.3 copy.37
  695.4 2.4 convert_bitcast_fusion
  698.5 1.9 pad_maximum_fusion.1.mine
  700.4 3.8 swap.3
  704.5 1.1 copy-done.9
  708.0 1.4 bitcast_dynamic-update-slice_fusion
  709.4 1.7 copy-done.16
  (92 shorter events, 18.9 us)
Async XLA Ops:
  0.6 44.3 %copy-start = (bf16[4,256,1536]{2,1,0:T(8,128)(2,1)S(1)}, bf16[4,256,1536]{2,1,0:T(8,128)(2,1)}, u32[]{:S(2)}) copy-start(bf16[4,256,1536]{2,1,0:T(8,128)(2,1)} %param.17) | copy-start | bytes 9437188
  0.7 4.7 copy-start.20
  11.8 18.6 %copy-start.6 = (bf16[2,256,1536]{2,1,0:T(8,128)(2,1)S(1)}, bf16[2,256,1536]{2,1,0:T(8,128)(2,1)}, u32[]{:S(2)}) copy-start(bf16[2,256,1536]{2,1,0:T(8,128)(2,1)} %get-tuple-element.147) | copy-start | bytes 4718596
  11.8 18.6 %copy-start.19 = (f32[2,256]{1,0:T(2,128)S(1)}, f32[2,256]{1,0:T(2,128)}, u32[]{:S(2)}) copy-start(f32[2,256]{1,0:T(2,128)} %get-tuple-element.177) | copy-start | bytes 6148
  36.0 10.7 %copy-start.2 = (f32[2,256,1920]{2,1,0:T(8,128)}, f32[2,256,1920]{2,1,0:T(8,128)S(1)}, u32[]{:S(2)}) copy-start(f32[2,256,1920]{2,1,0:T(8,128)S(1)} %fusion.4.proj.refs_4_) | copy-start | bytes 11796484
  36.1 12.1 %collective-permute-start = (bf16[2,3,1024]{2,1,0:T(4,128)(2,1)S(1)}, bf16[2,3,1024]{2,1,0:T(4,128)(2,1)S(1)}, u32[]{:S(2)}, u32[]{:S(2)}) collective-permute-start(bf16[2,3,1024]{2,1,0:T(4,128)(2,1)S(1)} %slice.276), channel_id=1, source_target_pairs={{0,4},{4,8},{8,12},{1,5},{5,9},{9,13},{2,6},{6,10},{10,14},{3,7},{... | collective-permute-start | bytes 36872 | tf_op jit(solution)/shard_map/ppermute | solution.py:977
  45.0 95.5 %copy-start.7 = (bf16[2,256,1536]{2,1,0:T(8,128)(2,1)}, bf16[2,256,1536]{2,1,0:T(8,128)(2,1)S(1)}, u32[]{:S(2)}) copy-start(bf16[2,256,1536]{2,1,0:T(8,128)(2,1)S(1)} %constant_dynamic-slice_fusion) | copy-start | bytes 4718596
  123.8 16.7 %slice-start = ((s8[4718592]{0:T(1024)(128)(4,1)}), s8[4194304]{0:T(1024)(128)(4,1)S(1)}, s32[]{:S(2)}) async-start(s8[4718592]{0:T(1024)(128)(4,1)} %bitcast.155), calls=%async_computation | async-start | bytes 8388608
  125.8 6.2 copy-start.15
  125.8 14.7 %slice-start.1 = ((s8[4718592]{0:T(1024)(128)(4,1)}), s8[524288]{0:T(1024)(128)(4,1)S(1)}, s32[]{:S(2)}) async-start(s8[4718592]{0:T(1024)(128)(4,1)} %bitcast.155), calls=%async_computation.1 | async-start | bytes 1048576
  132.0 1.9 copy-start.3
  133.9 9.2 %collective-permute-start.1 = (bf16[2,3,1024]{2,1,0:T(4,128)(2,1)S(1)}, bf16[2,3,1024]{2,1,0:T(4,128)(2,1)S(1)}, u32[]{:S(2)}, u32[]{:S(2)}) collective-permute-start(bf16[2,3,1024]{2,1,0:T(4,128)(2,1)S(1)} %slice.275), channel_id=1, source_target_pairs={{0,4},{4,8},{8,12},{1,5},{5,9},{9,13},{2,6},{6,10},{10,14},{3,7},{... | collective-permute-start | bytes 36872 | tf_op jit(solution)/shard_map/ppermute | solution.py:977
  150.5 22.2 %slice-start.2 = ((s8[4718592]{0:T(1024)(128)(4,1)}), s8[4194304]{0:T(1024)(128)(4,1)S(1)}, s32[]{:S(2)}) async-start(s8[4718592]{0:T(1024)(128)(4,1)} %bitcast.157), calls=%async_computation.2 | async-start | bytes 8388608
  164.4 8.3 %slice-start.3 = ((s8[4718592]{0:T(1024)(128)(4,1)}), s8[524288]{0:T(1024)(128)(4,1)S(1)}, s32[]{:S(2)}) async-start(s8[4718592]{0:T(1024)(128)(4,1)} %bitcast.157), calls=%async_computation.3 | async-start | bytes 1048576
  251.8 25.7 %copy-start.4 = (bf16[512,1536]{1,0:T(8,128)(2,1)S(1)}, bf16[512,1536]{1,0:T(8,128)(2,1)}, u32[]{:S(2)}) copy-start(bf16[512,1536]{1,0:T(8,128)(2,1)} %get-tuple-element.74.u) | copy-start | bytes 4718596
  251.8 25.7 %copy-start.10 = (bf16[512,1536]{1,0:T(8,128)(2,1)S(1)}, bf16[512,1536]{1,0:T(8,128)(2,1)}, u32[]{:S(2)}) copy-start(bf16[512,1536]{1,0:T(8,128)(2,1)} %get-tuple-element.82) | copy-start | bytes 4718596
  276.0 5.8 collective-permute-start.2
  294.5 39.7 %copy-start.17 = (f32[2,256,768]{2,1,0:T(8,128)S(1)}, f32[2,256,768]{2,1,0:T(8,128)}, u32[]{:S(2)}) copy-start(f32[2,256,768]{2,1,0:T(8,128)} %get-tuple-element.91.y) | copy-start | bytes 4718596
  396.5 4.6 copy-start.5
  397.5 21.1 %collective-permute-start.3 = (f32[2,3,1024]{2,1,0:T(4,128)S(1)}, f32[2,3,1024]{2,1,0:T(4,128)S(1)}, u32[]{:S(2)}, u32[]{:S(2)}) collective-permute-start(f32[2,3,1024]{2,1,0:T(4,128)S(1)} %slice.178), channel_id=1, source_target_pairs={{4,0},{8,4},{12,8},{5,1},{9,5},{13,9},{6,2},{10,6},{14,10},{7,3},{... | collective-permute-start | bytes 73736 | tf_op jit(solution)/shard_map/ppermute | solution.py:977
  683.1 7.3 %copy-start.18 = (bf16[4,80,1536]{2,1,0:T(8,128)(2,1)S(1)}, bf16[4,80,1536]{2,1,0:T(8,128)(2,1)}, u32[]{:S(2)}) copy-start(bf16[4,80,1536]{2,1,0:T(8,128)(2,1)} %get-tuple-element.110) | copy-start | bytes 2949124
  687.7 10.8 %copy-start.8 = (bf16[512,1536]{1,0:T(8,128)(2,1)S(1)}, bf16[512,1536]{1,0:T(8,128)(2,1)}, u32[]{:S(2)}) copy-start(bf16[512,1536]{1,0:T(8,128)(2,1)} %get-tuple-element.90.go) | copy-start | bytes 4718596
  687.7 10.8 %copy-start.11 = (bf16[512,1536]{1,0:T(8,128)(2,1)S(1)}, bf16[512,1536]{1,0:T(8,128)(2,1)}, u32[]{:S(2)}) copy-start(bf16[512,1536]{1,0:T(8,128)(2,1)} %get-tuple-element.99) | copy-start | bytes 4718596
  704.2 1.4 copy-start.9
  704.2 1.9 copy-start.12
  706.1 1.4 copy-start.13
  706.1 1.9 copy-start.14
  706.1 5.0 copy-start.1
  709.4 1.7 copy-start.16

commit v2 on v1

v2 whole, which is shorter than its diff:
```python
import functools

import jax
import jax.numpy as jnp
from jax import lax
from jax.experimental import pallas as pl
from jax.experimental.pallas import tpu as pltpu
from jax.sharding import PartitionSpec as P

EPSILON = 1e-05
MESH = pl.DeviceIdType.MESH
HIGH = lax.Precision.HIGHEST
BF = jnp.bfloat16
F32 = jnp.float32
LANES = 128
VMEM_LIMIT = 56 * 2**20


def shape(dims, kind):
    return jax.ShapeDtypeStruct(dims, kind)


def dot(a, b, dims=((1,), (0,)), precision=None):
    return lax.dot_general(a, b, (dims, ((), ())), precision=precision, preferred_element_type=F32)


NT = ((1,), (1,))
TN = ((0,), (0,))


def halves(v):
    high = v.astype(BF)
    return high, (v - high.astype(F32)).astype(BF)


def dot_mask(v, mask, dims=((1,), (0,))):
    high, rest = halves(v)
    return dot(high, mask, dims) + dot(rest, mask, dims)


def dot3(a, b, dims=((1,), (0,))):
    a_high, a_rest = halves(a)
    b_high, b_rest = halves(b)
    return dot(a_high, b_high, dims) + dot(a_rest, b_high, dims) + dot(a_high, b_rest, dims)


def mask_dot(mask, v):
    high, rest = halves(v)
    return dot(mask, high) + dot(mask, rest)


def head_mask(width, heads):
    size = width // heads
    return (
        lax.broadcasted_iota(jnp.int32, (LANES, width), 0)
        == lax.broadcasted_iota(jnp.int32, (LANES, width), 1) // size
    ).astype(F32).astype(BF)


def order_mask(n, lower):
    rows = lax.broadcasted_iota(jnp.int32, (n, n), 0)
    columns = lax.broadcasted_iota(jnp.int32, (n, n), 1)
    return (rows >= columns) if lower else (rows <= columns)


def sigmoid(v):
    return 1.0 / (1.0 + jnp.exp(-v))


def softplus(v):
    return jnp.maximum(v, 0.0) + jnp.log1p(jnp.exp(-jnp.abs(v)))


def column(row_block):
    n = row_block.shape[1]
    return [
        jnp.transpose(jnp.broadcast_to(row_block[i : i + 1, :], (LANES, n))) for i in range(2)
    ]


def rows_of(columns):
    n = columns[0].shape[0]
    rows = [jnp.transpose(jnp.broadcast_to(c, (n, LANES)))[0:1] for c in columns]
    return jnp.concatenate(rows + [jnp.zeros((8 - len(rows), n), F32)], axis=0)


def conv_pre(ext, proj_xbc, halo, taps, bias):
    n = proj_xbc.shape[0]
    ext[0:8, :] = halo
    ext[8 : 8 + n, :] = proj_xbc
    pre = bias + taps[3:4, :] * proj_xbc
    for k in range(3):
        pre = pre + taps[k : k + 1, :] * ext[5 + k : 5 + k + n, :]
    return pre


def push(src, dst, send, recv, device):
    copy = pltpu.make_async_remote_copy(
        src_ref=src, dst_ref=dst, send_sem=send, recv_sem=recv, device_id=device, device_id_type=MESH
    )
    copy.start()
    return copy


def both_layers_kernel(places, *refs):
    count = len(places)
    ins, outs = refs[:count], refs[count:-3]
    send, recv, local = refs[-3:]
    me = lax.axis_index("section")
    other = {"section": 1 - me}
    barrier = pltpu.get_barrier_semaphore()
    pl.semaphore_signal(barrier, inc=1, device_id=other, device_id_type=MESH)
    pl.semaphore_wait(barrier, 1)
    copies = []
    for i, (which, start) in enumerate(places):
        target = outs[which].at[me, :, pl.ds(start, ins[i].shape[1])]
        copies.append(push(ins[i], target, send.at[i], recv.at[i], other))
        own = pltpu.make_async_copy(ins[i], target, local.at[i])
        own.start()
        copies.append(own)
    for copy in copies:
        copy.wait()


def both_layers(groups):
    places, flat, outs = [], [], []
    for i, group in enumerate(groups):
        start = 0
        for a in group:
            places.append((i, start))
            flat.append(a)
            start += a.shape[1]
        outs.append(shape((2, group[0].shape[0], start), group[0].dtype))
    count = len(flat)
    vm = pl.BlockSpec(memory_space=pltpu.VMEM)
    anywhere = pl.BlockSpec(memory_space=pl.ANY)
    return pl.pallas_call(
        functools.partial(both_layers_kernel, places),
        out_shape=tuple(outs),
        in_specs=[vm] * count,
        out_specs=(anywhere,) * len(outs),
        scratch_shapes=[pltpu.SemaphoreType.DMA((count,)) for _ in range(3)],
        compiler_params=pltpu.CompilerParams(
            collective_id=0, has_side_effects=True, vmem_limit_bytes=VMEM_LIMIT
        ),
        name="both_layers",
    )(*flat)


class Line:
    def __init__(self, forward, size, parts, outgoing, incoming, send, recv):
        self.me = lax.axis_index("seq")
        self.size, self.parts = size, parts
        self.outgoing, self.incoming, self.send, self.recv = outgoing, incoming, send, recv
        first, last = self.me == 0, self.me == size - 1
        self.starts, self.ends = (first, last) if forward else (last, first)
        self.place = self.me if forward else size - 1 - self.me
        step = 1 if forward else -1
        self.target, self.source = {"seq": self.me + step}, {"seq": self.me - step}

    def greet(self, barrier):
        @pl.when(jnp.logical_not(self.starts))
        def _():
            pl.semaphore_signal(barrier, inc=1, device_id=self.source, device_id_type=MESH)

    def met(self, barrier, others=0):
        @pl.when(jnp.logical_not(self.ends))
        def _():
            pl.semaphore_wait(barrier, others + 1)

        if others:

            @pl.when(self.ends)
            def _():
                pl.semaphore_wait(barrier, others)

    def copy(self, m, p):
        width = self.outgoing.shape[2] // self.parts
        at = pl.ds(p * width, width)
        return pltpu.make_async_remote_copy(
            src_ref=self.outgoing.at[m, :, at],
            dst_ref=self.incoming.at[m, :, at],
            send_sem=self.send.at[m * self.parts + p],
            recv_sem=self.recv.at[m * self.parts + p],
            device_id=self.target,
            device_id_type=MESH,
        )

    def begin(self, m, own):
        @pl.when(self.starts)
        def _():
            self.incoming[m] = jnp.zeros_like(self.incoming[m])
            self.outgoing[m] = own.astype(self.outgoing.dtype)
            for p in range(self.parts):
                self.copy(m, p).start()

    def relay(self, own, decay, at_step, steps, lag, apart):
        width = self.outgoing.shape[2] // self.parts
        for i in range(self.outgoing.shape[0] * self.parts):
            m, p = i // self.parts, i % self.parts
            at = slice(p * width, (p + 1) * width)
            due = jnp.minimum(self.place * lag + apart * i, steps - 1)

            @pl.when(jnp.logical_and(self.place > 0, due == at_step))
            def _():
                self.copy(m, p).wait_recv()

                @pl.when(jnp.logical_not(self.ends))
                def _():
                    passed = decay[m, 0:1, at] * self.incoming[m, :, at].astype(F32) + own[m, :, at]
                    self.outgoing[m, :, at] = passed.astype(self.outgoing.dtype)
                    self.copy(m, p).start()

    def finish(self):
        @pl.when(jnp.logical_not(self.ends))
        def _():
            for m in range(self.outgoing.shape[0]):
                for p in range(self.parts):
                    self.copy(m, p).wait_send()

    def halo(self, src, dst, m, send, recv):
        return pltpu.make_async_remote_copy(
            src_ref=src, dst_ref=dst, send_sem=send.at[m], recv_sem=recv.at[m],
            device_id=self.target, device_id_type=MESH,
        )


PARTS = 3


def ssd_fwd_kernel(dims, size, heads_axis, full, has_dyn, *refs):
    proj, taps, bias, dt_bias, a_neg, skip, gain = refs[:7]
    dyn = refs[7] if has_dyn else None
    (cx, dt_o, cum_o, state, halo, y_o, yn_o, stats_o,
     ext, own, decay, rim, outgoing, incoming, gates, square, square_got,
     send, recv, halo_send, halo_recv, stat_send, stat_recv) = refs[7 + has_dyn :]
    heads, inner, states = dims
    batch, n = proj.shape[0], proj.shape[1]
    wide = inner + 2 * states
    head_lanes = inner // heads
    columns = slice(inner, inner + wide)
    line = Line(True, size, PARTS, outgoing, incoming, send, recv)
    head = lax.axis_index("head")
    peers = [{"head": lax.rem(head + d, heads_axis)} for d in range(1, heads_axis)]
    barrier = pltpu.get_barrier_semaphore()
    line.greet(barrier)
    for peer in peers:
        pl.semaphore_signal(barrier, inc=1, device_id=peer, device_id_type=MESH)
    for m in range(batch):
        rim[m] = proj[m, n - 16 :, columns].astype(BF)
    line.met(barrier, len(peers))

    @pl.when(jnp.logical_not(line.ends))
    def _():
        for m in range(batch):
            line.halo(rim.at[m], halo.at[m], m, halo_send, halo_recv).start()

    @pl.when(line.starts)
    def _():
        halo[...] = jnp.zeros_like(halo)

    expand = head_mask(inner, heads)
    for m in range(batch):

        @pl.when(jnp.logical_not(line.starts))
        def _():
            line.halo(rim.at[m], halo.at[m], m, halo_send, halo_recv).wait_recv()

        xbc = proj[m, :, columns].astype(BF).astype(F32)
        pre = conv_pre(ext, xbc, halo[m, 8:].astype(F32), taps[...], bias[...])
        act = pre * sigmoid(pre)
        cx[m] = act
        dt = softplus(proj[m, :, inner + wide :] + dt_bias[...])
        cum = mask_dot(order_mask(n, True).astype(F32).astype(BF), dt * a_neg[...])
        dt_o[m] = dt
        cum_o[m] = cum
        last = cum[n - 1 : n, :]
        weight = dot_mask(jnp.exp(last - cum) * dt, expand)
        mine = dot3(act[:, inner : inner + states], act[:, :inner] * weight, TN)
        own[m] = mine
        decay[m] = dot_mask(jnp.broadcast_to(jnp.exp(last), (8, LANES)), expand)
        line.begin(m, mine)
    keep = order_mask(n, True)
    first = lax.broadcasted_iota(jnp.int32, (n, LANES), 1) < head_lanes
    pairs = heads // 2
    for m in range(batch):
        scores = dot3(cx[m, :, inner + states :], cx[m, :, inner : inner + states], NT)
        cums = cum_o[m]
        cums_t = jnp.transpose(cums)
        dt_wide = dot_mask(dt_o[m], expand)
        for p in range(pairs):

            line.relay(own, decay, m * pairs + p, batch * pairs, 4, 2)
            lanes = slice(p * LANES, (p + 1) * LANES)
            x = cx[m, :, lanes]
            dtx, dtx_rest = halves(x * dt_wide[:, lanes])
            both = []
            for h in (2 * p, 2 * p + 1):
                lag = jnp.where(keep, cums[:, h : h + 1] - cums_t[h : h + 1, :], -1e30)
                high, rest = halves(scores * jnp.exp(lag))
                both.append(dot(high, dtx) + dot(rest, dtx) + dot(high, dtx_rest))
            y_o[m, :, lanes] = skip[:, lanes] * x + jnp.where(first, both[0], both[1])
    for m in range(batch):
        entered = incoming[m]
        state[m] = entered
        y = y_o[m] + dot_mask(jnp.exp(cum_o[m]), expand) * dot3(cx[m, :, inner + states :], entered)
        y_o[m] = y
        z = proj[m, :, :inner]
        gated = y * z * sigmoid(z)
        gates[m] = gated
        stats = [jnp.sum(gated * gated, axis=1, keepdims=True)]
        if has_dyn:
            stats.append(jnp.sum(gated * gain[...] * dyn[m], axis=1, keepdims=True))
        square[m] = rows_of(stats)
    copies = [
        push(square, square_got.at[d], stat_send.at[d], stat_recv.at[d], peer) for d, peer in enumerate(peers)
    ]
    for copy in copies:
        copy.wait()
    for m in range(batch):
        total = square[m]
        for d in range(heads_axis - 1):
            total = total + square_got[d, m]
        gs = lax.rsqrt(total[0:1] / full + EPSILON)
        stats_o[m] = jnp.concatenate([gs, total[1:]], axis=0)
        yn_o[m] = (gates[m] * column(stats_o[m])[0][:, 0:1] * gain[...]).astype(BF)
    line.finish()

    @pl.when(jnp.logical_not(line.ends))
    def _():
        for m in range(batch):
            line.halo(rim.at[m], halo.at[m], m, halo_send, halo_recv).wait_send()


def ssd_fwd(proj, taps, bias, dt_bias, a_neg, skip, gain, dyn, dims, size, heads_axis, full):
    heads, inner, states = dims
    batch, n, _ = proj.shape
    wide = inner + 2 * states
    vm = pl.BlockSpec(memory_space=pltpu.VMEM)
    has_dyn = dyn is not None
    moved = (batch, states, inner)
    outs = (
        shape((batch, n, wide), F32),
        shape((batch, n, LANES), F32),
        shape((batch, n, LANES), F32),
        shape(moved, F32),
        shape((batch, 16, wide), BF),
        shape((batch, n, inner), F32),
        shape((batch, n, inner), BF),
        shape((batch, 8, n), F32),
    )
    return pl.pallas_call(
        functools.partial(ssd_fwd_kernel, dims, size, heads_axis, full, has_dyn),
        out_shape=outs,
        in_specs=[vm] * (7 + has_dyn),
        out_specs=(vm,) * len(outs),
        scratch_shapes=[
            pltpu.VMEM((n + 8, wide), F32),
            pltpu.VMEM(moved, F32),
            pltpu.VMEM((batch, 8, inner), F32),
            pltpu.VMEM((batch, 16, wide), BF),
            pltpu.VMEM(moved, F32),
            pltpu.VMEM(moved, F32),
            pltpu.VMEM((batch, n, inner), F32),
            pltpu.VMEM((batch, 8, n), F32),
            pltpu.VMEM((heads_axis - 1, batch, 8, n), F32),
            pltpu.SemaphoreType.DMA((batch * PARTS,)),
            pltpu.SemaphoreType.DMA((batch * PARTS,)),
            pltpu.SemaphoreType.DMA((batch,)),
            pltpu.SemaphoreType.DMA((batch,)),
            pltpu.SemaphoreType.DMA((heads_axis - 1,)),
            pltpu.SemaphoreType.DMA((heads_axis - 1,)),
        ],
        compiler_params=pltpu.CompilerParams(
            collective_id=1 + has_dyn, has_side_effects=True, vmem_limit_bytes=VMEM_LIMIT
        ),
        name="ssd_fwd",
    )(proj, taps, bias, dt_bias, a_neg, skip, gain, *([dyn] if has_dyn else []))


def ssd_bwd_kernel(
    dims, size, heads_axis, full, has_across,
    dyn, y, proj, halo, cx, dt, cum, state, stats, taps, bias, dt_bias, a_neg, skip, gain, *refs
):
    if has_across:
        h_rows, h_whole, h_o, *refs = refs[:2] + refs[6:7] + refs[2:6] + refs[7:]
        *refs, c_local, c_send, c_recv = refs
    (
    g_in, gate_o, conv_o, small_o,
    dy, dxw, dpre, own, decay, ext, rowq, colq, d_scores, outgoing, incoming, rim, square, square_got,
    send, recv, rim_send, rim_recv, stat_send, stat_recv,
    ) = refs
    heads, inner, states = dims
    batch, n = dyn.shape[0], dyn.shape[1]
    wide = inner + 2 * states
    columns = slice(inner, inner + wide)
    size_p = inner // heads
    pairs = heads // 2
    line = Line(False, size, PARTS, outgoing, incoming, send, recv)
    head = lax.axis_index("head")
    peers = [{"head": lax.rem(head + d, heads_axis)} for d in range(1, heads_axis)]
    barrier = pltpu.get_barrier_semaphore()
    line.greet(barrier)
    if has_across:
        outputs = Collect(1, heads_axis, h_rows, h_whole, h_o, c_local, c_send, c_recv)
        peers = outputs.greeted()
    for peer in peers:
        pl.semaphore_signal(barrier, inc=1, device_id=peer, device_id_type=MESH)
    if not has_across:
        for m in range(batch):
            z = proj[m, :, :inner]
            square[m] = rows_of([jnp.sum(dyn[m] * gain[...] * y[m] * z * sigmoid(z), axis=1, keepdims=True)])
    line.met(barrier, len(peers))
    if has_across:
        outputs.start()
    else:
        copies = [
            push(square, square_got.at[d], stat_send.at[d], stat_recv.at[d], peers[d])
            for d in range(heads_axis - 1)
        ]
    expand = head_mask(inner, heads)
    if not has_across:
        for copy in copies:
            copy.wait()
    for m in range(batch):
        gs, across = [v[:, 0:1] for v in column(stats[m])]
        if has_across:
            pass
        else:
            total = square[m]
            for d in range(heads_axis - 1):
                total = total + square_got[d, m]
            across = column(total)[0][:, 0:1]
        z = proj[m, :, :inner]
        sig = sigmoid(z)
        yv = y[m]
        gated = yv * z * sig
        dynv = dyn[m]
        scaled = gated * gs
        gate_o[m] = jnp.broadcast_to(jnp.sum(dynv * scaled, axis=0, keepdims=True), (8, inner))
        dgated = gs * gain[...] * dynv - gated * (gs * gs * gs * across / full)
        dyv = dgated * z * sig
        dy[m] = dyv
        g_in[m, :, :inner] = (dgated * yv * sig * (1.0 + z * (1.0 - sig))).astype(BF)
        cums = cum[m]
        moved = dot_mask(jnp.exp(cums), expand) * dyv
        mine = dot3(cx[m, :, inner + states :], moved, TN)
        own[m] = mine
        decay[m] = dot_mask(jnp.broadcast_to(jnp.exp(cums[n - 1 : n, :]), (8, LANES)), expand)
        line.begin(m, mine)
    keep = order_mask(n, False)
    lane = lax.broadcasted_iota(jnp.int32, (n, LANES), 1)
    first = lane < size_p
    rowq[...] = jnp.zeros_like(rowq)
    for m in range(batch):
        scores_t = dot3(cx[m, :, inner : inner + states], cx[m, :, inner + states :], NT)
        cums = cum[m]
        cums_t = jnp.transpose(cums)
        dt_wide = dot_mask(dt[m], expand)
        colq[m] = jnp.zeros_like(colq[m])
        d_scores[m] = jnp.zeros_like(d_scores[m])
        for p in range(pairs):

            line.relay(own, decay, m * pairs + p, batch * pairs, 2, 1)
            lanes = slice(p * LANES, (p + 1) * LANES)
            dtx = cx[m, :, lanes] * dt_wide[:, lanes]
            dyb, dy_rest = halves(dy[m, :, lanes])
            both = []
            for j, h in enumerate((2 * p, 2 * p + 1)):
                lag = jnp.where(keep, cums_t[h : h + 1, :] - cums[:, h : h + 1], -1e30)
                decays = jnp.exp(lag)
                weights = scores_t * decays
                mine, mine_rest = halves(jnp.where(first if j == 0 else jnp.logical_not(first), dtx, 0.0))
                d_weights = dot(mine, dyb, NT) + dot(mine, dy_rest, NT) + dot(mine_rest, dyb, NT)
                q = d_weights * weights
                d_scores[m] += d_weights * decays
                rowq[m, h : h + 1, :] = jnp.sum(q, axis=0, keepdims=True)
                colq[m] += jnp.where(lane == h, jnp.sum(q, axis=1, keepdims=True), 0.0)
                both.append(dot(weights.astype(BF), dyb))
            dxw[m, :, lanes] = jnp.where(first, both[0], both[1])
    fold = lambda v: dot_mask(v, expand, NT)
    for m in range(batch):
        x = cx[m, :, :inner]
        b = cx[m, :, inner : inner + states]
        c = cx[m, :, inner + states :]
        b_high, b_rest = halves(b)
        dyv, dxv, dtv, cums = dy[m], dxw[m], dt[m], cum[m]
        last = cums[n - 1 : n, :]
        entered, later_b = state[m], incoming[m]
        moved = dot_mask(jnp.exp(cums), expand) * dyv
        carried = dot3(c, entered)
        tail = jnp.exp(last - cums)
        weight = tail * dtv
        weight_wide = dot_mask(weight, expand)
        pulled = dot(b_high, later_b) + dot(b_rest, later_b)
        dx = dot_mask(dtv, expand) * dxv + weight_wide * pulled + skip[...] * dyv
        dw = fold(x * pulled)
        wdw = weight * dw
        change = jnp.transpose(rowq[m]) + fold(carried * moved) - colq[m] - wdw
        ends = jnp.sum(entered * later_b.astype(F32), axis=0, keepdims=True)
        ends = jnp.sum(wdw, axis=0, keepdims=True) + jnp.exp(last) * fold(jnp.broadcast_to(ends, (8, inner)))[0:1]
        log_grad = mask_dot(order_mask(n, False).astype(F32).astype(BF), change) + ends
        ddt = fold(x * dxv) + tail * dw + a_neg[...] * log_grad
        ddt_raw = ddt * sigmoid(proj[m, :, inner + wide :] + dt_bias[...])
        g_in[m, :, inner + wide :] = ddt_raw.astype(BF)
        small_o[m] = jnp.concatenate(
            [
                jnp.sum(ddt_raw, axis=0, keepdims=True),
                jnp.sum(dtv * log_grad, axis=0, keepdims=True) * a_neg[...],
                fold(jnp.broadcast_to(jnp.sum(x * dyv, axis=0, keepdims=True), (8, inner)))[0:1],
                jnp.zeros((5, LANES), F32),
            ],
            axis=0,
        )
        xw_high, xw_rest = halves(x * weight_wide)
        dc = dot3(d_scores[m], b, TN) + dot3(moved, entered, NT)
        db = dot3(d_scores[m], c) + dot(xw_high, later_b, NT) + dot(xw_rest, later_b, NT)
        xbc = proj[m, :, columns].astype(BF).astype(F32)
        pre = conv_pre(ext, xbc, halo[m, 8:].astype(F32), taps[...], bias[...])
        sig = sigmoid(pre)
        d_act = jnp.concatenate([dx, db, dc], axis=1) * sig * (1.0 + pre * (1.0 - sig))
        dpre[m, 0:n, :] = d_act
        rim_copy = line.halo(dpre.at[m, pl.ds(0, 8)], rim.at[m], m, rim_send, rim_recv)
        pl.when(jnp.logical_not(line.ends))(rim_copy.start)
        rows = [jnp.sum(d_act * ext[5 + k : 5 + k + n, :], axis=0, keepdims=True) for k in range(4)]
        rows.append(jnp.sum(d_act, axis=0, keepdims=True))
        conv_o[m] = jnp.concatenate(rows + [jnp.zeros((3, wide), F32)], axis=0)

    @pl.when(line.starts)
    def _():
        rim[...] = jnp.zeros_like(rim)

    for m in range(batch):
        rim_copy = line.halo(dpre.at[m, pl.ds(0, 8)], rim.at[m], m, rim_send, rim_recv)
        pl.when(jnp.logical_not(line.starts))(rim_copy.wait_recv)
        dpre[m, n : n + 8, :] = rim[m]
        total = taps[3:4, :] * dpre[m, 0:n, :]
        for k in range(3):
            total = total + taps[k : k + 1, :] * dpre[m, 3 - k : 3 - k + n, :]
        g_in[m, :, columns] = total.astype(BF)
        pl.when(jnp.logical_not(line.ends))(rim_copy.wait_send)
    line.finish()
    if has_across:
        outputs.finish()


def ssd_bwd(dyn, y, proj, halo, cx, dt, cum, state, stats, taps, bias, dt_bias, a_neg, skip, gain, outputs,
            dims, size, heads_axis, full):
    has_across = bool(outputs)
    heads, inner, states = dims
    batch, n, wide = cx.shape
    vm = pl.BlockSpec(memory_space=pltpu.VMEM)
    moved = (batch, states, inner)
    outs = (
        shape((batch, n, inner + wide + LANES), BF),
        shape((batch, 8, inner), F32),
        shape((batch, 8, wide), F32),
        shape((batch, 8, LANES), F32),
    ) + tuple(shape((2 * a.shape[0], a.shape[1]), BF) for a in outputs[1:])
    sems = lambda k: pltpu.SemaphoreType.DMA((k,))
    return pl.pallas_call(
        functools.partial(ssd_bwd_kernel, dims, size, heads_axis, full, has_across),
        out_shape=outs,
        in_specs=[vm] * (15 + len(outputs)),
        out_specs=(vm,) * 4 + (pl.BlockSpec(memory_space=pl.ANY),) * has_across,
        scratch_shapes=[
            pltpu.VMEM((batch, n, inner), F32),
            pltpu.VMEM((batch, n, inner), F32),
            pltpu.VMEM((batch, n + 8, wide), F32),
            pltpu.VMEM(moved, F32),
            pltpu.VMEM((batch, 8, inner), F32),
            pltpu.VMEM((n + 8, wide), F32),
            pltpu.VMEM((batch, LANES, n), F32),
            pltpu.VMEM((batch, n, LANES), F32),
            pltpu.VMEM((batch, n, n), F32),
            pltpu.VMEM(moved, BF),
            pltpu.VMEM(moved, BF),
            pltpu.VMEM((batch, 8, wide), F32),
            pltpu.VMEM((batch, 8, n), F32),
            pltpu.VMEM((heads_axis - 1, batch, 8, n), F32),
            sems(batch * PARTS),
            sems(batch * PARTS),
            sems(batch),
            sems(batch),
            sems(heads_axis - 1),
            sems(heads_axis - 1),
        ]
        + (collect_sems(heads_axis) if has_across else []),
        compiler_params=pltpu.CompilerParams(
            collective_id=10 + has_across, has_side_effects=True, vmem_limit_bytes=VMEM_LIMIT
        ),
        name="ssd_bwd",
    )(dyn, y, proj, halo, cx, dt, cum, state, stats, taps, bias, dt_bias, a_neg, skip, gain, *outputs)


def greet(size, core=False):
    me = lax.axis_index("head")
    barrier = pltpu.get_barrier_semaphore()
    peers = [{"head": lax.rem(me + d, size)} for d in range(1, size)]
    others = [{"section": 1 - lax.axis_index("section")}] if core else []
    for peer in peers + others:
        pl.semaphore_signal(barrier, inc=1, device_id=peer, device_id_type=MESH)
    pl.semaphore_wait(barrier, len(peers) + len(others))
    return me, peers


def block_of(index, rows):
    return pl.ds(pl.multiple_of(index * rows, rows), rows)


def normal(u, gain):
    uv = u.astype(F32)
    s = lax.rsqrt(jnp.sum(uv * uv, axis=1, keepdims=True) / uv.shape[1] + EPSILON)
    return (uv * s * gain).astype(BF)


def head_fwd_kernel(size, onward, yn, w_out, u, *refs):
    if onward:
        w_in, gain, h_o, normed_o, proj_o, out, got, send, recv = refs
    else:
        h_o, out, got, send, recv = refs
    rows = yn.shape[0] // size
    me, peers = greet(size)
    copies = []
    for d, peer in enumerate(peers):
        to = lax.rem(me + d + 1, size)
        out[d] = dot(yn[block_of(to, rows), :], w_out[...]).astype(out.dtype)
        copies.append(push(out.at[d], got.at[d], send.at[0, d], recv.at[0, d], peer))
    mine = block_of(me, rows)
    total = dot(yn[mine, :], w_out[...])
    for copy in copies:
        copy.wait()
    for d in range(size - 1):
        total = total + got[d].astype(F32)
    h = (u[mine, :].astype(F32) + total).astype(BF)
    if not onward:
        h_o[...] = h
        return
    h_o[mine, :] = h
    copies = [
        push(h_o.at[mine], h_o.at[mine], send.at[1, d], recv.at[1, d], peer) for d, peer in enumerate(peers)
    ]

    def project(at):
        normed = normal(h_o[at, :], gain[...])
        normed_o[at, :] = normed
        proj_o[at, :] = dot(normed, w_in[...])

    project(mine)
    for d, copy in enumerate(copies):
        copy.wait_recv()
        project(block_of(lax.rem(me + size - d - 1, size), rows))
    for copy in copies:
        copy.wait_send()


def head_fwd(yn, w_out, u, size, onward):
    n, d_model = u.shape
    rows = n // size
    vm = pl.BlockSpec(memory_space=pltpu.VMEM)
    kind = F32 if onward else BF
    outs = [shape((n if onward else rows, d_model), BF)]
    if onward:
        outs += [shape((n, d_model), BF), shape((n, onward[0].shape[1]), F32)]
    return pl.pallas_call(
        functools.partial(head_fwd_kernel, size, bool(onward)),
        out_shape=tuple(outs),
        in_specs=[vm] * (3 + len(onward)),
        out_specs=(vm,) * len(outs),
        scratch_shapes=[
            pltpu.VMEM((size - 1, rows, d_model), kind),
            pltpu.VMEM((size - 1, rows, d_model), kind),
            pltpu.SemaphoreType.DMA((2, size - 1)),
            pltpu.SemaphoreType.DMA((2, size - 1)),
        ],
        compiler_params=pltpu.CompilerParams(
            collective_id=3 if onward else 6, has_side_effects=True, vmem_limit_bytes=VMEM_LIMIT
        ),
        name="head_fwd",
    )(yn, w_out, u, *onward)


def input_gradient(dn, u, gain, above):
    uv = u.astype(F32)
    width = uv.shape[1]
    s = lax.rsqrt(jnp.sum(uv * uv, axis=1, keepdims=True) / width + EPSILON)
    scaled = dn * gain
    inner = jnp.sum(scaled * uv, axis=1, keepdims=True)
    return (
        above.astype(F32) + s * scaled - uv * (s * s * s * inner / width),
        jnp.sum(dn * uv * s, axis=0, keepdims=True),
    )


def body_tile(normed, g_in, yn, go, half, i):
    tile, count = 256, normed.shape[1] // 256
    wide = yn.shape[1]
    at = pl.ds(pl.multiple_of(half * wide, wide), wide)
    if i < count:
        return dot(normed[:, i * tile : (i + 1) * tile], g_in[:, at], TN)
    return dot(yn[:, (i - count) * tile : (i - count + 1) * tile], go[:, at], TN)


def head_bwd_kernel(size, g_in, w_in, upper, u, gain, w_out, normed, yn, du_o, mine_o, grad_o, dyn_o, body_o,
                    out, got, body_send, body_got, send, recv, body_ss, body_rs):
    rows = u.shape[0] // size
    me, peers = greet(size, core=True)
    layer = lax.axis_index("section")
    other = {"section": 1 - layer}
    copies = []
    for d, peer in enumerate(peers):
        to = lax.rem(me + d + 1, size)
        out[d] = dot(g_in[block_of(to, rows), :], w_in[...], NT).astype(BF)
        copies.append(push(out.at[d], got.at[d], send.at[0, d], recv.at[0, d], peer))
    mine = block_of(me, rows)
    dn = dot(g_in[mine, :], w_in[...], NT)
    tiles = body_o.shape[0] // 256
    body_copies = []
    for i in range(tiles):
        at = pl.ds(i * 256, 256)
        body_send[at, :] = body_tile(normed, g_in, yn, upper, 1 - layer, i).astype(BF)
        body_copies.append(push(body_send.at[at], body_got.at[at], body_ss.at[i], body_rs.at[i], other))
    for i in range(tiles):
        body_o[i * 256 : (i + 1) * 256, :] = body_tile(normed, g_in, yn, upper, layer, i).astype(BF)
    for copy in copies:
        copy.wait()
    for d in range(size - 1):
        dn = dn + got[d].astype(F32)
    du, grad = input_gradient(dn, u[mine, :], gain[...], upper[mine, :])
    grad_o[...] = jnp.broadcast_to(grad, grad_o.shape)
    mine_o[...] = du
    du_o[mine, :] = du.astype(BF)
    copies = [
        push(du_o.at[mine], du_o.at[mine], send.at[1, d], recv.at[1, d], peer) for d, peer in enumerate(peers)
    ]
    for i in range(tiles):
        at = slice(i * 256, (i + 1) * 256)
        body_copies[i].wait()
        body_o[at, :] = (body_o[at, :].astype(F32) + body_got[at, :].astype(F32)).astype(BF)
    dyn_o[mine, :] = dot(du_o[mine, :], w_out[...], NT)
    for d, copy in enumerate(copies):
        copy.wait_recv()
        at = block_of(lax.rem(me + size - d - 1, size), rows)
        dyn_o[at, :] = dot(du_o[at, :], w_out[...], NT)
    for copy in copies:
        copy.wait_send()


def head_bwd(g_in, w_in, upper, u, gain, w_out, normed, yn, size):
    n, d_model = u.shape
    inner = yn.shape[1]
    rows = n // size
    tiles = (d_model + inner) // 256
    body = (d_model + inner, d_model // 2)
    vm = pl.BlockSpec(memory_space=pltpu.VMEM)
    return pl.pallas_call(
        functools.partial(head_bwd_kernel, size),
        out_shape=(
            shape((n, d_model), BF),
            shape((rows, d_model), F32),
            shape((8, d_model), F32),
            shape((n, inner), F32),
            shape(body, BF),
        ),
        in_specs=[vm] * 8,
        out_specs=(vm,) * 5,
        scratch_shapes=[
            pltpu.VMEM((size - 1, rows, d_model), BF),
            pltpu.VMEM((size - 1, rows, d_model), BF),
            pltpu.VMEM(body, BF),
            pltpu.VMEM(body, BF),
            pltpu.SemaphoreType.DMA((2, size - 1)),
            pltpu.SemaphoreType.DMA((2, size - 1)),
            pltpu.SemaphoreType.DMA((tiles,)),
            pltpu.SemaphoreType.DMA((tiles,)),
        ],
        compiler_params=pltpu.CompilerParams(
            collective_id=5, has_side_effects=True, vmem_limit_bytes=VMEM_LIMIT
        ),
        name="head_bwd",
    )(g_in, w_in, upper, u, gain, w_out, normed, yn)


class Collect:
    def __init__(self, by_rows, size, rows, whole, out, local, send, recv):
        self.by_rows, self.size = by_rows, size
        self.rows, self.whole, self.out = rows, whole, out
        self.local, self.send, self.recv = local, send, recv
        self.core, self.head = lax.axis_index("section"), lax.axis_index("head")
        count = rows.shape[0]
        self.row_part = pl.ds(pl.multiple_of(self.core * whole.shape[0] + self.head * count, count), count)
        self.whole_part = block_of(self.core, whole.shape[0])

    def greeted(self):
        return [
            {"section": lax.rem(self.core + c, 2), "head": lax.rem(self.head + d, self.size)}
            for c in range(2)
            for d in range(self.size)
            if c or d
        ]

    def row_copy(self, sender, d):
        return pltpu.make_async_remote_copy(
            src_ref=self.rows, dst_ref=self.out.at[self.row_part],
            send_sem=self.send.at[d], recv_sem=self.recv.at[sender * self.size + d],
            device_id={"section": self.by_rows, "head": lax.rem(self.head + d, self.size)}, device_id_type=MESH,
        )

    def whole_copy(self):
        return pltpu.make_async_remote_copy(
            src_ref=self.whole, dst_ref=self.out.at[self.whole_part],
            send_sem=self.send.at[self.size], recv_sem=self.recv.at[2 * self.size],
            device_id={"section": 1 - self.by_rows}, device_id_type=MESH,
        )

    def start(self):
        @pl.when(self.core == self.by_rows)
        def _():
            pltpu.make_async_copy(self.rows, self.out.at[self.row_part], self.local).start()
            for d in range(1, self.size):
                self.row_copy(self.by_rows, d).start()
            self.whole_copy().start()

        @pl.when(self.core != self.by_rows)
        def _():
            pltpu.make_async_copy(self.whole, self.out.at[self.whole_part], self.local).start()
            for d in range(self.size):
                self.row_copy(1 - self.by_rows, d).start()

    def finish(self):
        @pl.when(self.core == self.by_rows)
        def _():
            pltpu.make_async_copy(self.rows, self.out.at[self.row_part], self.local).wait()
            for d in range(1, self.size):
                self.row_copy(self.by_rows, d).wait()
            for d in range(self.size):
                self.row_copy(1 - self.by_rows, d).wait_recv()
            self.whole_copy().wait_send()

        @pl.when(self.core != self.by_rows)
        def _():
            pltpu.make_async_copy(self.whole, self.out.at[self.whole_part], self.local).wait()
            for d in range(self.size):
                self.row_copy(1 - self.by_rows, d).wait_send()
            self.whole_copy().wait_recv()


def collect_sems(size):
    return [
        pltpu.SemaphoreType.DMA,
        pltpu.SemaphoreType.DMA((size + 1,)),
        pltpu.SemaphoreType.DMA((2 * size + 1,)),
    ]


OWN = 32
SHARED = 160
PIECE = 32
TAIL = (OWN + SHARED) // PIECE
FEW = 16


def grad_tail_kernel(dims, normed, g_in, conv, scalars, gate, gain, tail, few):
    heads, inner, states = dims
    half = normed.shape[1] // 2
    split = 2 * inner + 2 * states
    rest = dot(g_in[:, 2 * inner :], normed[...], TN).astype(BF)
    step = (tail.shape[0] - OWN) // 2
    tail[...] = jnp.zeros_like(tail)
    for i in range(2):
        lanes = slice(i * half, (i + 1) * half)
        tail[i * OWN // 2 : (i + 1) * OWN // 2, :] = rest[2 * states : 2 * states + OWN // 2, lanes]
        tail[OWN + i * step : OWN + i * step + 2 * states, :] = rest[: 2 * states, lanes]
    conv_sum, scalar_sum, gate_sum = conv[0], scalars[0], gate[0]
    for i in range(1, conv.shape[0]):
        conv_sum, scalar_sum, gate_sum = conv_sum + conv[i], scalar_sum + scalars[i], gate_sum + gate[i]
    few[...] = jnp.zeros_like(few)
    few[0:5, :] = conv_sum[0:5, :inner]
    few[5:6, :] = gate_sum[0:1]
    for i in range(3):
        few[6:7, i * LANES : (i + 1) * LANES] = scalar_sum[i : i + 1]
    few[8:9, :] = gain[0:1, :half]
    few[9:10, :] = gain[0:1, half:]
    few[10:15, 0 : 2 * states] = conv_sum[0:5, inner:]


def grad_tail(normed, g_in, conv, scalars, gate, gain, dims, head_size):
    heads, inner, states = dims
    width = normed.shape[1]
    vm = pl.BlockSpec(memory_space=pltpu.VMEM)
    return pl.pallas_call(
        functools.partial(grad_tail_kernel, dims),
        out_shape=(shape((OWN + head_size * SHARED, width // 2), BF), shape((FEW, width // 2), F32)),
        in_specs=[vm] * 6,
        out_specs=(vm, vm),
        compiler_params=pltpu.CompilerParams(vmem_limit_bytes=VMEM_LIMIT),
        name="grad_tail",
    )(normed, g_in, conv, scalars, gate, gain)


def grad_sum_kernel(size, heads, skew, g_in, w_in, above, u, gain, normed, yn, go, tail0, tail1, few0, few1, done,
                    out, shared_o, few_o, traded, du_o,
                    own, core, got, shared, shared_core, shared_got, few_core, few_seq, few_head,
                    body_send, du_out, du_got, du_rows, few_mine,
                    cs, cr, rs, rr, bs, br, ts, tr, hs, hr, xs, fs, fr, gs, gr, ds, dr, c_local, c_send, c_recv):
    me, layer, head = lax.axis_index("seq"), lax.axis_index("section"), lax.axis_index("head")
    rows = out.shape[0]
    plain = rows - SHARED
    half = rows // 2
    parts = half // PIECE
    up, down, other = {"seq": me + 1}, {"seq": me - 1}, {"section": 1 - layer}
    peers = [{"head": lax.rem(head + d, heads)} for d in range(1, heads)]
    blocks = [{"seq": lax.rem(me + d, size)} for d in range(1, size)]
    low_end, high_end = me == 0, me == size - 1
    barrier = pltpu.get_barrier_semaphore()
    inputs = Collect(0, heads, du_rows, go, du_o, c_local, c_send, c_recv)
    plane = inputs.greeted()
    for peer in plane + blocks:
        pl.semaphore_signal(barrier, inc=1, device_id=peer, device_id_type=MESH)
    pl.semaphore_wait(barrier, len(plane) + len(blocks))
    rows_here = u.shape[0] // heads
    du_copies = []
    for d, peer in enumerate(peers):
        to = block_of(lax.rem(head + d + 1, heads), rows_here)
        du_out[d] = dot(g_in[to, :], w_in[...], NT).astype(BF)
        du_copies.append(push(du_out.at[d], du_got.at[d], ds.at[d], dr.at[d], peer))
    tiles = body_send.shape[0] // 256
    body_copies = []
    for i in range(tiles):
        at = pl.ds(i * 256, 256)
        body_send[at, :] = body_tile(normed, g_in, yn, go, 1 - layer, i).astype(BF)
        body_copies.append(push(body_send.at[at], core.at[at], cs.at[i], cr.at[i], other))
    for i in range(tiles):
        own[i * 256 : (i + 1) * 256, :] = body_tile(normed, g_in, yn, go, layer, i).astype(BF)
    here = block_of(head, rows_here)
    dn = dot(g_in[here, :], w_in[...], NT)
    for d in range(heads - 1):
        du_copies[d].wait()
        dn = dn + du_got[d].astype(F32)
    du, grad = input_gradient(dn, u[here, :], gain[...], above[...])
    du_rows[...] = du.astype(BF)
    inputs.start()
    few_mine[...] = few0[...]
    wide = few0.shape[1]
    for i in range(2):
        few_mine[8 + i : 9 + i, :] = grad[:, i * wide : (i + 1) * wide]
    for i in range(tiles):
        at = slice(i * 256, (i + 1) * 256)
        body_copies[i].wait()
        own[at, :] = (own[at, :].astype(F32) + core[at, :].astype(F32)).astype(BF)

    def fetch_tail(ours, others):
        return (
            pltpu.make_async_copy(ours, shared, xs.at[0]),
            pltpu.make_async_remote_copy(
                src_ref=others, dst_ref=shared_core, send_sem=xs.at[1], recv_sem=xs.at[2],
                device_id=other, device_id_type=MESH,
            ),
        )

    def start_all(copies):
        for copy in copies:
            copy.start()

    pl.when(layer == 0)(lambda: start_all(fetch_tail(tail0, tail1)))
    pl.when(layer == 1)(lambda: start_all(fetch_tail(tail1, tail0)))

    def few_to_core(src):
        return pltpu.make_async_remote_copy(
            src_ref=src, dst_ref=few_core, send_sem=xs.at[3], recv_sem=xs.at[4],
            device_id=other, device_id_type=MESH,
        )

    few_to_seq = lambda d: pltpu.make_async_remote_copy(
        src_ref=few_seq.at[me], dst_ref=few_seq.at[me], send_sem=fs.at[d], recv_sem=fr.at[d],
        device_id=blocks[d], device_id_type=MESH,
    )
    few_to_head = lambda d: pltpu.make_async_remote_copy(
        src_ref=few_head.at[head], dst_ref=few_head.at[head], send_sem=gs.at[d], recv_sem=gr.at[d],
        device_id=peers[d], device_id_type=MESH,
    )
    give_all = pltpu.make_async_remote_copy(
        src_ref=done, dst_ref=traded, send_sem=xs.at[5], recv_sem=xs.at[6],
        device_id=other, device_id_type=MESH,
    )
    pl.when(layer == 0)(lambda: few_to_core(few1).start())
    pl.when(layer == 1)(lambda: few_to_core(few_mine).start())
    pl.when(layer == 0)(give_all.start)

    shift = parts * 3 // 5

    def order(side, p):
        return lax.rem(p + (shift if side else 0), parts)

    def place(side, p):
        return pl.ds(pl.multiple_of(side * half + order(side, p) * PIECE, PIECE), PIECE)

    def unless_tail(side, p, act):
        if side:
            pl.when(order(side, p) < parts - TAIL)(act)
        else:
            act()

    for copy in fetch_tail(tail0, tail1):
        copy.wait()
    shared[...] = (shared[...].astype(F32) + shared_core[...].astype(F32)).astype(BF)
    block = lambda i: pl.ds(pl.multiple_of(OWN + i * SHARED, 32), SHARED)
    scatter = lambda d: pltpu.make_async_remote_copy(
        src_ref=shared.at[block(lax.rem(head + d + 1, heads))], dst_ref=shared_got.at[d],
        send_sem=hs.at[0, d], recv_sem=hr.at[0, d], device_id=peers[d], device_id_type=MESH,
    )
    gather = lambda d: pltpu.make_async_remote_copy(
        src_ref=shared_o.at[head], dst_ref=shared_o.at[head],
        send_sem=hs.at[1, d], recv_sem=hr.at[1, d], device_id=peers[d], device_id_type=MESH,
    )
    for d in range(heads - 1):
        scatter(d).start()

    def sending(side, p, back, source):
        at = place(side, p)
        towards = down if (side == 0) != back else up
        target, send, recv = (out, bs, br) if back else (got, rs, rr)
        return pltpu.make_async_remote_copy(
            src_ref=source.at[at], dst_ref=target.at[at], send_sem=send.at[side, p],
            recv_sem=recv.at[side, p], device_id=towards, device_id_type=MESH,
        )

    def give(side, p):
        at = place(side, p)
        return pltpu.make_async_remote_copy(
            src_ref=out.at[at], dst_ref=traded.at[at], send_sem=ts.at[side, p], recv_sem=tr.at[side, p],
            device_id=other, device_id_type=MESH,
        )

    def start_give(side, p):
        unless_tail(side, p, lambda: pl.when(layer == 1)(give(side, p).start))

    def reduce(side, p):
        start, end = (high_end, low_end) if side == 0 else (low_end, high_end)
        at = place(side, p)

        @pl.when(start)
        def _():
            sending(side, p, False, own).start()

        @pl.when(jnp.logical_not(start))
        def _():
            sending(side, p, False, got).wait_recv()
            summed = (own[at, :].astype(F32) + got[at, :].astype(F32)).astype(BF)

            @pl.when(end)
            def _():
                out[at, :] = summed
                sending(side, p, True, out).start()
                start_give(side, p)

            @pl.when(jnp.logical_not(end))
            def _():
                got[at, :] = summed
                sending(side, p, False, got).start()

    def back(side, p):
        start, end = (high_end, low_end) if side == 0 else (low_end, high_end)

        @pl.when(jnp.logical_not(end))
        def _():
            sending(side, p, True, out).wait_recv()

            @pl.when(jnp.logical_not(start))
            def _():
                sending(side, p, True, out).start()

            start_give(side, p)

    def guarded(act, side, p):
        @pl.when(jnp.logical_and(p >= 0, p < parts))
        def _():
            act(side, p)

    far = size - 1
    ready = parts - shift - TAIL - 1
    finished = parts - shift + skew * (2 * far - me)

    def step(t, _):
        @pl.when(t == 2)
        def _():
            few_to_core(few_mine).wait()
            pl.when(layer == 0)(lambda: few_seq.__setitem__(me, few_mine[...] + few_core[...]))
            pl.when(layer == 1)(lambda: few_seq.__setitem__(me, few1[...] + few_core[...]))
            for d in range(size - 1):
                few_to_seq(d).start()

        @pl.when(t == 8)
        def _():
            for d in range(size - 1):
                few_to_seq(d).wait()
            total = few_seq[0]
            for i in range(1, size):
                total = total + few_seq[i]
            few_o[0 : FEW // 2, :] = total[0 : FEW // 2]
            few_head[head] = total[FEW // 2 :]
            for d in range(heads - 1):
                few_to_head(d).start()

        @pl.when(t == 14)
        def _():
            for d in range(heads - 1):
                few_to_head(d).wait()
            total = few_head[0]
            for i in range(1, heads):
                total = total + few_head[i]
            few_o[FEW // 2 :, :] = total

        @pl.when(t == ready)
        def _():
            total = shared[block(head), :].astype(F32)
            for d in range(heads - 1):
                scatter(d).wait()
                total = total + shared_got[d].astype(F32)
            own[plain : plain + SHARED, :] = total.astype(BF)
            own[plain - OWN : plain, :] = shared[0:OWN, :]

        guarded(reduce, 0, t - skew * (far - me))
        guarded(reduce, 1, t - skew * me)
        guarded(back, 0, t - skew * (far + me))
        guarded(back, 1, t - skew * (2 * far - me))

        @pl.when(t == finished)
        def _():
            shared_o[head] = out[plain:rows, :]
            for d in range(heads - 1):
                gather(d).start()

        return 0

    lax.fori_loop(0, parts + 2 * skew * far, step, 0)

    def drain(p, _):
        for side in range(2):
            start, end = (high_end, low_end) if side == 0 else (low_end, high_end)

            @pl.when(jnp.logical_not(end))
            def _():
                sending(side, p, False, got).wait_send()

            @pl.when(jnp.logical_not(start))
            def _():
                sending(side, p, True, out).wait_send()

        return 0

    lax.fori_loop(0, parts, drain, 0)
    for d in range(heads - 1):
        gather(d).wait()

    def drain_trade(p, _):
        for side in range(2):
            unless_tail(side, p, lambda: pl.when(layer == 0)(give(side, p).wait_recv))
            unless_tail(side, p, lambda: pl.when(layer == 1)(give(side, p).wait_send))
        return 0

    lax.fori_loop(0, parts, drain_trade, 0)
    pl.when(layer == 0)(give_all.wait_send)
    pl.when(layer == 1)(give_all.wait_recv)
    inputs.finish()


def grad_sum(layer0, tails, fews, done, size, heads, skew=2):
    width = done.shape[1]
    rows = done.shape[0] + OWN + SHARED
    parts = rows // 2 // PIECE
    n, d_model = layer0[3].shape
    vm = pl.BlockSpec(memory_space=pltpu.VMEM)
    anywhere = pl.BlockSpec(memory_space=pl.ANY)
    pair = pltpu.SemaphoreType.DMA((2, parts))
    sems = lambda *k: pltpu.SemaphoreType.DMA(k)
    tiles = done.shape[0] // 256
    return pl.pallas_call(
        functools.partial(grad_sum_kernel, size, heads, skew),
        out_shape=(
            shape((rows, width), BF),
            shape((heads, SHARED, width), BF),
            shape((FEW, width), F32),
            shape(done.shape, BF),
            shape((2 * n, d_model), BF),
        ),
        in_specs=[vm] * 8 + [anywhere] * 2 + [vm] * 2 + [anywhere],
        out_specs=(vm, vm, vm, anywhere, anywhere),
        scratch_shapes=[pltpu.VMEM((rows, width), BF) for _ in range(3)]
        + [pltpu.VMEM((OWN + heads * SHARED, width), BF) for _ in range(2)]
        + [pltpu.VMEM((heads - 1, SHARED, width), BF)]
        + [pltpu.VMEM((FEW, width), F32), pltpu.VMEM((size, FEW, width), F32)]
        + [pltpu.VMEM((heads, FEW // 2, width), F32)]
        + [pltpu.VMEM(done.shape, BF)]
        + [pltpu.VMEM((heads - 1, n // heads, d_model), BF) for _ in range(2)]
        + [pltpu.VMEM((n // heads, d_model), BF), pltpu.VMEM((FEW, width), F32)]
        + [sems(tiles)] * 2
        + [pair] * 6
        + [sems(2, heads - 1)] * 2
        + [sems(7)]
        + [sems(size - 1)] * 2
        + [sems(heads - 1)] * 4
        + collect_sems(heads),
        compiler_params=pltpu.CompilerParams(
            collective_id=8, has_side_effects=True, vmem_limit_bytes=VMEM_LIMIT
        ),
        name="grad_sum",
    )(*layer0, *tails, *fews, done)


def unpack_kernel(dims, mine, traded, done, mine_low, traded_low, done_low, own, shared, few,
                  z_o, x_o, out_o, bc_o, dt_o, conv_o, conv_bias_o, bc_conv_o, bc_bias_o,
                  dt_bias_o, a_log_o, skip_o, gate_o, gain_o):
    heads, inner, states = dims
    layer = lax.axis_index("section")
    half = own.shape[1]

    @pl.when(layer == 0)
    def _():
        z_o[...] = mine[...].astype(F32)
        x_o[...] = traded[...].astype(F32)
        out_o[:, :half] = mine_low[...].astype(F32)
        out_o[:, half:] = traded_low[...].astype(F32)

    @pl.when(layer == 1)
    def _():
        z_o[...] = traded[...].astype(F32)
        x_o[...] = done[...].astype(F32)
        out_o[:, :half] = traded_low[...].astype(F32)
        out_o[:, half:] = done_low[...].astype(F32)

    @pl.when(pl.program_id(0) == 0)
    def _():
        blocks = jnp.concatenate([shared[i] for i in range(shared.shape[0])], axis=0)
        step = blocks.shape[0] // 2
        for i in range(2):
            rows = slice(i * half, (i + 1) * half)
            bc_o[rows, :] = jnp.transpose(blocks[i * step : i * step + 2 * states].astype(F32))
            dts = own[i * OWN // 2 : (i + 1) * OWN // 2, :].astype(F32)
            dts = jnp.concatenate([dts, jnp.zeros((LANES - OWN // 2, half), F32)], axis=0)
            dt_o[rows, :] = jnp.transpose(dts)[:, :heads]
            gain_o[:, rows] = few[8 + i : 9 + i, :]
        conv_o[...] = few[0:4, :]
        conv_bias_o[...] = few[4:5, :]
        gate_o[...] = few[5:6, :]
        bc_conv_o[...] = few[10:14, 0 : 2 * states]
        bc_bias_o[...] = few[14:15, 0 : 2 * states]
        dt_bias_o[...] = few[6:7, 0:heads]
        a_log_o[...] = few[6:7, LANES : LANES + heads]
        skip_o[...] = few[6:7, 2 * LANES : 2 * LANES + heads]


def unpack(grads, traded, done, shared, few, dims, steps=6):
    heads, inner, states = dims
    half = grads.shape[1]
    width = 2 * half
    tall, low = width // steps, inner // steps
    upper = pl.BlockSpec((tall, half), lambda i: (i, 0))
    lower = pl.BlockSpec((low, half), lambda i: (width // low + i, 0))
    whole = lambda a: pl.BlockSpec(a.shape, lambda i: (0,) * len(a.shape))
    outs = [
        ((width, inner), (tall, inner)),
        ((width, inner), (tall, inner)),
        ((inner, width), (low, width)),
    ]
    fixed = [
        (width, 2 * states), (width, heads), (4, inner), (1, inner), (4, 2 * states), (1, 2 * states),
        (1, heads), (1, heads), (1, heads), (1, inner), (1, width),
    ]
    return pl.pallas_call(
        functools.partial(unpack_kernel, dims),
        grid=(steps,),
        out_shape=[shape(a, F32) for a, _ in outs] + [shape(a, F32) for a in fixed],
        in_specs=[upper] * 3
        + [lower] * 3
        + [pl.BlockSpec((OWN, half), lambda i: ((width + inner) // OWN, 0)), whole(shared), whole(few)],
        out_specs=[pl.BlockSpec(b, lambda i: (i, 0)) for _, b in outs]
        + [pl.BlockSpec(a, lambda i: (0, 0)) for a in fixed],
        compiler_params=pltpu.CompilerParams(vmem_limit_bytes=VMEM_LIMIT),
        name="unpack",
    )(grads, traded, done, grads, traded, done, grads, shared, few)


def normalise(u, gain):
    uv = u.astype(F32)
    s = lax.rsqrt(jnp.mean(uv * uv, axis=-1, keepdims=True) + EPSILON)
    return (uv * s * gain).astype(BF)


def on_device(
    inputs, cotangent, norm_gain, w_z, w_x, w_bc, w_dt, conv_x, conv_x_bias, conv_bc, conv_bc_bias,
    dt_bias, a_log, d_skip, gate_gain, w_out,
):
    me = lax.axis_index("section")
    seq_size, head_size = lax.axis_size("seq"), lax.axis_size("head")
    micro, n, d_model = inputs.shape
    batch = micro // 2
    tokens = batch * n
    inner, heads, states = w_z.shape[2], w_dt.shape[2], w_bc.shape[2] // 2
    wide = inner + 2 * states
    full = inner * head_size
    dims = (heads, inner, states)
    pad_heads = lambda a: jnp.pad(a, ((0, 0),) * (a.ndim - 1) + ((0, LANES - heads),))

    taps_x = jnp.concatenate([conv_x[0], conv_x_bias, jnp.zeros((3, inner), F32)], axis=0)
    taps_bc = jnp.concatenate([conv_bc[0], conv_bc_bias, jnp.zeros((3, 2 * states), F32)], axis=0)
    taps = jnp.concatenate([taps_x, taps_bc], axis=1)
    scalars = pad_heads(jnp.concatenate([dt_bias, -jnp.exp(a_log)], axis=0)).reshape(1, -1)
    vectors = jnp.concatenate(
        [
            jnp.repeat(d_skip[0], inner // heads)[None],
            gate_gain,
            jnp.pad(scalars, ((0, 0), (0, inner - 2 * LANES))),
            jnp.zeros((5, inner), F32),
        ],
        axis=0,
    )
    gains = jnp.broadcast_to(norm_gain, (8, d_model))
    w_in2, w_out2, vectors2 = both_layers(
        [[w_z[0], w_x[0], w_bc[0], pad_heads(w_dt[0])], [w_out[0]], [taps, vectors, gains]]
    )
    gains2 = vectors2[:, :, wide + inner :]
    taps2, vectors2 = vectors2[:, :, :wide], vectors2[:, :, wide : wide + inner]

    u = lax.dynamic_slice_in_dim(inputs, me * batch, batch, 0).reshape(tokens, d_model)
    cot = lax.dynamic_slice_in_dim(cotangent, me * batch, batch, 0).reshape(tokens, d_model)

    consts = []
    for l in range(2):
        gain = gains2[l, 0:1]
        kernel, bias = taps2[l, 0:4], taps2[l, 4:5]
        skip, gate = vectors2[l, 0:1], vectors2[l, 1:2]
        dt_b, a_neg = vectors2[l, 2:3, :LANES], vectors2[l, 2:3, LANES : 2 * LANES]
        consts.append((gain, kernel, bias, dt_b, a_neg, skip, gate))
    flat = lambda a: a.reshape(tokens, -1)
    stacked = lambda a: a.reshape(batch, n, -1)

    normed0 = normalise(u, consts[0][0])
    proj0 = stacked(dot(normed0, w_in2[0]))
    cx0, dt0, cum0, state0, halo0, y0, yn0, stats0 = ssd_fwd(
        proj0, *consts[0][1:], None, dims, seq_size, head_size, full
    )
    h0, normed1, proj1 = head_fwd(flat(yn0), w_out2[0], u, head_size, [w_in2[1], consts[1][0]])
    proj1 = stacked(proj1)
    dyn1 = stacked(dot(cot, w_out2[1], NT))
    cx1, dt1, cum1, state1, halo1, y1, yn1, stats1 = ssd_fwd(
        proj1, *consts[1][1:], dyn1, dims, seq_size, head_size, full
    )
    (h1_rows,) = head_fwd(flat(yn1), w_out2[1], h0, head_size, [])

    g_in1, gate1, conv1, small1, layer_outputs = ssd_bwd(
        dyn1, y1, proj1, halo1, cx1, dt1, cum1, state1, stats1, *consts[1][1:], [h1_rows, h0],
        dims, seq_size, head_size, full,
    )
    g_in1 = flat(g_in1)
    du1, du1_rows, gain1, dyn0, body1 = head_bwd(
        g_in1, w_in2[1], cot, h0, consts[1][0], w_out2[0], normed1, flat(yn1), head_size
    )
    done = lax.psum(body1, "seq")
    tail1, few1 = grad_tail(normed1, g_in1, conv1, small1, gate1, gain1, dims, head_size)
    g_in0, gate0, conv0, small0 = ssd_bwd(
        stacked(dyn0), y0, proj0, halo0, cx0, dt0, cum0, state0, stats0, *consts[0][1:], [],
        dims, seq_size, head_size, full,
    )
    g_in0 = flat(g_in0)
    tail0, few0 = grad_tail(normed0, g_in0, conv0, small0, gate0, jnp.zeros_like(gain1), dims, head_size)
    grads, shared, few, traded, input_grads = grad_sum(
        (g_in0, w_in2[0], du1_rows, u, consts[0][0], normed0, flat(yn0), du1),
        (tail0, tail1), (few0, few1), done, seq_size, head_size,
    )
    g_z, g_x, g_out, g_bc, g_dt, g_conv, g_conv_bias, g_bc_conv, g_bc_bias, *scalars, g_gate, g_gain = unpack(
        grads, traded, done, shared, few, dims
    )

    return (
        layer_outputs.reshape(1, micro, n, d_model),
        input_grads.reshape(1, micro, n, d_model),
        g_gain,
        g_z[None],
        g_x[None],
        g_bc[None],
        g_dt[None],
        g_conv[None],
        g_conv_bias,
        g_bc_conv[None],
        g_bc_bias,
        *scalars,
        g_gate,
        g_out[None],
    )


def solution(mesh):
    in_specs = (
        P(None, "seq", None),
        P(None, "seq", None),
        P("section", None),
        P("section", None, "head"),
        P("section", None, "head"),
        P("section", None, None),
        P("section", None, "head"),
        P("section", None, "head"),
        P("section", "head"),
        P("section", None, None),
        P("section", None),
        P("section", "head"),
        P("section", "head"),
        P("section", "head"),
        P("section", "head"),
        P("section", "head", None),
    )
    out_specs = (
        P("section", None, "seq", None),
        P("section", None, "seq", None),
        P("section", None),
        P("section", None, "head"),
        P("section", None, "head"),
        P("section", None, None),
        P("section", None, "head"),
        P("section", None, "head"),
        P("section", "head"),
        P("section", None, None),
        P("section", None),
        P("section", "head"),
        P("section", "head"),
        P("section", "head"),
        P("section", "head"),
        P("section", "head", None),
    )
    return jax.shard_map(
        on_device, mesh=mesh, in_specs=in_specs, out_specs=out_specs, check_vma=False
    )
```

time: 720 us -> 649 us (0.901)
  waiting for transfers between devices: 2.35 us -> 70.9 us
  Pallas kernels: 568 us -> 506 us
  matrix products: 42.9 us -> 7.95 us
  other arithmetic: 36.7 us -> 8.3 us
  starting transfers between devices: 14.6 us -> 0.04 us
  between operations: 1.28 us -> 14.7 us
  blocking collectives: 12.3 us -> 0 us
    psum x0 -> x1, waiting for transfers between devices: none -> 70.9 us  [on_device(): done = lax.psum(body1, 'seq')]
    pallas_call x1, Pallas kernels: 190 us -> 150 us  [grad_sum(): pl.pallas_call(functools.partial(grad_sum_kernel, size, heads, skew), out...]
    dot_general x8 -> x2, matrix products: 42.9 us -> 7.95 us  [dot(): lax.dot_general(a, b, (dims, ((), ())), precision=precision, preferred_el...]
    pallas_call x22 -> x10, Pallas kernels: 361 us -> 339 us  [the longest x2 121 us: ssd_bwd(): pl.pallas_call(functools.partial(ssd_bwd_kernel, dims, size, heads_axis,...]
    squeeze x0 -> x3, local copies, waits for them, and re-layouts: none -> 15.3 us  [the longest x1 11.2 us: on_device(): proj0 = stacked(dot(normed0, w_in2[0]))]
    ppermute x4 -> x0, starting transfers between devices: 14.6 us -> none  [over_seq(): return lax.ppermute(block, 'seq', route)]
    convert_element_type x5 -> x0, other arithmetic: 13 us -> none  [the longest x1 6.86 us: on_device(): grads[None, :d_model, inner:].astype(F32)]
    psum x1 -> x0, blocking collectives: 12.3 us -> none  [on_device(): across = lax.psum(jnp.sum(dyn * gate * y * z * sigmoid(z), axis=-1), 'head')]
  transfers between devices with their start and end apart: 4 -> 1, of which waited for: 1 -> 1; matrix products, arithmetic and copies ran while one was open for 2% -> 0% of each run, Pallas kernels for 2% -> 11%
where the time goes in v2:
time: 649 us; the launch traced here: 641 us
  Pallas kernels  506 us (78%)
  waiting for transfers between devices  70.9 us (11%)
  local copies, waits for them, and re-layouts  32.6 us (5%)
  between operations  14.7 us (2%)
  other arithmetic  8.3 us (1%)
  matrix products  7.95 us (1%)
    pallas_call x1, Pallas kernels, grad_sum(): pl.pallas_call(functools.partial(grad_sum_kernel, size, heads, skew), out...  150 us
    pallas_call x2, Pallas kernels, ssd_bwd(): pl.pallas_call(functools.partial(ssd_bwd_kernel, dims, size, heads_axis,...  121 us
    pallas_call x2, Pallas kernels, head_fwd(): pl.pallas_call(functools.partial(head_fwd_kernel, size, bool(onward)), ou...  88.2 us
    psum x1, waiting for transfers between devices, on_device(): done = lax.psum(body1, 'seq')  70.9 us
    pallas_call x2, Pallas kernels, ssd_fwd(): pl.pallas_call(functools.partial(ssd_fwd_kernel, dims, size, heads_axis,...  58.2 us
    pallas_call x1, Pallas kernels, head_bwd(): pl.pallas_call(functools.partial(head_bwd_kernel, size), out_shape=(shape...  53.1 us
    pallas_call x1, Pallas kernels, both_layers(): pl.pallas_call(functools.partial(both_layers_kernel, places), out_shape=t...  17 us
  transfers between devices with their start and end apart: 1, of which 1 were waited for; matrix products, arithmetic and copies ran while one was open for 0% of the time, Pallas kernels for 11%

profile of v2, /device:TPU:0, one launch (start us, length us, event | category | flops | bytes accessed | tf_op | source)
XLA Modules:
  0.0 640.5 jit_solution(6081173366891722093)
XLA Ops:
  7.2 0.0 copy-start
  7.2 0.0 all-reduce.5.cloned.1.call-start
  7.2 1.2 copy.32
  8.4 0.7 broadcast_in_dim.46
  9.2 0.1 broadcast_in_dim_reshape.3
  9.3 0.7 exponential_negate_fusion
  9.9 0.8 pad.12.refs_3_
  10.7 0.7 reduce.1
  11.5 0.7 select_maximum_fusion.1
  12.1 0.1 pad.18.clone
  12.2 1.4 fusion.12.refs_6_
  13.6 1.4 maximum_maximum_fusion.refs_5_
  15.0 0.6 broadcast_in_dim.49.refs_7_
  15.6 17.0 %both_layers.1 = (bf16[2,1536,1920]{2,1,0:T(8,128)(2,1)}, bf16[2,768,1536]{2,1,0:T(8,128)(2,1)}, f32[2,8,3328]{2,1,0:T(8,128)}) custom-call(bf16[1536,768]{1,0:T(8,128)(2,1)} %bitcast.92, bf16[1536,768]{1,0:T(8,128)(2,1)} %bitcast.93, bf16[1536,256]{1,0:T(8,128)(2,1)} %bitcast.97, bf16[1536,128]{1,0:T(8,128)(2,1)} %pad.12.refs_3_, ...), custom_call_target="tpu_custom_call" | custom-call | tf_op jit(solution)/shard_map/both_layers/pallas_call | solution.py:137
  32.6 1.4 slice_bitcast_fusion.9
  34.0 1.4 slice_bitcast_fusion.10
  35.5 1.2 slice_bitcast_fusion.14
  36.7 1.4 slice_bitcast_fusion.4
  38.1 1.4 slice_bitcast_fusion.7
  39.4 0.0 slice-start.3
  39.4 1.9 fusion.3
  41.4 0.0 copy-start.2
  41.4 0.0 slice-start.4
  41.4 0.0 slice-start
  41.4 0.0 slice-start.1
  41.4 11.2 %slice_bitcast_fusion.1 = (bf16[1536,1920]{1,0:T(8,128)(2,1)}, bf16[1536,1920]{1,0:T(8,128)(2,1)}) fusion(bf16[2,1536,1920]{2,1,0:T(8,128)(2,1)} %get-tuple-element.77), kind=kLoop, calls=%fused_computation.4 | loop fusion | bytes 23592960 | tf_op jit(solution)/shard_map/squeeze | solution.py:1339
  52.6 0.0 slice-done.3
  52.6 0.0 slice-done.4
  52.6 0.0 slice-start.2
  52.6 2.7 slice_bitcast_fusion.3
  55.3 0.0 copy-done
  55.4 0.1 constant_dynamic-slice_fusion.1
  55.5 0.0 copy-start.4
  55.5 2.6 fusion.6.refs_7_.dyn
  58.0 0.0 copy-done.4
  58.0 0.0 copy-done.2
  58.0 0.0 slice-done
  58.0 0.0 slice-done.1
  58.0 0.0 slice-done.2
  58.1 5.4 fusion.refs_0_.proj
  63.5 27.6 %ssd_fwd.2 = (f32[2,256,1024]{2,1,0:T(8,128)}, f32[2,256,128]{2,1,0:T(8,128)}, f32[2,256,128]{2,1,0:T(8,128)}, f32[2,128,768]{2,1,0:T(8,128)}, bf16[2,16,1024]{2...) custom-call(f32[2,256,1920]{2,1,0:T(8,128)} %fusion.refs_0_.proj, ...), custom_call_target="tpu_custom_call" | custom-call | tf_op jit(solution)/shard_map/ssd_fwd/pallas_call | solution.py:352
  91.1 64.3 %head_fwd.2 = (bf16[512,1536]{1,0:T(8,128)(2,1)}, bf16[512,1536]{1,0:T(8,128)(2,1)}, f32[512,1920]{1,0:T(8,128)}) custom-call(bf16[512,768]{1,0:T(8,128)(2,1)} %bitcast.88, bf16[768,1536]{1,0:T(8,128)(2,1)} %get-tuple-element.155.w_out, bf16[512,1536]{1,0:T(8,128)(2,1)} %bitcast.73, bf16[1536,1920]{1,0:T(8,128)(2,1)} %get-tuple-element.153.refs_0_.w_in, ...), custom_call_target="tpu_custom_call" | custom-call | tf_op jit(solution)/shard_map/head_fwd/pallas_call | solution.py:665
  155.4 30.6 %ssd_fwd.3 = (f32[2,256,1024]{2,1,0:T(8,128)}, f32[2,256,128]{2,1,0:T(8,128)}, f32[2,256,128]{2,1,0:T(8,128)}, f32[2,128,768]{2,1,0:T(8,128)}, bf16[2,16,1024]{2...) custom-call(f32[2,256,1920]{2,1,0:T(8,128)} %bitcast.75, ...), custom_call_target="tpu_custom_call" | custom-call | tf_op jit(solution)/shard_map/ssd_fwd/pallas_call | solution.py:352
  186.0 23.8 %head_fwd.3.refs_0_ = bf16[128,1536]{1,0:T(8,128)(2,1)} custom-call(bf16[512,768]{1,0:T(8,128)(2,1)} %bitcast.86, bf16[768,1536]{1,0:T(8,128)(2,1)} %get-tuple-element.154.w_out, bf16[512,1536]{1,0:T(8,128)(2,1)} %get-tuple-element.88.u.refs_1_), custom_call_target="tpu_custom_call" | custom-call | tf_op jit(solution)/shard_map/head_fwd/pallas_call | solution.py:665
  209.8 60.7 %ssd_bwd.2 = (bf16[2,256,1920]{2,1,0:T(8,128)(2,1)}, f32[2,8,768]{2,1,0:T(8,128)}, f32[2,8,1024]{2,1,0:T(8,128)}, f32[2,8,128]{2,1,0:T(8,128)}, bf16[1024,1536]{1,0:T(8,128)(2,1)}) custom-call(f32[2,256,768]{2,1,0:T(8,128)} %fusion.6.refs_7_.dyn, f32[2,256,768]{2,1,0:T(8,128)} %get-tuple-element.80.y, f32[2,256,1920]{2,1,0:T(8,128)} %bitcast.76, ...), custom_call_target="tpu_custom_call" | custom-call | tf_op jit(solution)/shard_map/ssd_bwd/pallas_call | solution.py:561
  270.5 53.1 %head_bwd.1 = (bf16[512,1536]{1,0:T(8,128)(2,1)}, f32[128,1536]{1,0:T(8,128)}, f32[8,1536]{1,0:T(8,128)}, f32[512,768]{1,0:T(8,128)}, bf16[2304,768]{1,0:T(8,128)(2,1)}) custom-call(bf16[512,1920]{1,0:T(8,128)(2,1)} %bitcast.81, bf16[1536,1920]{1,0:T(8,128)(2,1)} %get-tuple-element.153.refs_0_.w_in, bf16[512,1536]{1,0:T(8,128)(2,1)} %bitcast.83, ...), custom_call_target="tpu_custom_call" | custom-call | tf_op jit(solution)/shard_map/head_bwd/pallas_call | solution.py:756
  323.6 0.0 all-reduce.5.cloned.1.call-update
  323.6 3.8 grad_tail.3
  327.4 0.0 copy-start.3
  327.4 59.9 %ssd_bwd.3 = (bf16[2,256,1920]{2,1,0:T(8,128)(2,1)}, f32[2,8,768]{2,1,0:T(8,128)}, f32[2,8,1024]{2,1,0:T(8,128)}, f32[2,8,128]{2,1,0:T(8,128)}) custom-call(f32[2,256,768]{2,1,0:T(8,128)} %bitcast.96, f32[2,256,768]{2,1,0:T(8,128)} %get-tuple-element.93.y, f32[2,256,1920]{2,1,0:T(8,128)} %fusion.refs_0_.proj, bf16[2,16,1024]{2,1,0:T(8,128)(2,1)} %get-tuple-element.94.halo, ...), custom_call_target="tpu_custom_call" | custom-call | tf_op jit(solution)/shard_map/ssd_bwd/pallas_call | solution.py:561
  387.2 0.0 copy-done.3
  387.2 1.6 multiply_convert_fusion.normed
  388.8 0.6 broadcast_in_dim.50.gain
  389.4 3.8 grad_tail.2
  393.2 70.9 %all-reduce.5.cloned.1.call-done.done.done_low = bf16[2304,768]{1,0:T(8,128)(2,1)} async-done(((bf16[2304,768]{1,0:T(8,128)(2,1)}), bf16[2304,768]{1,0:T(8,128)(2,1)}) %all-reduce.5.cloned.1.call-update) | async-done | bytes 3538960 | tf_op jit(solution)/shard_map/psum | solution.py:1359
  464.1 150.1 %grad_sum.1 = (bf16[2496,768]{1,0:T(8,128)(2,1)}, bf16[4,160,768]{2,1,0:T(8,128)(2,1)}, f32[16,768]{1,0:T(8,128)}, bf16[2304,768]{1,0:T(8,128)(2,1)}, bf16[1024,1536]{1,0:T(8,128)(2,1)}) custom-call(bf16[512,1920]{1,0:T(8,128)(2,1)} %bitcast.80, bf16[1536,1920]{1,0:T(8,128)(2,1)} %get-tuple-element.152.w_in, f32[128,1536]{1,0:T(8,128)} %get-tuple-element.101.above, ...), custom_call_target="tpu_custom_call" | custom-call | tf_op jit(solution)/shard_map/grad_sum/pallas_call | solution.py:1178
  614.2 11.4 %unpack.1 = (f32[1536,768]{1,0:T(8,128)}, f32[1536,768]{1,0:T(8,128)}, f32[768,1536]{1,0:T(8,128)}, f32[1536,256]{1,0:T(8,128)}, f32[1536,12]{1,0:T(8,128)}, /*i...) custom-call(bf16[2496,768]{1,0:T(8,128)(2,1)} %get-tuple-element.116, ...), custom_call_target="tpu_custom_call" | custom-call | tf_op jit(solution)/shard_map/unpack/pallas_call | solution.py:1270
  625.6 2.0 copy.33
  627.6 0.0 copy-start.5
  627.6 0.0 copy-start.1
  627.6 3.9 copy.38
  631.5 0.0 copy-done.5
  631.6 1.7 copy.39
  633.2 0.0 copy-done.1
  (7 shorter events, 0.0 us)
Async XLA Ops:
  7.2 48.2 %copy-start = (bf16[4,256,1536]{2,1,0:T(8,128)(2,1)S(1)}, bf16[4,256,1536]{2,1,0:T(8,128)(2,1)}, u32[]{:S(2)}) copy-start(bf16[4,256,1536]{2,1,0:T(8,128)(2,1)} %param.17) | copy-start | bytes 9437188
  7.2 456.9 %all-reduce.5.cloned.1.call-start = ((), (), s32[]{:S(2)}) async-start(), calls=%async_computation | async-start | bytes 7077888 | tf_op jit(solution)/shard_map/psum | solution.py:1359
  39.4 13.2 %slice-start.3 = ((s8[4718592]{0:T(1024)(128)(4,1)}), s8[4194304]{0:T(1024)(128)(4,1)S(1)}, s32[]{:S(2)}) async-start(s8[4718592]{0:T(1024)(128)(4,1)} %bitcast.84), calls=%async_computation.4 | async-start | bytes 8388608
  41.4 16.7 %copy-start.2 = (bf16[2,256,1536]{2,1,0:T(8,128)(2,1)}, bf16[2,256,1536]{2,1,0:T(8,128)(2,1)S(1)}, u32[]{:S(2)}) copy-start(bf16[2,256,1536]{2,1,0:T(8,128)(2,1)S(1)} %get-tuple-element.151) | copy-start | bytes 4718596
  41.4 11.2 %slice-start.4 = ((s8[4718592]{0:T(1024)(128)(4,1)}), s8[524288]{0:T(1024)(128)(4,1)S(1)}, s32[]{:S(2)}) async-start(s8[4718592]{0:T(1024)(128)(4,1)} %bitcast.84), calls=%async_computation.5 | async-start | bytes 1048576
  41.4 16.6 %slice-start = ((s8[11796480]{0:T(1024)(128)(4,1)}), s8[4194304]{0:T(1024)(128)(4,1)S(1)}, s32[]{:S(2)}) async-start(s8[11796480]{0:T(1024)(128)(4,1)} %bitcast.77), calls=%async_computation.1 | async-start | bytes 8388608
  41.4 16.6 %slice-start.1 = ((s8[11796480]{0:T(1024)(128)(4,1)}), s8[4194304]{0:T(1024)(128)(4,1)S(1)}, s32[]{:S(2)}) async-start(s8[11796480]{0:T(1024)(128)(4,1)} %bitcast.77), calls=%async_computation.2 | async-start | bytes 8388608
  52.6 5.4 slice-start.2
  55.5 2.6 copy-start.4
  327.4 59.9 %copy-start.3 = (bf16[2,256,1536]{2,1,0:T(8,128)(2,1)S(1)}, bf16[2,256,1536]{2,1,0:T(8,128)(2,1)}, u32[]{:S(2)}) copy-start(bf16[2,256,1536]{2,1,0:T(8,128)(2,1)} %copy-done.2) | copy-start | bytes 4718596
  627.6 3.9 copy-start.5
  627.6 5.6 copy-start.1
Sparse Core Ops, SparseCore 0:
  323.7 140.3 all-reduce.4

commit v3 on v2

--- a/solution.py
+++ b/solution.py
@@ -104,6 +104,7 @@
 
 def both_layers_kernel(places, *refs):
     count = len(places)
+    groups = places[-1][0] + 1
     ins, outs = refs[:count], refs[count:-3]
     send, recv, local = refs[-3:]
     me = lax.axis_index("section")
@@ -111,15 +112,28 @@
     barrier = pltpu.get_barrier_semaphore()
     pl.semaphore_signal(barrier, inc=1, device_id=other, device_id_type=MESH)
     pl.semaphore_wait(barrier, 1)
-    copies = []
+
+    def copies(i, which, start, layer):
+        target = outs[layer * groups + which].at[:, pl.ds(start, ins[i].shape[1])]
+        return (
+            pltpu.make_async_remote_copy(
+                src_ref=ins[i], dst_ref=target, send_sem=send.at[i], recv_sem=recv.at[i],
+                device_id=other, device_id_type=MESH,
+            ),
+            pltpu.make_async_copy(ins[i], target, local.at[i]),
+        )
+
+    for layer in range(2):
+
+        @pl.when(me == layer)
+        def _():
+            for i, (which, start) in enumerate(places):
+                for copy in copies(i, which, start, layer):
+                    copy.start()
+
     for i, (which, start) in enumerate(places):
-        target = outs[which].at[me, :, pl.ds(start, ins[i].shape[1])]
-        copies.append(push(ins[i], target, send.at[i], recv.at[i], other))
-        own = pltpu.make_async_copy(ins[i], target, local.at[i])
-        own.start()
-        copies.append(own)
-    for copy in copies:
-        copy.wait()
+        for copy in copies(i, which, start, 0):
+            copy.wait()
 
 
 def both_layers(groups):
@@ -130,21 +144,38 @@
             places.append((i, start))
             flat.append(a)
             start += a.shape[1]
-        outs.append(shape((2, group[0].shape[0], start), group[0].dtype))
+        outs.append(shape((group[0].shape[0], start), group[0].dtype))
     count = len(flat)
     vm = pl.BlockSpec(memory_space=pltpu.VMEM)
     anywhere = pl.BlockSpec(memory_space=pl.ANY)
     return pl.pallas_call(
         functools.partial(both_layers_kernel, places),
-        out_shape=tuple(outs),
+        out_shape=tuple(outs) * 2,
         in_specs=[vm] * count,
-        out_specs=(anywhere,) * len(outs),
+        out_specs=(anywhere,) * (2 * len(outs)),
         scratch_shapes=[pltpu.SemaphoreType.DMA((count,)) for _ in range(3)],
         compiler_params=pltpu.CompilerParams(
             collective_id=0, has_side_effects=True, vmem_limit_bytes=VMEM_LIMIT
         ),
         name="both_layers",
     )(*flat)
+
+
+def constants(block, dims):
+    heads, inner, states = dims
+    wide = inner + 2 * states
+    return (
+        block.at[0:4, 0:wide],
+        block.at[4:5, 0:wide],
+        block.at[2:3, wide : wide + LANES],
+        block.at[2:3, wide + LANES : wide + 2 * LANES],
+        block.at[0:1, wide : wide + inner],
+        block.at[1:2, wide : wide + inner],
+    )
+
+
+def norm_gain_of(block, d_model):
+    return block.at[0:1, block.shape[1] - d_model :]
 
 
 class Line:
@@ -229,11 +260,12 @@
 
 
 def ssd_fwd_kernel(dims, size, heads_axis, full, has_dyn, *refs):
-    proj, taps, bias, dt_bias, a_neg, skip, gain = refs[:7]
-    dyn = refs[7] if has_dyn else None
+    proj, block = refs[:2]
+    taps, bias, dt_bias, a_neg, skip, gain = constants(block, dims)
+    dyn = refs[2] if has_dyn else None
     (cx, dt_o, cum_o, state, halo, y_o, yn_o, stats_o,
      ext, own, decay, rim, outgoing, incoming, gates, square, square_got,
-     send, recv, halo_send, halo_recv, stat_send, stat_recv) = refs[7 + has_dyn :]
+     send, recv, halo_send, halo_recv, stat_send, stat_recv) = refs[2 + has_dyn :]
     heads, inner, states = dims
     batch, n = proj.shape[0], proj.shape[1]
     wide = inner + 2 * states
@@ -296,9 +328,13 @@
             dtx, dtx_rest = halves(x * dt_wide[:, lanes])
             both = []
             for h in (2 * p, 2 * p + 1):
-                lag = jnp.where(keep, cums[:, h : h + 1] - cums_t[h : h + 1, :], -1e30)
-                high, rest = halves(scores * jnp.exp(lag))
-                both.append(dot(high, dtx) + dot(rest, dtx) + dot(high, dtx_rest))
+                sums = []
+                for low, high in ((0, n // 2), (n // 2, n)):
+                    lag = cums[low:high, h : h + 1] - cums_t[h : h + 1, 0:high]
+                    lag = jnp.where(keep[low:high, 0:high], lag, -1e30)
+                    top, rest = halves(scores[low:high, 0:high] * jnp.exp(lag))
+                    sums.append(dot(top, dtx[0:high]) + dot(rest, dtx[0:high]) + dot(top, dtx_rest[0:high]))
+                both.append(jnp.concatenate(sums, axis=0))
             y_o[m, :, lanes] = skip[:, lanes] * x + jnp.where(first, both[0], both[1])
     for m in range(batch):
         entered = incoming[m]
@@ -332,7 +368,7 @@
             line.halo(rim.at[m], halo.at[m], m, halo_send, halo_recv).wait_send()
 
 
-def ssd_fwd(proj, taps, bias, dt_bias, a_neg, skip, gain, dyn, dims, size, heads_axis, full):
+def ssd_fwd(proj, block, dyn, dims, size, heads_axis, full):
     heads, inner, states = dims
     batch, n, _ = proj.shape
     wide = inner + 2 * states
@@ -352,7 +388,7 @@
     return pl.pallas_call(
         functools.partial(ssd_fwd_kernel, dims, size, heads_axis, full, has_dyn),
         out_shape=outs,
-        in_specs=[vm] * (7 + has_dyn),
+        in_specs=[vm] * (2 + has_dyn),
         out_specs=(vm,) * len(outs),
         scratch_shapes=[
             pltpu.VMEM((n + 8, wide), F32),
@@ -375,13 +411,14 @@
             collective_id=1 + has_dyn, has_side_effects=True, vmem_limit_bytes=VMEM_LIMIT
         ),
         name="ssd_fwd",
-    )(proj, taps, bias, dt_bias, a_neg, skip, gain, *([dyn] if has_dyn else []))
+    )(proj, block, *([dyn] if has_dyn else []))
 
 
 def ssd_bwd_kernel(
     dims, size, heads_axis, full, has_across,
-    dyn, y, proj, halo, cx, dt, cum, state, stats, taps, bias, dt_bias, a_neg, skip, gain, *refs
+    dyn, y, proj, halo, cx, dt, cum, state, stats, block, *refs
 ):
+    taps, bias, dt_bias, a_neg, skip, gain = constants(block, dims)
     if has_across:
         h_rows, h_whole, h_o, *refs = refs[:2] + refs[6:7] + refs[2:6] + refs[7:]
         *refs, c_local, c_send, c_recv = refs
@@ -463,20 +500,35 @@
 
             line.relay(own, decay, m * pairs + p, batch * pairs, 2, 1)
             lanes = slice(p * LANES, (p + 1) * LANES)
-            dtx = cx[m, :, lanes] * dt_wide[:, lanes]
+            dtx, dtx_rest = halves(cx[m, :, lanes] * dt_wide[:, lanes])
             dyb, dy_rest = halves(dy[m, :, lanes])
-            both = []
+            both, gathered = [], [0.0, 0.0]
             for j, h in enumerate((2 * p, 2 * p + 1)):
-                lag = jnp.where(keep, cums_t[h : h + 1, :] - cums[:, h : h + 1], -1e30)
-                decays = jnp.exp(lag)
-                weights = scores_t * decays
-                mine, mine_rest = halves(jnp.where(first if j == 0 else jnp.logical_not(first), dtx, 0.0))
-                d_weights = dot(mine, dyb, NT) + dot(mine, dy_rest, NT) + dot(mine_rest, dyb, NT)
-                q = d_weights * weights
-                d_scores[m] += d_weights * decays
-                rowq[m, h : h + 1, :] = jnp.sum(q, axis=0, keepdims=True)
-                colq[m] += jnp.where(lane == h, jnp.sum(q, axis=1, keepdims=True), 0.0)
-                both.append(dot(weights.astype(BF), dyb))
+                side = first if j == 0 else jnp.logical_not(first)
+                mine, mine_rest = [jnp.where(side, v, jnp.zeros((), BF)) for v in (dtx, dtx_rest)]
+                sums, row_sums, column_sums = [], [], []
+                for i, (low, high) in enumerate(((0, n // 2), (n // 2, n))):
+                    lag = jnp.where(
+                        keep[low:high, low:n], cums_t[h : h + 1, low:n] - cums[low:high, h : h + 1], -1e30
+                    )
+                    decays = jnp.exp(lag)
+                    weights = scores_t[low:high, low:n] * decays
+                    d_weights = (
+                        dot(mine[low:high], dyb[low:n], NT)
+                        + dot(mine[low:high], dy_rest[low:n], NT)
+                        + dot(mine_rest[low:high], dyb[low:n], NT)
+                    )
+                    q = d_weights * weights
+                    gathered[i] = gathered[i] + d_weights * decays
+                    row_sums.append(jnp.sum(q, axis=0, keepdims=True))
+                    column_sums.append(jnp.sum(q, axis=1, keepdims=True))
+                    sums.append(dot(weights.astype(BF), dyb[low:n]))
+                rowq[m, h : h + 1, :] = row_sums[0]
+                rowq[m, h : h + 1, n // 2 :] += row_sums[1]
+                colq[m] += jnp.where(lane == h, jnp.concatenate(column_sums, axis=0), 0.0)
+                both.append(jnp.concatenate(sums, axis=0))
+            d_scores[m, 0 : n // 2, :] += gathered[0]
+            d_scores[m, n // 2 :, n // 2 :] += gathered[1]
             dxw[m, :, lanes] = jnp.where(first, both[0], both[1])
     fold = lambda v: dot_mask(v, expand, NT)
     for m in range(batch):
@@ -544,7 +596,7 @@
         outputs.finish()
 
 
-def ssd_bwd(dyn, y, proj, halo, cx, dt, cum, state, stats, taps, bias, dt_bias, a_neg, skip, gain, outputs,
+def ssd_bwd(dyn, y, proj, halo, cx, dt, cum, state, stats, block, outputs,
             dims, size, heads_axis, full):
     has_across = bool(outputs)
     heads, inner, states = dims
@@ -561,7 +613,7 @@
     return pl.pallas_call(
         functools.partial(ssd_bwd_kernel, dims, size, heads_axis, full, has_across),
         out_shape=outs,
-        in_specs=[vm] * (15 + len(outputs)),
+        in_specs=[vm] * (10 + len(outputs)),
         out_specs=(vm,) * 4 + (pl.BlockSpec(memory_space=pl.ANY),) * has_across,
         scratch_shapes=[
             pltpu.VMEM((batch, n, inner), F32),
@@ -590,7 +642,7 @@
             collective_id=10 + has_across, has_side_effects=True, vmem_limit_bytes=VMEM_LIMIT
         ),
         name="ssd_bwd",
-    )(dyn, y, proj, halo, cx, dt, cum, state, stats, taps, bias, dt_bias, a_neg, skip, gain, *outputs)
+    )(dyn, y, proj, halo, cx, dt, cum, state, stats, block, *outputs)
 
 
 def greet(size, core=False):
@@ -616,11 +668,12 @@
 
 def head_fwd_kernel(size, onward, yn, w_out, u, *refs):
     if onward:
-        w_in, gain, h_o, normed_o, proj_o, out, got, send, recv = refs
+        w_in, block, h_o, normed_o, proj_o, out, got, send, recv = refs
+        gain = norm_gain_of(block, u.shape[1])
     else:
-        h_o, out, got, send, recv = refs
+        go, h_o, body_o, out, got, body_send, body_got, send, recv, body_ss, body_rs = refs
     rows = yn.shape[0] // size
-    me, peers = greet(size)
+    me, peers = greet(size, core=not onward)
     copies = []
     for d, peer in enumerate(peers):
         to = lax.rem(me + d + 1, size)
@@ -628,6 +681,8 @@
         copies.append(push(out.at[d], got.at[d], send.at[0, d], recv.at[0, d], peer))
     mine = block_of(me, rows)
     total = dot(yn[mine, :], w_out[...])
+    if not onward:
+        body = body_halves(lambda which, i: body_tile(None, None, yn, go, which, i), body_o, body_send, body_got, body_ss, body_rs)
     for copy in copies:
         copy.wait()
     for d in range(size - 1):
@@ -635,6 +690,7 @@
     h = (u[mine, :].astype(F32) + total).astype(BF)
     if not onward:
         h_o[...] = h
+        add_halves(body, body_o, body_got)
         return
     h_o[mine, :] = h
     copies = [
@@ -654,27 +710,34 @@
         copy.wait_send()
 
 
-def head_fwd(yn, w_out, u, size, onward):
+def head_fwd(yn, w_out, u, size, onward, go=None):
     n, d_model = u.shape
+    body = (yn.shape[1], d_model // 2)
+    tiles = body[0] // 256
     rows = n // size
     vm = pl.BlockSpec(memory_space=pltpu.VMEM)
     kind = F32 if onward else BF
     outs = [shape((n if onward else rows, d_model), BF)]
     if onward:
         outs += [shape((n, d_model), BF), shape((n, onward[0].shape[1]), F32)]
+    else:
+        outs += [shape(body, BF)]
+        onward = [go]
+    more = go is not None
     return pl.pallas_call(
-        functools.partial(head_fwd_kernel, size, bool(onward)),
+        functools.partial(head_fwd_kernel, size, not more),
         out_shape=tuple(outs),
         in_specs=[vm] * (3 + len(onward)),
         out_specs=(vm,) * len(outs),
         scratch_shapes=[
             pltpu.VMEM((size - 1, rows, d_model), kind),
             pltpu.VMEM((size - 1, rows, d_model), kind),
-            pltpu.SemaphoreType.DMA((2, size - 1)),
-            pltpu.SemaphoreType.DMA((2, size - 1)),
-        ],
+        ]
+        + [pltpu.VMEM(body, BF)] * (2 * more)
+        + [pltpu.SemaphoreType.DMA((2, size - 1))] * 2
+        + [pltpu.SemaphoreType.DMA((tiles,))] * (2 * more),
         compiler_params=pltpu.CompilerParams(
-            collective_id=3 if onward else 6, has_side_effects=True, vmem_limit_bytes=VMEM_LIMIT
+            collective_id=6 if more else 3, has_side_effects=True, vmem_limit_bytes=VMEM_LIMIT
         ),
         name="head_fwd",
     )(yn, w_out, u, *onward)
@@ -693,20 +756,36 @@
 
 
 def body_tile(normed, g_in, yn, go, half, i):
-    tile, count = 256, normed.shape[1] // 256
+    left, right = (yn, go) if normed is None else (normed, g_in)
     wide = yn.shape[1]
     at = pl.ds(pl.multiple_of(half * wide, wide), wide)
-    if i < count:
-        return dot(normed[:, i * tile : (i + 1) * tile], g_in[:, at], TN)
-    return dot(yn[:, (i - count) * tile : (i - count + 1) * tile], go[:, at], TN)
-
-
-def head_bwd_kernel(size, g_in, w_in, upper, u, gain, w_out, normed, yn, du_o, mine_o, grad_o, dyn_o, body_o,
+    return dot(left[:, i * 256 : (i + 1) * 256], right[:, at], TN)
+
+
+def body_halves(make, out, sent, got, send, recv):
+    layer = lax.axis_index("section")
+    copies = []
+    for i in range(out.shape[0] // 256):
+        at = pl.ds(i * 256, 256)
+        sent[at, :] = make(1 - layer, i).astype(BF)
+        copies.append(push(sent.at[at], got.at[at], send.at[i], recv.at[i], {"section": 1 - layer}))
+    for i in range(out.shape[0] // 256):
+        out[i * 256 : (i + 1) * 256, :] = make(layer, i).astype(BF)
+    return copies
+
+
+def add_halves(copies, out, got):
+    for i, copy in enumerate(copies):
+        at = slice(i * 256, (i + 1) * 256)
+        copy.wait()
+        out[at, :] = (out[at, :].astype(F32) + got[at, :].astype(F32)).astype(BF)
+
+
+def head_bwd_kernel(size, g_in, w_in, upper, u, block, w_out, normed, yn, du_o, mine_o, grad_o, dyn_o, body_o,
                     out, got, body_send, body_got, send, recv, body_ss, body_rs):
     rows = u.shape[0] // size
+    gain = norm_gain_of(block, u.shape[1])
     me, peers = greet(size, core=True)
-    layer = lax.axis_index("section")
-    other = {"section": 1 - layer}
     copies = []
     for d, peer in enumerate(peers):
         to = lax.rem(me + d + 1, size)
@@ -714,14 +793,8 @@
         copies.append(push(out.at[d], got.at[d], send.at[0, d], recv.at[0, d], peer))
     mine = block_of(me, rows)
     dn = dot(g_in[mine, :], w_in[...], NT)
-    tiles = body_o.shape[0] // 256
-    body_copies = []
-    for i in range(tiles):
-        at = pl.ds(i * 256, 256)
-        body_send[at, :] = body_tile(normed, g_in, yn, upper, 1 - layer, i).astype(BF)
-        body_copies.append(push(body_send.at[at], body_got.at[at], body_ss.at[i], body_rs.at[i], other))
-    for i in range(tiles):
-        body_o[i * 256 : (i + 1) * 256, :] = body_tile(normed, g_in, yn, upper, layer, i).astype(BF)
+    make = lambda which, i: body_tile(normed, g_in, yn, upper, which, i)
+    body = body_halves(make, body_o, body_send, body_got, body_ss, body_rs)
     for copy in copies:
         copy.wait()
     for d in range(size - 1):
@@ -733,10 +806,7 @@
     copies = [
         push(du_o.at[mine], du_o.at[mine], send.at[1, d], recv.at[1, d], peer) for d, peer in enumerate(peers)
     ]
-    for i in range(tiles):
-        at = slice(i * 256, (i + 1) * 256)
-        body_copies[i].wait()
-        body_o[at, :] = (body_o[at, :].astype(F32) + body_got[at, :].astype(F32)).astype(BF)
+    add_halves(body, body_o, body_got)
     dyn_o[mine, :] = dot(du_o[mine, :], w_out[...], NT)
     for d, copy in enumerate(copies):
         copy.wait_recv()
@@ -750,8 +820,8 @@
     n, d_model = u.shape
     inner = yn.shape[1]
     rows = n // size
-    tiles = (d_model + inner) // 256
-    body = (d_model + inner, d_model // 2)
+    tiles = d_model // 256
+    body = (d_model, d_model // 2)
     vm = pl.BlockSpec(memory_space=pltpu.VMEM)
     return pl.pallas_call(
         functools.partial(head_bwd_kernel, size),
@@ -855,8 +925,9 @@
 
 OWN = 32
 SHARED = 160
-PIECE = 32
+PIECE = 48
 TAIL = (OWN + SHARED) // PIECE
+LATE = 6
 FEW = 16
 
 
@@ -898,16 +969,18 @@
     )(normed, g_in, conv, scalars, gate, gain)
 
 
-def grad_sum_kernel(size, heads, skew, g_in, w_in, above, u, gain, normed, yn, go, tail0, tail1, few0, few1, done,
-                    out, shared_o, few_o, traded, du_o,
-                    own, core, got, shared, shared_core, shared_got, few_core, few_seq, few_head,
-                    body_send, du_out, du_got, du_rows, few_mine,
-                    cs, cr, rs, rr, bs, br, ts, tr, hs, hr, xs, fs, fr, gs, gr, ds, dr, c_local, c_send, c_recv):
+def grad_sum_kernel(size, heads, skew, g_in, w_in, above, u, block, normed, yn, go, body1, tail0, tail1, few0, few1, done, done_out,
+                    first_o, second_o, tail_o, shared_o, few_o, du_o,
+                    own, core, got, out, shared, shared_core, shared_got, few_core, few_seq, few_head,
+                    body_send, body_own, du_out, du_got, du_rows, few_mine,
+                    cs, cr, rs, rr, bs, br, ts, tr, ls, hs, hr, xs, fs, fr, gs, gr, ds, dr, c_local, c_send, c_recv):
     me, layer, head = lax.axis_index("seq"), lax.axis_index("section"), lax.axis_index("head")
-    rows = out.shape[0]
-    plain = rows - SHARED
-    half = rows // 2
+    half = out.shape[0] // 2
     parts = half // PIECE
+    total0 = body_own.shape[0]
+    early = done.shape[0]
+    cut = (parts - LATE) * PIECE
+    far = size - 1
     up, down, other = {"seq": me + 1}, {"seq": me - 1}, {"section": 1 - layer}
     peers = [{"head": lax.rem(head + d, heads)} for d in range(1, heads)]
     blocks = [{"seq": lax.rem(me + d, size)} for d in range(1, size)]
@@ -918,36 +991,34 @@
     for peer in plane + blocks:
         pl.semaphore_signal(barrier, inc=1, device_id=peer, device_id_type=MESH)
     pl.semaphore_wait(barrier, len(plane) + len(blocks))
-    rows_here = u.shape[0] // heads
-    du_copies = []
-    for d, peer in enumerate(peers):
-        to = block_of(lax.rem(head + d + 1, heads), rows_here)
-        du_out[d] = dot(g_in[to, :], w_in[...], NT).astype(BF)
-        du_copies.append(push(du_out.at[d], du_got.at[d], ds.at[d], dr.at[d], peer))
-    tiles = body_send.shape[0] // 256
-    body_copies = []
-    for i in range(tiles):
-        at = pl.ds(i * 256, 256)
-        body_send[at, :] = body_tile(normed, g_in, yn, go, 1 - layer, i).astype(BF)
-        body_copies.append(push(body_send.at[at], core.at[at], cs.at[i], cr.at[i], other))
-    for i in range(tiles):
-        own[i * 256 : (i + 1) * 256, :] = body_tile(normed, g_in, yn, go, layer, i).astype(BF)
-    here = block_of(head, rows_here)
-    dn = dot(g_in[here, :], w_in[...], NT)
-    for d in range(heads - 1):
-        du_copies[d].wait()
-        dn = dn + du_got[d].astype(F32)
-    du, grad = input_gradient(dn, u[here, :], gain[...], above[...])
-    du_rows[...] = du.astype(BF)
-    inputs.start()
-    few_mine[...] = few0[...]
-    wide = few0.shape[1]
-    for i in range(2):
-        few_mine[8 + i : 9 + i, :] = grad[:, i * wide : (i + 1) * wide]
-    for i in range(tiles):
-        at = slice(i * 256, (i + 1) * 256)
-        body_copies[i].wait()
-        own[at, :] = (own[at, :].astype(F32) + core[at, :].astype(F32)).astype(BF)
+
+    late = [
+        pltpu.make_async_copy(
+            body1.at[pl.ds(early + side * LATE * PIECE, LATE * PIECE)],
+            own.at[pl.ds(side * half, LATE * PIECE)],
+            xs.at[7 + side],
+        )
+        for side in range(2)
+    ]
+    for copy in late:
+        copy.start()
+
+    ready = [(done, pl.ds(0, early)), (done_out, pl.ds(normed.shape[1], done_out.shape[0]))]
+    given = [
+        pltpu.make_async_remote_copy(
+            src_ref=src, dst_ref=first_o.at[at], send_sem=xs.at[9 + i], recv_sem=xs.at[5 + i],
+            device_id=other, device_id_type=MESH,
+        )
+        for i, (src, at) in enumerate(ready)
+    ]
+    kept = [pltpu.make_async_copy(src, second_o.at[at], xs.at[9 + i]) for i, (src, at) in enumerate(ready)]
+
+    def all_of(copies, act):
+        for copy in copies:
+            act(copy)
+
+    pl.when(layer == 0)(lambda: all_of(given, lambda copy: copy.start()))
+    pl.when(layer == 1)(lambda: all_of(kept, lambda copy: copy.start()))
 
     def fetch_tail(ours, others):
         return (
@@ -965,6 +1036,12 @@
     pl.when(layer == 0)(lambda: start_all(fetch_tail(tail0, tail1)))
     pl.when(layer == 1)(lambda: start_all(fetch_tail(tail1, tail0)))
 
+    rows_here = u.shape[0] // heads
+    du_copy = lambda d: pltpu.make_async_remote_copy(
+        src_ref=du_out.at[d], dst_ref=du_got.at[d], send_sem=ds.at[d], recv_sem=dr.at[d],
+        device_id=peers[d], device_id_type=MESH,
+    )
+
     def few_to_core(src):
         return pltpu.make_async_remote_copy(
             src_ref=src, dst_ref=few_core, send_sem=xs.at[3], recv_sem=xs.at[4],
@@ -979,42 +1056,50 @@
         src_ref=few_head.at[head], dst_ref=few_head.at[head], send_sem=gs.at[d], recv_sem=gr.at[d],
         device_id=peers[d], device_id_type=MESH,
     )
-    give_all = pltpu.make_async_remote_copy(
-        src_ref=done, dst_ref=traded, send_sem=xs.at[5], recv_sem=xs.at[6],
-        device_id=other, device_id_type=MESH,
-    )
-    pl.when(layer == 0)(lambda: few_to_core(few1).start())
-    pl.when(layer == 1)(lambda: few_to_core(few_mine).start())
-    pl.when(layer == 0)(give_all.start)
-
-    shift = parts * 3 // 5
-
-    def order(side, p):
-        return lax.rem(p + (shift if side else 0), parts)
-
-    def place(side, p):
-        return pl.ds(pl.multiple_of(side * half + order(side, p) * PIECE, PIECE), PIECE)
-
-    def unless_tail(side, p, act):
-        if side:
-            pl.when(order(side, p) < parts - TAIL)(act)
-        else:
-            act()
+    shared_block = lambda i: pl.ds(pl.multiple_of(OWN + i * SHARED, 32), SHARED)
+    scatter = lambda d: pltpu.make_async_remote_copy(
+        src_ref=shared.at[shared_block(lax.rem(head + d + 1, heads))], dst_ref=shared_got.at[d],
+        send_sem=hs.at[0, d], recv_sem=hr.at[0, d], device_id=peers[d], device_id_type=MESH,
+    )
+    gather = lambda d: pltpu.make_async_remote_copy(
+        src_ref=shared_o.at[head], dst_ref=shared_o.at[head],
+        send_sem=hs.at[1, d], recv_sem=hr.at[1, d], device_id=peers[d], device_id_type=MESH,
+    )
 
     for copy in fetch_tail(tail0, tail1):
         copy.wait()
     shared[...] = (shared[...].astype(F32) + shared_core[...].astype(F32)).astype(BF)
-    block = lambda i: pl.ds(pl.multiple_of(OWN + i * SHARED, 32), SHARED)
-    scatter = lambda d: pltpu.make_async_remote_copy(
-        src_ref=shared.at[block(lax.rem(head + d + 1, heads))], dst_ref=shared_got.at[d],
-        send_sem=hs.at[0, d], recv_sem=hr.at[0, d], device_id=peers[d], device_id_type=MESH,
-    )
-    gather = lambda d: pltpu.make_async_remote_copy(
-        src_ref=shared_o.at[head], dst_ref=shared_o.at[head],
-        send_sem=hs.at[1, d], recv_sem=hr.at[1, d], device_id=peers[d], device_id_type=MESH,
-    )
     for d in range(heads - 1):
         scatter(d).start()
+    for d in range(heads - 1):
+        to = block_of(lax.rem(head + d + 1, heads), rows_here)
+        du_out[d] = dot(g_in[to, :], w_in[...], NT).astype(BF)
+        du_copy(d).start()
+
+    tile = 256
+    in_tiles = normed.shape[1] // tile
+    tiles = total0 // tile
+
+    def body_copy(i):
+        at = block_of(i, tile)
+        return pltpu.make_async_remote_copy(
+            src_ref=body_send.at[at], dst_ref=core.at[at], send_sem=cs.at[i], recv_sem=cr.at[i],
+            device_id=other, device_id_type=MESH,
+        )
+
+    def make_tile(i, left, right):
+        at = block_of(i, tile)
+        wide = yn.shape[1]
+        for which, target in ((1 - layer, body_send), (layer, body_own)):
+            columns = pl.ds(pl.multiple_of(which * wide, wide), wide)
+            target[at, :] = dot(left, right[:, columns], TN).astype(BF)
+        body_copy(i).start()
+
+    place = lambda side, p: pl.ds(pl.multiple_of(side * half + p * PIECE, PIECE), PIECE)
+    is_late = lambda p: p < LATE
+    is_tail = lambda side, p: jnp.logical_and(side == 1, jnp.logical_and(p >= LATE, p < LATE + TAIL))
+    start0 = lambda side, p: (p - LATE) * PIECE + (cut - TAIL * PIECE) * side
+    start1 = lambda side, p: early + side * LATE * PIECE + p * PIECE
 
     def sending(side, p, back, source):
         at = place(side, p)
@@ -1025,19 +1110,35 @@
             recv_sem=recv.at[side, p], device_id=towards, device_id_type=MESH,
         )
 
-    def give(side, p):
-        at = place(side, p)
+    def give(side, p, target, at):
         return pltpu.make_async_remote_copy(
-            src_ref=out.at[at], dst_ref=traded.at[at], send_sem=ts.at[side, p], recv_sem=tr.at[side, p],
-            device_id=other, device_id_type=MESH,
+            src_ref=out.at[place(side, p)], dst_ref=target.at[at], send_sem=ts.at[side, p],
+            recv_sem=tr.at[side, p], device_id=other, device_id_type=MESH,
         )
 
-    def start_give(side, p):
-        unless_tail(side, p, lambda: pl.when(layer == 1)(give(side, p).start))
+    def keep(side, p, target, at):
+        return pltpu.make_async_copy(out.at[place(side, p)], target.at[at], ls.at[side, p])
+
+    def final(side, p, act_keep, act_give):
+        at0 = lambda: pl.ds(pl.multiple_of(start0(side, p), PIECE), PIECE)
+        at1 = lambda: pl.ds(pl.multiple_of(start1(side, p), PIECE), PIECE)
+        late_piece = is_late(p)
+        body0 = jnp.logical_not(jnp.logical_or(late_piece, is_tail(side, p)))
+        pl.when(jnp.logical_and(body0, layer == 0))(lambda: act_keep(keep(side, p, first_o, at0())))
+        pl.when(jnp.logical_and(body0, layer == 1))(lambda: act_give(give(side, p, second_o, at0())))
+        pl.when(jnp.logical_and(late_piece, layer == 0))(lambda: act_give(give(side, p, first_o, at1())))
+        pl.when(jnp.logical_and(late_piece, layer == 1))(lambda: act_keep(keep(side, p, second_o, at1())))
+
+    begin = lambda copy: copy.start()
 
     def reduce(side, p):
         start, end = (high_end, low_end) if side == 0 else (low_end, high_end)
         at = place(side, p)
+
+        @pl.when(jnp.logical_not(jnp.logical_or(is_late(p), is_tail(side, p))))
+        def _():
+            mine = pl.ds(pl.multiple_of(start0(side, p), PIECE), PIECE)
+            own[at, :] = (body_own[mine, :].astype(F32) + core[mine, :].astype(F32)).astype(BF)
 
         @pl.when(start)
         def _():
@@ -1052,7 +1153,7 @@
             def _():
                 out[at, :] = summed
                 sending(side, p, True, out).start()
-                start_give(side, p)
+                final(side, p, begin, begin)
 
             @pl.when(jnp.logical_not(end))
             def _():
@@ -1070,19 +1171,53 @@
             def _():
                 sending(side, p, True, out).start()
 
-            start_give(side, p)
+            final(side, p, begin, begin)
 
     def guarded(act, side, p):
         @pl.when(jnp.logical_and(p >= 0, p < parts))
         def _():
             act(side, p)
 
-    far = size - 1
-    ready = parts - shift - TAIL - 1
-    finished = parts - shift + skew * (2 * far - me)
+    tail_at = half + LATE * PIECE
+    finished = LATE + TAIL + skew * (2 * far - me)
+    for copy in late:
+        copy.wait()
 
     def step(t, _):
-        @pl.when(t == 2)
+        def one_tile(k, _):
+            i = 2 * t + k
+
+            @pl.when(i < in_tiles)
+            def _():
+                make_tile(i, normed[:, block_of(i, tile)], g_in)
+
+            @pl.when(jnp.logical_and(i >= in_tiles, i < tiles))
+            def _():
+                make_tile(i, yn[:, block_of(i - in_tiles, tile)], go)
+
+            pl.when(jnp.logical_and(i >= 2, i < tiles + 2))(lambda: body_copy(i - 2).wait())
+            return 0
+
+        lax.fori_loop(0, 2, one_tile, 0)
+
+        @pl.when(t == 5)
+        def _():
+            here = block_of(head, rows_here)
+            dn = dot(g_in[here, :], w_in[...], NT)
+            for d in range(heads - 1):
+                du_copy(d).wait()
+                dn = dn + du_got[d].astype(F32)
+            du, grad = input_gradient(dn, u[here, :], norm_gain_of(block, u.shape[1])[...], above[...])
+            du_rows[...] = du.astype(BF)
+            inputs.start()
+            few_mine[...] = few0[...]
+            wide = few0.shape[1]
+            for i in range(2):
+                few_mine[8 + i : 9 + i, :] = grad[:, i * wide : (i + 1) * wide]
+            pl.when(layer == 0)(lambda: few_to_core(few1).start())
+            pl.when(layer == 1)(lambda: few_to_core(few_mine).start())
+
+        @pl.when(t == 7)
         def _():
             few_to_core(few_mine).wait()
             pl.when(layer == 0)(lambda: few_seq.__setitem__(me, few_mine[...] + few_core[...]))
@@ -1090,7 +1225,7 @@
             for d in range(size - 1):
                 few_to_seq(d).start()
 
-        @pl.when(t == 8)
+        @pl.when(t == 11)
         def _():
             for d in range(size - 1):
                 few_to_seq(d).wait()
@@ -1102,7 +1237,7 @@
             for d in range(heads - 1):
                 few_to_head(d).start()
 
-        @pl.when(t == 14)
+        @pl.when(t == 16)
         def _():
             for d in range(heads - 1):
                 few_to_head(d).wait()
@@ -1111,14 +1246,14 @@
                 total = total + few_head[i]
             few_o[FEW // 2 :, :] = total
 
-        @pl.when(t == ready)
-        def _():
-            total = shared[block(head), :].astype(F32)
+        @pl.when(t == 4)
+        def _():
+            total = shared[shared_block(head), :].astype(F32)
             for d in range(heads - 1):
                 scatter(d).wait()
                 total = total + shared_got[d].astype(F32)
-            own[plain : plain + SHARED, :] = total.astype(BF)
-            own[plain - OWN : plain, :] = shared[0:OWN, :]
+            own[tail_at + OWN : tail_at + OWN + SHARED, :] = total.astype(BF)
+            own[tail_at : tail_at + OWN, :] = shared[0:OWN, :]
 
         guarded(reduce, 0, t - skew * (far - me))
         guarded(reduce, 1, t - skew * me)
@@ -1127,7 +1262,8 @@
 
         @pl.when(t == finished)
         def _():
-            shared_o[head] = out[plain:rows, :]
+            tail_o[...] = out[tail_at : tail_at + OWN, :]
+            shared_o[head] = out[tail_at + OWN : tail_at + OWN + SHARED, :]
             for d in range(heads - 1):
                 gather(d).start()
 
@@ -1147,57 +1283,57 @@
             def _():
                 sending(side, p, True, out).wait_send()
 
+            final(side, p, lambda copy: copy.wait(), lambda copy: copy.wait_send())
+            final(side, p, lambda copy: give(side, p, first_o, pl.ds(0, PIECE)).wait_recv(), lambda copy: None)
         return 0
 
     lax.fori_loop(0, parts, drain, 0)
     for d in range(heads - 1):
         gather(d).wait()
-
-    def drain_trade(p, _):
-        for side in range(2):
-            unless_tail(side, p, lambda: pl.when(layer == 0)(give(side, p).wait_recv))
-            unless_tail(side, p, lambda: pl.when(layer == 1)(give(side, p).wait_send))
-        return 0
-
-    lax.fori_loop(0, parts, drain_trade, 0)
-    pl.when(layer == 0)(give_all.wait_send)
-    pl.when(layer == 1)(give_all.wait_recv)
+    pl.when(layer == 0)(lambda: all_of(given, lambda copy: copy.wait_send()))
+    pl.when(layer == 1)(lambda: all_of(kept, lambda copy: copy.wait()))
+    pl.when(layer == 1)(lambda: all_of(given, lambda copy: copy.wait_recv()))
+
     inputs.finish()
 
 
-def grad_sum(layer0, tails, fews, done, size, heads, skew=2):
-    width = done.shape[1]
-    rows = done.shape[0] + OWN + SHARED
-    parts = rows // 2 // PIECE
+def grad_sum(layer0, body1, tails, fews, done, size, heads, skew=2):
+    width = body1.shape[1]
+    total = body1.shape[0] + done[1].shape[0]
     n, d_model = layer0[3].shape
+    half = LATE * PIECE + (total + OWN + SHARED) // 2
+    parts = half // PIECE
     vm = pl.BlockSpec(memory_space=pltpu.VMEM)
     anywhere = pl.BlockSpec(memory_space=pl.ANY)
     pair = pltpu.SemaphoreType.DMA((2, parts))
     sems = lambda *k: pltpu.SemaphoreType.DMA(k)
-    tiles = done.shape[0] // 256
+    tiles = total // 256
+    big = pltpu.VMEM((2 * half, width), BF)
+    body = pltpu.VMEM((total, width), BF)
     return pl.pallas_call(
         functools.partial(grad_sum_kernel, size, heads, skew),
         out_shape=(
-            shape((rows, width), BF),
+            shape((total, width), BF),
+            shape((total, width), BF),
+            shape((OWN, width), BF),
             shape((heads, SHARED, width), BF),
             shape((FEW, width), F32),
-            shape(done.shape, BF),
             shape((2 * n, d_model), BF),
         ),
-        in_specs=[vm] * 8 + [anywhere] * 2 + [vm] * 2 + [anywhere],
-        out_specs=(vm, vm, vm, anywhere, anywhere),
-        scratch_shapes=[pltpu.VMEM((rows, width), BF) for _ in range(3)]
+        in_specs=[vm] * 8 + [anywhere] * 3 + [vm] * 2 + [anywhere] * 2,
+        out_specs=(anywhere, anywhere, vm, vm, vm, anywhere),
+        scratch_shapes=[big, body, big, big]
         + [pltpu.VMEM((OWN + heads * SHARED, width), BF) for _ in range(2)]
         + [pltpu.VMEM((heads - 1, SHARED, width), BF)]
         + [pltpu.VMEM((FEW, width), F32), pltpu.VMEM((size, FEW, width), F32)]
         + [pltpu.VMEM((heads, FEW // 2, width), F32)]
-        + [pltpu.VMEM(done.shape, BF)]
+        + [body] * 2
         + [pltpu.VMEM((heads - 1, n // heads, d_model), BF) for _ in range(2)]
         + [pltpu.VMEM((n // heads, d_model), BF), pltpu.VMEM((FEW, width), F32)]
         + [sems(tiles)] * 2
-        + [pair] * 6
+        + [pair] * 7
         + [sems(2, heads - 1)] * 2
-        + [sems(7)]
+        + [sems(11)]
         + [sems(size - 1)] * 2
         + [sems(heads - 1)] * 4
         + collect_sems(heads),
@@ -1205,29 +1341,18 @@
             collective_id=8, has_side_effects=True, vmem_limit_bytes=VMEM_LIMIT
         ),
         name="grad_sum",
-    )(*layer0, *tails, *fews, done)
-
-
-def unpack_kernel(dims, mine, traded, done, mine_low, traded_low, done_low, own, shared, few,
+    )(*layer0, body1, *tails, *fews, *done)
+
+
+def unpack_kernel(dims, first, second, first_low, second_low, own, shared, few,
                   z_o, x_o, out_o, bc_o, dt_o, conv_o, conv_bias_o, bc_conv_o, bc_bias_o,
                   dt_bias_o, a_log_o, skip_o, gate_o, gain_o):
     heads, inner, states = dims
-    layer = lax.axis_index("section")
     half = own.shape[1]
-
-    @pl.when(layer == 0)
-    def _():
-        z_o[...] = mine[...].astype(F32)
-        x_o[...] = traded[...].astype(F32)
-        out_o[:, :half] = mine_low[...].astype(F32)
-        out_o[:, half:] = traded_low[...].astype(F32)
-
-    @pl.when(layer == 1)
-    def _():
-        z_o[...] = traded[...].astype(F32)
-        x_o[...] = done[...].astype(F32)
-        out_o[:, :half] = traded_low[...].astype(F32)
-        out_o[:, half:] = done_low[...].astype(F32)
+    z_o[...] = first[...].astype(F32)
+    x_o[...] = second[...].astype(F32)
+    out_o[:, :half] = first_low[...].astype(F32)
+    out_o[:, half:] = second_low[...].astype(F32)
 
     @pl.when(pl.program_id(0) == 0)
     def _():
@@ -1250,9 +1375,9 @@
         skip_o[...] = few[6:7, 2 * LANES : 2 * LANES + heads]
 
 
-def unpack(grads, traded, done, shared, few, dims, steps=6):
+def unpack(first, second, own, shared, few, dims, steps=6):
     heads, inner, states = dims
-    half = grads.shape[1]
+    half = first.shape[1]
     width = 2 * half
     tall, low = width // steps, inner // steps
     upper = pl.BlockSpec((tall, half), lambda i: (i, 0))
@@ -1271,14 +1396,12 @@
         functools.partial(unpack_kernel, dims),
         grid=(steps,),
         out_shape=[shape(a, F32) for a, _ in outs] + [shape(a, F32) for a in fixed],
-        in_specs=[upper] * 3
-        + [lower] * 3
-        + [pl.BlockSpec((OWN, half), lambda i: ((width + inner) // OWN, 0)), whole(shared), whole(few)],
+        in_specs=[upper] * 2 + [lower] * 2 + [whole(own), whole(shared), whole(few)],
         out_specs=[pl.BlockSpec(b, lambda i: (i, 0)) for _, b in outs]
         + [pl.BlockSpec(a, lambda i: (0, 0)) for a in fixed],
         compiler_params=pltpu.CompilerParams(vmem_limit_bytes=VMEM_LIMIT),
         name="unpack",
-    )(grads, traded, done, grads, traded, done, grads, shared, few)
+    )(first, second, first, second, own, shared, few)
 
 
 def normalise(u, gain):
@@ -1316,60 +1439,53 @@
         axis=0,
     )
     gains = jnp.broadcast_to(norm_gain, (8, d_model))
-    w_in2, w_out2, vectors2 = both_layers(
+    w_in0, w_out0, block0, w_in1, w_out1, block1 = both_layers(
         [[w_z[0], w_x[0], w_bc[0], pad_heads(w_dt[0])], [w_out[0]], [taps, vectors, gains]]
     )
-    gains2 = vectors2[:, :, wide + inner :]
-    taps2, vectors2 = vectors2[:, :, :wide], vectors2[:, :, wide : wide + inner]
 
     u = lax.dynamic_slice_in_dim(inputs, me * batch, batch, 0).reshape(tokens, d_model)
     cot = lax.dynamic_slice_in_dim(cotangent, me * batch, batch, 0).reshape(tokens, d_model)
 
-    consts = []
-    for l in range(2):
-        gain = gains2[l, 0:1]
-        kernel, bias = taps2[l, 0:4], taps2[l, 4:5]
-        skip, gate = vectors2[l, 0:1], vectors2[l, 1:2]
-        dt_b, a_neg = vectors2[l, 2:3, :LANES], vectors2[l, 2:3, LANES : 2 * LANES]
-        consts.append((gain, kernel, bias, dt_b, a_neg, skip, gate))
     flat = lambda a: a.reshape(tokens, -1)
     stacked = lambda a: a.reshape(batch, n, -1)
 
-    normed0 = normalise(u, consts[0][0])
-    proj0 = stacked(dot(normed0, w_in2[0]))
+    normed0 = normalise(u, block0[0:1, block0.shape[1] - d_model :])
+    proj0 = stacked(dot(normed0, w_in0))
     cx0, dt0, cum0, state0, halo0, y0, yn0, stats0 = ssd_fwd(
-        proj0, *consts[0][1:], None, dims, seq_size, head_size, full
-    )
-    h0, normed1, proj1 = head_fwd(flat(yn0), w_out2[0], u, head_size, [w_in2[1], consts[1][0]])
+        proj0, block0, None, dims, seq_size, head_size, full
+    )
+    h0, normed1, proj1 = head_fwd(flat(yn0), w_out0, u, head_size, [w_in1, block1])
     proj1 = stacked(proj1)
-    dyn1 = stacked(dot(cot, w_out2[1], NT))
+    dyn1 = stacked(dot(cot, w_out1, NT))
     cx1, dt1, cum1, state1, halo1, y1, yn1, stats1 = ssd_fwd(
-        proj1, *consts[1][1:], dyn1, dims, seq_size, head_size, full
-    )
-    (h1_rows,) = head_fwd(flat(yn1), w_out2[1], h0, head_size, [])
+        proj1, block1, dyn1, dims, seq_size, head_size, full
+    )
+    h1_rows, body1_out = head_fwd(flat(yn1), w_out1, h0, head_size, [], cot)
+    done_out = lax.psum(body1_out, "seq")
 
     g_in1, gate1, conv1, small1, layer_outputs = ssd_bwd(
-        dyn1, y1, proj1, halo1, cx1, dt1, cum1, state1, stats1, *consts[1][1:], [h1_rows, h0],
+        dyn1, y1, proj1, halo1, cx1, dt1, cum1, state1, stats1, block1, [h1_rows, h0],
         dims, seq_size, head_size, full,
     )
     g_in1 = flat(g_in1)
     du1, du1_rows, gain1, dyn0, body1 = head_bwd(
-        g_in1, w_in2[1], cot, h0, consts[1][0], w_out2[0], normed1, flat(yn1), head_size
-    )
-    done = lax.psum(body1, "seq")
+        g_in1, w_in1, cot, h0, block1, w_out0, normed1, flat(yn1), head_size
+    )
+    body1_early, done_out = lax.optimization_barrier((body1[: d_model - 2 * LATE * PIECE], done_out))
+    done = lax.psum(body1_early, "seq")
     tail1, few1 = grad_tail(normed1, g_in1, conv1, small1, gate1, gain1, dims, head_size)
     g_in0, gate0, conv0, small0 = ssd_bwd(
-        stacked(dyn0), y0, proj0, halo0, cx0, dt0, cum0, state0, stats0, *consts[0][1:], [],
+        stacked(dyn0), y0, proj0, halo0, cx0, dt0, cum0, state0, stats0, block0, [],
         dims, seq_size, head_size, full,
     )
     g_in0 = flat(g_in0)
     tail0, few0 = grad_tail(normed0, g_in0, conv0, small0, gate0, jnp.zeros_like(gain1), dims, head_size)
-    grads, shared, few, traded, input_grads = grad_sum(
-        (g_in0, w_in2[0], du1_rows, u, consts[0][0], normed0, flat(yn0), du1),
-        (tail0, tail1), (few0, few1), done, seq_size, head_size,
+    first, second, own, shared, few, input_grads = grad_sum(
+        (g_in0, w_in0, du1_rows, u, block0, normed0, flat(yn0), du1),
+        body1, (tail0, tail1), (few0, few1), (done, done_out), seq_size, head_size,
     )
     g_z, g_x, g_out, g_bc, g_dt, g_conv, g_conv_bias, g_bc_conv, g_bc_bias, *scalars, g_gate, g_gain = unpack(
-        grads, traded, done, shared, few, dims
+        first, second, own, shared, few, dims
     )
 
     return (

time: 649 us -> 590 us (0.909)
  waiting for transfers between devices: 70.9 us -> 14.3 us
  local copies, waits for them, and re-layouts: 32.6 us -> 17.4 us
  Pallas kernels: 506 us -> 515 us
    psum x1 -> x2, waiting for transfers between devices: 70.9 us -> 14.3 us  [the longest x1 14.3 us: on_device(): done = lax.psum(body1_early, 'seq')]
    squeeze x7 -> x0, local copies, waits for them, and re-layouts: 20.7 us -> none  [the longest x1 11.2 us: on_device(): proj0 = stacked(dot(normed0, w_in2[0]))]
    pallas_call x1, Pallas kernels: 150 us -> 157 us  [grad_sum(): pl.pallas_call(functools.partial(grad_sum_kernel, size, heads, skew), out...]
  transfers between devices with their start and end apart: 1 -> 2, of which waited for: 1 -> 1; matrix products, arithmetic and copies ran while one was open for 0% -> 1% of each run, Pallas kernels for 11% -> 31%
where the time goes in v3:
time: 590 us; the launch traced here: 581 us
  Pallas kernels  515 us (87%)
  local copies, waits for them, and re-layouts  17.4 us (3%)
  between operations  14.5 us (2%)
  waiting for transfers between devices  14.3 us (2%)
  matrix products  11.2 us (2%)
  other arithmetic  8.16 us (1%)
    pallas_call x1, Pallas kernels, grad_sum(): pl.pallas_call(functools.partial(grad_sum_kernel, size, heads, skew), out...  157 us
    pallas_call x2, Pallas kernels, ssd_bwd(): pl.pallas_call(functools.partial(ssd_bwd_kernel, dims, size, heads_axis,...  123 us
    pallas_call x2, Pallas kernels, head_fwd(): pl.pallas_call(functools.partial(head_fwd_kernel, size, not more), out_sh...  90 us
    pallas_call x2, Pallas kernels, ssd_fwd(): pl.pallas_call(functools.partial(ssd_fwd_kernel, dims, size, heads_axis,...  58 us
    pallas_call x1, Pallas kernels, head_bwd(): pl.pallas_call(functools.partial(head_bwd_kernel, size), out_shape=(shape...  52.1 us
    pallas_call x1, Pallas kernels, both_layers(): pl.pallas_call(functools.partial(both_layers_kernel, places), out_shape=t...  17.1 us
    psum x1, waiting for transfers between devices, on_device(): done = lax.psum(body1_early, 'seq')  14.3 us
  transfers between devices with their start and end apart: 2, of which 1 were waited for; matrix products, arithmetic and copies ran while one was open for 1% of the time, Pallas kernels for 31%

profile of v3, /device:TPU:0, one launch (start us, length us, event | category | flops | bytes accessed | tf_op | source)
XLA Modules:
  0.0 580.9 jit_solution(10859320186120343086)
XLA Ops:
  7.2 0.0 copy-start
  7.2 0.0 all-reduce.6.cloned.1.call-start
  7.2 1.2 copy.32
  8.4 0.7 broadcast_in_dim.46
  9.2 0.1 broadcast_in_dim_reshape.3
  9.3 0.7 exponential_negate_fusion
  9.9 0.8 pad.12.refs_3_
  10.8 0.7 reduce.1
  11.5 0.7 select_maximum_fusion.1
  12.1 0.1 pad.18.clone
  12.2 1.4 fusion.10.refs_6_
  13.6 1.4 maximum_maximum_fusion.refs_5_
  15.0 0.6 broadcast_in_dim.49.refs_7_
  15.6 17.1 %both_layers.1 = (bf16[1536,1920]{1,0:T(8,128)(2,1)}, bf16[768,1536]{1,0:T(8,128)(2,1)}, f32[8,3328]{1,0:T(8,128)}, bf16[1536,1920]{1,0:T(8,128)(2,1)}, bf16[768,1536]{1,0:T(8,128)(2,1)}, /*index=5*/f32[8,3328]{1,0:T(8,128)}) custom-call(bf16[1536,768]{1,0:T(8,128)(2,1)} %bitcast.53, bf16[1536,768]{1,0:T(8,128)(2,1)} %bitcast.54, ...), custom_call_target="tpu_custom_call" | custom-call | tf_op jit(solution)/shard_map/both_layers/pallas_call | solution.py:151
  32.7 0.8 slice_reduce_fusion
  33.5 1.8 fusion.2
  35.3 0.0 copy-start.2
  35.3 8.6 %fusion.refs_0_.proj = f32[2,256,1920]{2,1,0:T(8,128)} fusion(bf16[1536,1920]{1,0:T(8,128)(2,1)} %get-tuple-element.85.w_in, bf16[2,256,1536]{2,1,0:T(8,128)(2,1)S(1)} %get-tuple-element.167, f32[1536]{0:T(1024)S(1)} %slice_reduce_fusion, f32[2,256]{1,0:T(2,128)S(1)} %get-tuple-element.169), kind=kOutput, calls=%fused_computation | convolution fusion | flops 3023044608 | bytes 11411456 | tf_op jit(solution)/shard_map/dot_general | solution.py:24
  44.0 0.0 copy-done.2
  44.0 27.7 %ssd_fwd.2 = (f32[2,256,1024]{2,1,0:T(8,128)}, f32[2,256,128]{2,1,0:T(8,128)}, f32[2,256,128]{2,1,0:T(8,128)}, f32[2,128,768]{2,1,0:T(8,128)}, bf16[2,16,1024]{2...) custom-call(f32[2,256,1920]{2,1,0:T(8,128)} %fusion.refs_0_.proj, ...), custom_call_target="tpu_custom_call" | custom-call | tf_op jit(solution)/shard_map/ssd_fwd/pallas_call | solution.py:388
  71.6 0.0 copy-done
  71.7 0.0 copy-start.6
  71.7 0.1 constant_dynamic-slice_fusion.1
  71.8 0.0 copy-start.4
  71.8 2.1 copy-done.6
  73.9 2.6 fusion.5.refs_2_.dyn
  76.4 0.0 copy-done.4
  76.4 64.4 %head_fwd.2 = (bf16[512,1536]{1,0:T(8,128)(2,1)}, bf16[512,1536]{1,0:T(8,128)(2,1)}, f32[512,1920]{1,0:T(8,128)}) custom-call(bf16[512,768]{1,0:T(8,128)(2,1)} %bitcast.47, bf16[768,1536]{1,0:T(8,128)(2,1)} %get-tuple-element.87.w_out, bf16[512,1536]{1,0:T(8,128)(2,1)} %bitcast.37, bf16[1536,1920]{1,0:T(8,128)(2,1)} %get-tuple-element.88.refs_0_.w_in, ...), custom_call_target="tpu_custom_call" | custom-call | tf_op jit(solution)/shard_map/head_fwd/pallas_call | solution.py:727
  140.9 30.3 %ssd_fwd.3 = (f32[2,256,1024]{2,1,0:T(8,128)}, f32[2,256,128]{2,1,0:T(8,128)}, f32[2,256,128]{2,1,0:T(8,128)}, f32[2,128,768]{2,1,0:T(8,128)}, bf16[2,16,1024]{2...) custom-call(f32[2,256,1920]{2,1,0:T(8,128)} %bitcast.39, ...), custom_call_target="tpu_custom_call" | custom-call | tf_op jit(solution)/shard_map/ssd_fwd/pallas_call | solution.py:388
  171.2 25.6 %head_fwd.3 = (bf16[128,1536]{1,0:T(8,128)(2,1)}, bf16[768,768]{1,0:T(8,128)(2,1)}) custom-call(bf16[512,768]{1,0:T(8,128)(2,1)} %bitcast.49, bf16[768,1536]{1,0:T(8,128)(2,1)} %get-tuple-element.83.w_out, bf16[512,1536]{1,0:T(8,128)(2,1)} %get-tuple-element.99.u.refs_1_, bf16[512,1536]{1,0:T(8,128)(2,1)} %bitcast.41), custom_call_target="tpu_custom_call" | custom-call | tf_op jit(solution)/shard_map/head_fwd/pallas_call | solution.py:727
  196.7 0.0 all-reduce.6.cloned.1.call-update
  196.8 0.0 all-reduce.8.cloned.1.call-start
  196.8 72.5 %ssd_bwd.2 = (bf16[2,256,1920]{2,1,0:T(8,128)(2,1)}, f32[2,8,768]{2,1,0:T(8,128)}, f32[2,8,1024]{2,1,0:T(8,128)}, f32[2,8,128]{2,1,0:T(8,128)}, bf16[1024,1536]{1,0:T(8,128)(2,1)}) custom-call(f32[2,256,768]{2,1,0:T(8,128)} %fusion.5.refs_2_.dyn, f32[2,256,768]{2,1,0:T(8,128)} %get-tuple-element.91.y, f32[2,256,1920]{2,1,0:T(8,128)} %bitcast.40, ...), custom_call_target="tpu_custom_call" | custom-call | tf_op jit(solution)/shard_map/ssd_bwd/pallas_call | solution.py:613
  269.4 52.1 %head_bwd.1 = (bf16[512,1536]{1,0:T(8,128)(2,1)}, f32[128,1536]{1,0:T(8,128)}, f32[8,1536]{1,0:T(8,128)}, f32[512,768]{1,0:T(8,128)}, bf16[1536,768]{1,0:T(8,128)(2,1)}) custom-call(bf16[512,1920]{1,0:T(8,128)(2,1)} %bitcast.43, bf16[1536,1920]{1,0:T(8,128)(2,1)} %get-tuple-element.88.refs_0_.w_in, bf16[512,1536]{1,0:T(8,128)(2,1)} %bitcast.42, ...), custom_call_target="tpu_custom_call" | custom-call | tf_op jit(solution)/shard_map/head_bwd/pallas_call | solution.py:826
  321.5 2.6 slice.7
  324.1 0.0 all-reduce.6.cloned.1.call-done.done_out
  324.1 0.0 all-reduce.8.cloned.1.call-update
  324.1 3.8 grad_tail.3
  327.9 0.0 copy-start.3
  327.9 50.1 %ssd_bwd.3 = (bf16[2,256,1920]{2,1,0:T(8,128)(2,1)}, f32[2,8,768]{2,1,0:T(8,128)}, f32[2,8,1024]{2,1,0:T(8,128)}, f32[2,8,128]{2,1,0:T(8,128)}) custom-call(f32[2,256,768]{2,1,0:T(8,128)} %bitcast.56, f32[2,256,768]{2,1,0:T(8,128)} %get-tuple-element.105.y, f32[2,256,1920]{2,1,0:T(8,128)} %fusion.refs_0_.proj, bf16[2,16,1024]{2,1,0:T(8,128)(2,1)} %get-tuple-element.106.halo, ...), custom_call_target="tpu_custom_call" | custom-call | tf_op jit(solution)/shard_map/ssd_bwd/pallas_call | solution.py:613
  378.0 0.0 copy-done.3
  378.0 1.6 multiply_convert_fusion.normed
  379.5 0.6 broadcast_in_dim.50.gain
  380.2 3.8 grad_tail.2
  383.9 14.3 %all-reduce.8.cloned.1.call-done.done = bf16[960,768]{1,0:T(8,128)(2,1)} async-done(((bf16[960,768]{1,0:T(8,128)(2,1)}), bf16[960,768]{1,0:T(8,128)(2,1)}) %all-reduce.8.cloned.1.call-update) | async-done | bytes 1474576 | tf_op jit(solution)/shard_map/psum | solution.py:1475
  398.2 157.5 %grad_sum.1 = (bf16[2304,768]{1,0:T(8,128)(2,1)}, bf16[2304,768]{1,0:T(8,128)(2,1)}, bf16[32,768]{1,0:T(8,128)(2,1)}, bf16[4,160,768]{2,1,0:T(8,128)(2,1)}, f32[...) custom-call(bf16[512,1920]{1,0:T(8,128)(2,1)} %bitcast.46, bf16[1536,1920]{1,0:T(8,128)(2,1)} %get-tuple-element.85.w_in, ...), custom_call_target="tpu_custom_call" | custom-call | tf_op jit(solution)/shard_map/grad_sum/pallas_call | solution.py:1313
  555.7 10.5 %unpack.1 = (f32[1536,768]{1,0:T(8,128)}, f32[1536,768]{1,0:T(8,128)}, f32[768,1536]{1,0:T(8,128)}, f32[1536,256]{1,0:T(8,128)}, f32[1536,12]{1,0:T(8,128)}, /*i...) custom-call(bf16[2304,768]{1,0:T(8,128)(2,1)} %get-tuple-element.131, ...), custom_call_target="tpu_custom_call" | custom-call | tf_op jit(solution)/shard_map/unpack/pallas_call | solution.py:1395
  566.3 2.0 copy.33
  568.3 0.0 copy-start.5
  568.3 0.0 copy-start.1
  568.3 3.9 copy.39
  572.2 0.0 copy-done.5
  572.2 1.7 copy.40
  573.9 0.0 copy-done.1
  (5 shorter events, 0.0 us)
Async XLA Ops:
  7.2 64.5 %copy-start = (bf16[4,256,1536]{2,1,0:T(8,128)(2,1)S(1)}, bf16[4,256,1536]{2,1,0:T(8,128)(2,1)}, u32[]{:S(2)}) copy-start(bf16[4,256,1536]{2,1,0:T(8,128)(2,1)} %param.17) | copy-start | bytes 9437188
  7.2 316.9 %all-reduce.6.cloned.1.call-start = ((), (), s32[]{:S(2)}) async-start(), calls=%async_computation | async-start | bytes 2359296 | tf_op jit(solution)/shard_map/psum | solution.py:1464
  35.3 8.6 %copy-start.2 = (bf16[2,256,1536]{2,1,0:T(8,128)(2,1)}, bf16[2,256,1536]{2,1,0:T(8,128)(2,1)S(1)}, u32[]{:S(2)}) copy-start(bf16[2,256,1536]{2,1,0:T(8,128)(2,1)S(1)} %get-tuple-element.167) | copy-start | bytes 4718596
  71.7 2.2 copy-start.6
  71.8 4.7 copy-start.4
  196.8 201.5 %all-reduce.8.cloned.1.call-start = ((), (), s32[]{:S(2)}) async-start(), calls=%async_computation.1 | async-start | bytes 2949120 | tf_op jit(solution)/shard_map/psum | solution.py:1475
  327.9 50.1 %copy-start.3 = (bf16[2,256,1536]{2,1,0:T(8,128)(2,1)S(1)}, bf16[2,256,1536]{2,1,0:T(8,128)(2,1)}, u32[]{:S(2)}) copy-start(bf16[2,256,1536]{2,1,0:T(8,128)(2,1)} %copy-done.2) | copy-start | bytes 4718596
  568.3 3.9 copy-start.5
  568.3 5.6 copy-start.1
Sparse Core Ops, SparseCore 0:
  196.9 87.2 all-reduce.5
  324.2 73.9 all-reduce.7

commit v4 on v3

--- a/solution.py
+++ b/solution.py
@@ -925,9 +925,9 @@
 
 OWN = 32
 SHARED = 160
-PIECE = 48
+PIECE = 96
 TAIL = (OWN + SHARED) // PIECE
-LATE = 6
+LATE = 4
 FEW = 16
 
 
@@ -1297,7 +1297,7 @@
     inputs.finish()
 
 
-def grad_sum(layer0, body1, tails, fews, done, size, heads, skew=2):
+def grad_sum(layer0, body1, tails, fews, done, size, heads, skew=1):
     width = body1.shape[1]
     total = body1.shape[0] + done[1].shape[0]
     n, d_model = layer0[3].shape
@@ -1461,13 +1461,13 @@
         proj1, block1, dyn1, dims, seq_size, head_size, full
     )
     h1_rows, body1_out = head_fwd(flat(yn1), w_out1, h0, head_size, [], cot)
-    done_out = lax.psum(body1_out, "seq")
 
     g_in1, gate1, conv1, small1, layer_outputs = ssd_bwd(
         dyn1, y1, proj1, halo1, cx1, dt1, cum1, state1, stats1, block1, [h1_rows, h0],
         dims, seq_size, head_size, full,
     )
-    g_in1 = flat(g_in1)
+    g_in1, body1_out = lax.optimization_barrier((flat(g_in1), body1_out))
+    done_out = lax.psum(body1_out, "seq")
     du1, du1_rows, gain1, dyn0, body1 = head_bwd(
         g_in1, w_in1, cot, h0, block1, w_out0, normed1, flat(yn1), head_size
     )

time: 590 us -> 570 us (0.966)
  Pallas kernels: 515 us -> 502 us
  waiting for transfers between devices: 14.3 us -> 7.57 us
    pallas_call x2, Pallas kernels: 123 us -> 110 us  [ssd_bwd(): pl.pallas_call(functools.partial(ssd_bwd_kernel, dims, size, heads_axis,...]
    psum x1, waiting for transfers between devices: 14.3 us -> 7.54 us  [on_device(): done = lax.psum(body1_early, 'seq')]
  transfers between devices with their start and end apart: 2 -> 2, of which waited for: 1 -> 1; matrix products, arithmetic and copies ran while one was open for 1% -> 1% of each run, Pallas kernels for 31% -> 19%
where the time goes in v4:
time: 570 us; the launch traced here: 561 us
  Pallas kernels  502 us (88%)
  local copies, waits for them, and re-layouts  17.2 us (3%)
  between operations  14.5 us (3%)
  matrix products  11.2 us (2%)
  other arithmetic  8.16 us (1%)
  waiting for transfers between devices  7.57 us (1%)
    pallas_call x1, Pallas kernels, grad_sum(): pl.pallas_call(functools.partial(grad_sum_kernel, size, heads, skew), out...  157 us
    pallas_call x2, Pallas kernels, ssd_bwd(): pl.pallas_call(functools.partial(ssd_bwd_kernel, dims, size, heads_axis,...  110 us
    pallas_call x2, Pallas kernels, head_fwd(): pl.pallas_call(functools.partial(head_fwd_kernel, size, not more), out_sh...  90 us
    pallas_call x2, Pallas kernels, ssd_fwd(): pl.pallas_call(functools.partial(ssd_fwd_kernel, dims, size, heads_axis,...  57.9 us
    pallas_call x1, Pallas kernels, head_bwd(): pl.pallas_call(functools.partial(head_bwd_kernel, size), out_shape=(shape...  52.6 us
    pallas_call x1, Pallas kernels, both_layers(): pl.pallas_call(functools.partial(both_layers_kernel, places), out_shape=t...  17.1 us
  transfers between devices with their start and end apart: 2, of which 1 were waited for; matrix products, arithmetic and copies ran while one was open for 1% of the time, Pallas kernels for 19%

profile of v4, /device:TPU:0, one launch (start us, length us, event | category | flops | bytes accessed | tf_op | source)
XLA Modules:
  0.0 561.0 jit_solution(3867990246364426388)
XLA Ops:
  7.2 0.0 copy-start
  7.2 0.0 all-reduce.6.cloned.1.call-start
  7.2 1.2 copy.32
  8.4 0.7 broadcast_in_dim.46
  9.2 0.1 broadcast_in_dim_reshape.3
  9.3 0.7 exponential_negate_fusion
  9.9 0.8 pad.12.refs_3_
  10.8 0.7 reduce.1
  11.5 0.7 select_maximum_fusion.1
  12.1 0.1 pad.18.clone
  12.2 1.4 fusion.10.refs_6_
  13.6 1.4 maximum_maximum_fusion.refs_5_
  15.0 0.6 broadcast_in_dim.49.refs_7_
  15.6 17.1 %both_layers.1 = (bf16[1536,1920]{1,0:T(8,128)(2,1)}, bf16[768,1536]{1,0:T(8,128)(2,1)}, f32[8,3328]{1,0:T(8,128)}, bf16[1536,1920]{1,0:T(8,128)(2,1)}, bf16[768,1536]{1,0:T(8,128)(2,1)}, /*index=5*/f32[8,3328]{1,0:T(8,128)}) custom-call(bf16[1536,768]{1,0:T(8,128)(2,1)} %bitcast.53, bf16[1536,768]{1,0:T(8,128)(2,1)} %bitcast.54, ...), custom_call_target="tpu_custom_call" | custom-call | tf_op jit(solution)/shard_map/both_layers/pallas_call | solution.py:151
  32.7 0.8 slice_reduce_fusion
  33.5 1.8 fusion.2
  35.3 0.0 copy-start.2
  35.3 8.6 %fusion.refs_0_.proj = f32[2,256,1920]{2,1,0:T(8,128)} fusion(bf16[1536,1920]{1,0:T(8,128)(2,1)} %get-tuple-element.87.w_in, bf16[2,256,1536]{2,1,0:T(8,128)(2,1)S(1)} %get-tuple-element.171, f32[1536]{0:T(1024)S(1)} %slice_reduce_fusion, f32[2,256]{1,0:T(2,128)S(1)} %get-tuple-element.173), kind=kOutput, calls=%fused_computation | convolution fusion | flops 3023044608 | bytes 11411456 | tf_op jit(solution)/shard_map/dot_general | solution.py:24
  44.0 0.0 copy-done.2
  44.0 27.7 %ssd_fwd.2 = (f32[2,256,1024]{2,1,0:T(8,128)}, f32[2,256,128]{2,1,0:T(8,128)}, f32[2,256,128]{2,1,0:T(8,128)}, f32[2,128,768]{2,1,0:T(8,128)}, bf16[2,16,1024]{2...) custom-call(f32[2,256,1920]{2,1,0:T(8,128)} %fusion.refs_0_.proj, ...), custom_call_target="tpu_custom_call" | custom-call | tf_op jit(solution)/shard_map/ssd_fwd/pallas_call | solution.py:388
  71.7 0.0 copy-done
  71.7 0.0 copy-start.6
  71.7 0.1 constant_dynamic-slice_fusion.1
  71.8 0.0 copy-start.4
  71.8 2.1 copy-done.6
  73.9 2.6 fusion.5.refs_2_.dyn
  76.4 0.0 copy-done.4
  76.5 64.4 %head_fwd.2 = (bf16[512,1536]{1,0:T(8,128)(2,1)}, bf16[512,1536]{1,0:T(8,128)(2,1)}, f32[512,1920]{1,0:T(8,128)}) custom-call(bf16[512,768]{1,0:T(8,128)(2,1)} %bitcast.47, bf16[768,1536]{1,0:T(8,128)(2,1)} %get-tuple-element.89.w_out, bf16[512,1536]{1,0:T(8,128)(2,1)} %bitcast.37, bf16[1536,1920]{1,0:T(8,128)(2,1)} %get-tuple-element.90.refs_0_.w_in, ...), custom_call_target="tpu_custom_call" | custom-call | tf_op jit(solution)/shard_map/head_fwd/pallas_call | solution.py:727
  140.9 30.3 %ssd_fwd.3 = (f32[2,256,1024]{2,1,0:T(8,128)}, f32[2,256,128]{2,1,0:T(8,128)}, f32[2,256,128]{2,1,0:T(8,128)}, f32[2,128,768]{2,1,0:T(8,128)}, bf16[2,16,1024]{2...) custom-call(f32[2,256,1920]{2,1,0:T(8,128)} %bitcast.39, ...), custom_call_target="tpu_custom_call" | custom-call | tf_op jit(solution)/shard_map/ssd_fwd/pallas_call | solution.py:388
  171.1 25.6 %head_fwd.3 = (bf16[128,1536]{1,0:T(8,128)(2,1)}, bf16[768,768]{1,0:T(8,128)(2,1)}) custom-call(bf16[512,768]{1,0:T(8,128)(2,1)} %bitcast.49, bf16[768,1536]{1,0:T(8,128)(2,1)} %get-tuple-element.85.w_out, bf16[512,1536]{1,0:T(8,128)(2,1)} %get-tuple-element.101.u.refs_1_, bf16[512,1536]{1,0:T(8,128)(2,1)} %bitcast.41), custom_call_target="tpu_custom_call" | custom-call | tf_op jit(solution)/shard_map/head_fwd/pallas_call | solution.py:727
  196.7 60.3 %ssd_bwd.2 = (bf16[2,256,1920]{2,1,0:T(8,128)(2,1)}, f32[2,8,768]{2,1,0:T(8,128)}, f32[2,8,1024]{2,1,0:T(8,128)}, f32[2,8,128]{2,1,0:T(8,128)}, bf16[1024,1536]{1,0:T(8,128)(2,1)}) custom-call(f32[2,256,768]{2,1,0:T(8,128)} %fusion.5.refs_2_.dyn, f32[2,256,768]{2,1,0:T(8,128)} %get-tuple-element.93.y, f32[2,256,1920]{2,1,0:T(8,128)} %bitcast.40, ...), custom_call_target="tpu_custom_call" | custom-call | tf_op jit(solution)/shard_map/ssd_bwd/pallas_call | solution.py:613
  257.0 0.0 all-reduce.6.cloned.1.call-update
  257.1 0.2 all-reduce.8.cloned.1.call-start
  257.3 52.6 %head_bwd.1 = (bf16[512,1536]{1,0:T(8,128)(2,1)}, f32[128,1536]{1,0:T(8,128)}, f32[8,1536]{1,0:T(8,128)}, f32[512,768]{1,0:T(8,128)}, bf16[1536,768]{1,0:T(8,128)(2,1)}) custom-call(bf16[512,1920]{1,0:T(8,128)(2,1)} %bitcast.43, bf16[1536,1920]{1,0:T(8,128)(2,1)} %get-tuple-element.90.refs_0_.w_in, bf16[512,1536]{1,0:T(8,128)(2,1)} %bitcast.42, ...), custom_call_target="tpu_custom_call" | custom-call | tf_op jit(solution)/shard_map/head_bwd/pallas_call | solution.py:826
  309.9 2.4 slice.7
  312.3 0.0 all-reduce.6.cloned.1.call-done.done_out
  312.3 0.0 all-reduce.8.cloned.1.call-update
  312.3 3.8 grad_tail.3
  316.1 0.0 copy-start.3
  316.1 49.2 %ssd_bwd.3 = (bf16[2,256,1920]{2,1,0:T(8,128)(2,1)}, f32[2,8,768]{2,1,0:T(8,128)}, f32[2,8,1024]{2,1,0:T(8,128)}, f32[2,8,128]{2,1,0:T(8,128)}) custom-call(f32[2,256,768]{2,1,0:T(8,128)} %bitcast.56, f32[2,256,768]{2,1,0:T(8,128)} %get-tuple-element.109.y, f32[2,256,1920]{2,1,0:T(8,128)} %fusion.refs_0_.proj, bf16[2,16,1024]{2,1,0:T(8,128)(2,1)} %get-tuple-element.110.halo, ...), custom_call_target="tpu_custom_call" | custom-call | tf_op jit(solution)/shard_map/ssd_bwd/pallas_call | solution.py:613
  365.2 0.0 copy-done.3
  365.3 1.6 multiply_convert_fusion.normed
  366.8 0.6 broadcast_in_dim.50.gain
  367.5 3.8 grad_tail.2
  371.2 7.5 %all-reduce.8.cloned.1.call-done.done = bf16[768,768]{1,0:T(8,128)(2,1)} async-done(((bf16[768,768]{1,0:T(8,128)(2,1)}), bf16[768,768]{1,0:T(8,128)(2,1)}) %all-reduce.8.cloned.1.call-update) | async-done | bytes 1179664 | tf_op jit(solution)/shard_map/psum | solution.py:1475
  378.8 157.1 %grad_sum.1 = (bf16[2304,768]{1,0:T(8,128)(2,1)}, bf16[2304,768]{1,0:T(8,128)(2,1)}, bf16[32,768]{1,0:T(8,128)(2,1)}, bf16[4,160,768]{2,1,0:T(8,128)(2,1)}, f32[...) custom-call(bf16[512,1920]{1,0:T(8,128)(2,1)} %bitcast.46, bf16[1536,1920]{1,0:T(8,128)(2,1)} %get-tuple-element.87.w_in, ...), custom_call_target="tpu_custom_call" | custom-call | tf_op jit(solution)/shard_map/grad_sum/pallas_call | solution.py:1313
  535.8 10.5 %unpack.1 = (f32[1536,768]{1,0:T(8,128)}, f32[1536,768]{1,0:T(8,128)}, f32[768,1536]{1,0:T(8,128)}, f32[1536,256]{1,0:T(8,128)}, f32[1536,12]{1,0:T(8,128)}, /*i...) custom-call(bf16[2304,768]{1,0:T(8,128)(2,1)} %get-tuple-element.135, ...), custom_call_target="tpu_custom_call" | custom-call | tf_op jit(solution)/shard_map/unpack/pallas_call | solution.py:1395
  546.4 2.0 copy.33
  548.4 0.0 copy-start.5
  548.4 0.0 copy-start.1
  548.4 3.9 copy.39
  552.3 0.0 copy-done.5
  552.3 1.7 copy.40
  554.0 0.0 copy-done.1
  (5 shorter events, 0.0 us)
Async XLA Ops:
  7.2 64.5 %copy-start = (bf16[4,256,1536]{2,1,0:T(8,128)(2,1)S(1)}, bf16[4,256,1536]{2,1,0:T(8,128)(2,1)}, u32[]{:S(2)}) copy-start(bf16[4,256,1536]{2,1,0:T(8,128)(2,1)} %param.17) | copy-start | bytes 9437188
  7.2 305.1 %all-reduce.6.cloned.1.call-start = ((), (), s32[]{:S(2)}) async-start(), calls=%async_computation | async-start | bytes 2359296 | tf_op jit(solution)/shard_map/psum | solution.py:1470
  35.3 8.7 %copy-start.2 = (bf16[2,256,1536]{2,1,0:T(8,128)(2,1)}, bf16[2,256,1536]{2,1,0:T(8,128)(2,1)S(1)}, u32[]{:S(2)}) copy-start(bf16[2,256,1536]{2,1,0:T(8,128)(2,1)S(1)} %get-tuple-element.171) | copy-start | bytes 4718596
  71.7 2.2 copy-start.6
  71.8 4.7 copy-start.4
  257.1 121.7 %all-reduce.8.cloned.1.call-start = ((), (), s32[]{:S(2)}) async-start(), calls=%async_computation.1 | async-start | bytes 2359296 | tf_op jit(solution)/shard_map/psum | solution.py:1475
  316.1 49.2 %copy-start.3 = (bf16[2,256,1536]{2,1,0:T(8,128)(2,1)S(1)}, bf16[2,256,1536]{2,1,0:T(8,128)(2,1)}, u32[]{:S(2)}) copy-start(bf16[2,256,1536]{2,1,0:T(8,128)(2,1)} %copy-done.2) | copy-start | bytes 4718596
  548.4 3.9 copy-start.5
  548.4 5.6 copy-start.1
Sparse Core Ops, SparseCore 0:
  257.2 52.9 all-reduce.5
  313.2 65.5 all-reduce.7

commit v5 on v4

--- a/solution.py
+++ b/solution.py
@@ -230,7 +230,10 @@
         for i in range(self.outgoing.shape[0] * self.parts):
             m, p = i // self.parts, i % self.parts
             at = slice(p * width, (p + 1) * width)
-            due = jnp.minimum(self.place * lag + apart * i, steps - 1)
+            offset = apart * i // 2
+            if at_step < steps - 1 and (at_step - offset < lag or (at_step - offset) % lag):
+                continue
+            due = jnp.minimum(self.place * lag + offset, steps - 1)
 
             @pl.when(jnp.logical_and(self.place > 0, due == at_step))
             def _():
@@ -256,7 +259,7 @@
         )
 
 
-PARTS = 3
+PARTS = 6
 
 
 def ssd_fwd_kernel(dims, size, heads_axis, full, has_dyn, *refs):

time: 570 us -> 568 us (level)
  no operation moved by 1% of the time
where the time goes in v5:
time: 568 us; the launch traced here: 559 us
  Pallas kernels  499 us (88%)
  local copies, waits for them, and re-layouts  17.2 us (3%)
  between operations  14.7 us (3%)
  matrix products  11.2 us (2%)
  waiting for transfers between devices  8.36 us (1%)
  other arithmetic  8.16 us (1%)
    pallas_call x1, Pallas kernels, grad_sum(): pl.pallas_call(functools.partial(grad_sum_kernel, size, heads, skew), out...  158 us
    pallas_call x2, Pallas kernels, ssd_bwd(): pl.pallas_call(functools.partial(ssd_bwd_kernel, dims, size, heads_axis,...  105 us
    pallas_call x2, Pallas kernels, head_fwd(): pl.pallas_call(functools.partial(head_fwd_kernel, size, not more), out_sh...  90 us
    pallas_call x2, Pallas kernels, ssd_fwd(): pl.pallas_call(functools.partial(ssd_fwd_kernel, dims, size, heads_axis,...  58.4 us
    pallas_call x1, Pallas kernels, head_bwd(): pl.pallas_call(functools.partial(head_bwd_kernel, size), out_shape=(shape...  52.6 us
    pallas_call x1, Pallas kernels, both_layers(): pl.pallas_call(functools.partial(both_layers_kernel, places), out_shape=t...  17.1 us
  transfers between devices with their start and end apart: 2, of which 1 were waited for; matrix products, arithmetic and copies ran while one was open for 1% of the time, Pallas kernels for 19%

profile of v5, /device:TPU:0, one launch (start us, length us, event | category | flops | bytes accessed | tf_op | source)
XLA Modules:
  0.0 559.3 jit_solution(5316360026174382076)
XLA Ops:
  7.2 0.0 copy-start
  7.2 0.0 all-reduce.6.cloned.1.call-start
  7.2 1.2 copy.32
  8.4 0.7 broadcast_in_dim.46
  9.2 0.1 broadcast_in_dim_reshape.3
  9.3 0.7 exponential_negate_fusion
  9.9 0.8 pad.12.refs_3_
  10.8 0.7 reduce.1
  11.5 0.7 select_maximum_fusion.1
  12.1 0.1 pad.18.clone
  12.2 1.4 fusion.10.refs_6_
  13.6 1.4 maximum_maximum_fusion.refs_5_
  15.0 0.6 broadcast_in_dim.49.refs_7_
  15.6 17.1 %both_layers.1 = (bf16[1536,1920]{1,0:T(8,128)(2,1)}, bf16[768,1536]{1,0:T(8,128)(2,1)}, f32[8,3328]{1,0:T(8,128)}, bf16[1536,1920]{1,0:T(8,128)(2,1)}, bf16[768,1536]{1,0:T(8,128)(2,1)}, /*index=5*/f32[8,3328]{1,0:T(8,128)}) custom-call(bf16[1536,768]{1,0:T(8,128)(2,1)} %bitcast.53, bf16[1536,768]{1,0:T(8,128)(2,1)} %bitcast.54, ...), custom_call_target="tpu_custom_call" | custom-call | tf_op jit(solution)/shard_map/both_layers/pallas_call | solution.py:151
  32.7 0.8 slice_reduce_fusion
  33.5 1.8 fusion.2
  35.3 0.0 copy-start.2
  35.3 8.6 %fusion.refs_0_.proj = f32[2,256,1920]{2,1,0:T(8,128)} fusion(bf16[1536,1920]{1,0:T(8,128)(2,1)} %get-tuple-element.87.w_in, bf16[2,256,1536]{2,1,0:T(8,128)(2,1)S(1)} %get-tuple-element.171, f32[1536]{0:T(1024)S(1)} %slice_reduce_fusion, f32[2,256]{1,0:T(2,128)S(1)} %get-tuple-element.173), kind=kOutput, calls=%fused_computation | convolution fusion | flops 3023044608 | bytes 11411456 | tf_op jit(solution)/shard_map/dot_general | solution.py:24
  44.0 0.0 copy-done.2
  44.0 27.8 %ssd_fwd.2 = (f32[2,256,1024]{2,1,0:T(8,128)}, f32[2,256,128]{2,1,0:T(8,128)}, f32[2,256,128]{2,1,0:T(8,128)}, f32[2,128,768]{2,1,0:T(8,128)}, bf16[2,16,1024]{2...) custom-call(f32[2,256,1920]{2,1,0:T(8,128)} %fusion.refs_0_.proj, ...), custom_call_target="tpu_custom_call" | custom-call | tf_op jit(solution)/shard_map/ssd_fwd/pallas_call | solution.py:391
  71.8 0.0 copy-done
  71.8 0.0 copy-start.6
  71.8 0.1 constant_dynamic-slice_fusion.1
  71.9 0.0 copy-start.4
  71.9 2.1 copy-done.6
  74.0 2.5 fusion.5.refs_2_.dyn
  76.6 0.0 copy-done.4
  76.6 64.4 %head_fwd.2 = (bf16[512,1536]{1,0:T(8,128)(2,1)}, bf16[512,1536]{1,0:T(8,128)(2,1)}, f32[512,1920]{1,0:T(8,128)}) custom-call(bf16[512,768]{1,0:T(8,128)(2,1)} %bitcast.47, bf16[768,1536]{1,0:T(8,128)(2,1)} %get-tuple-element.89.w_out, bf16[512,1536]{1,0:T(8,128)(2,1)} %bitcast.37, bf16[1536,1920]{1,0:T(8,128)(2,1)} %get-tuple-element.90.refs_0_.w_in, ...), custom_call_target="tpu_custom_call" | custom-call | tf_op jit(solution)/shard_map/head_fwd/pallas_call | solution.py:730
  141.0 30.6 %ssd_fwd.3 = (f32[2,256,1024]{2,1,0:T(8,128)}, f32[2,256,128]{2,1,0:T(8,128)}, f32[2,256,128]{2,1,0:T(8,128)}, f32[2,128,768]{2,1,0:T(8,128)}, bf16[2,16,1024]{2...) custom-call(f32[2,256,1920]{2,1,0:T(8,128)} %bitcast.39, ...), custom_call_target="tpu_custom_call" | custom-call | tf_op jit(solution)/shard_map/ssd_fwd/pallas_call | solution.py:391
  171.6 25.6 %head_fwd.3 = (bf16[128,1536]{1,0:T(8,128)(2,1)}, bf16[768,768]{1,0:T(8,128)(2,1)}) custom-call(bf16[512,768]{1,0:T(8,128)(2,1)} %bitcast.49, bf16[768,1536]{1,0:T(8,128)(2,1)} %get-tuple-element.85.w_out, bf16[512,1536]{1,0:T(8,128)(2,1)} %get-tuple-element.101.u.refs_1_, bf16[512,1536]{1,0:T(8,128)(2,1)} %bitcast.41), custom_call_target="tpu_custom_call" | custom-call | tf_op jit(solution)/shard_map/head_fwd/pallas_call | solution.py:730
  197.2 57.3 %ssd_bwd.2 = (bf16[2,256,1920]{2,1,0:T(8,128)(2,1)}, f32[2,8,768]{2,1,0:T(8,128)}, f32[2,8,1024]{2,1,0:T(8,128)}, f32[2,8,128]{2,1,0:T(8,128)}, bf16[1024,1536]{1,0:T(8,128)(2,1)}) custom-call(f32[2,256,768]{2,1,0:T(8,128)} %fusion.5.refs_2_.dyn, f32[2,256,768]{2,1,0:T(8,128)} %get-tuple-element.93.y, f32[2,256,1920]{2,1,0:T(8,128)} %bitcast.40, ...), custom_call_target="tpu_custom_call" | custom-call | tf_op jit(solution)/shard_map/ssd_bwd/pallas_call | solution.py:616
  254.5 0.0 all-reduce.6.cloned.1.call-update
  254.5 0.4 all-reduce.8.cloned.1.call-start
  255.0 52.6 %head_bwd.1 = (bf16[512,1536]{1,0:T(8,128)(2,1)}, f32[128,1536]{1,0:T(8,128)}, f32[8,1536]{1,0:T(8,128)}, f32[512,768]{1,0:T(8,128)}, bf16[1536,768]{1,0:T(8,128)(2,1)}) custom-call(bf16[512,1920]{1,0:T(8,128)(2,1)} %bitcast.43, bf16[1536,1920]{1,0:T(8,128)(2,1)} %get-tuple-element.90.refs_0_.w_in, bf16[512,1536]{1,0:T(8,128)(2,1)} %bitcast.42, ...), custom_call_target="tpu_custom_call" | custom-call | tf_op jit(solution)/shard_map/head_bwd/pallas_call | solution.py:829
  307.6 2.4 slice.7
  310.0 0.0 all-reduce.6.cloned.1.call-done.done_out
  310.0 0.0 all-reduce.8.cloned.1.call-update
  310.0 3.8 grad_tail.3
  313.8 0.0 copy-start.3
  313.8 47.9 %ssd_bwd.3 = (bf16[2,256,1920]{2,1,0:T(8,128)(2,1)}, f32[2,8,768]{2,1,0:T(8,128)}, f32[2,8,1024]{2,1,0:T(8,128)}, f32[2,8,128]{2,1,0:T(8,128)}) custom-call(f32[2,256,768]{2,1,0:T(8,128)} %bitcast.56, f32[2,256,768]{2,1,0:T(8,128)} %get-tuple-element.109.y, f32[2,256,1920]{2,1,0:T(8,128)} %fusion.refs_0_.proj, bf16[2,16,1024]{2,1,0:T(8,128)(2,1)} %get-tuple-element.110.halo, ...), custom_call_target="tpu_custom_call" | custom-call | tf_op jit(solution)/shard_map/ssd_bwd/pallas_call | solution.py:616
  361.6 0.0 copy-done.3
  361.6 1.6 multiply_convert_fusion.normed
  363.2 0.6 broadcast_in_dim.50.gain
  363.8 3.8 grad_tail.2
  367.6 8.3 %all-reduce.8.cloned.1.call-done.done = bf16[768,768]{1,0:T(8,128)(2,1)} async-done(((bf16[768,768]{1,0:T(8,128)(2,1)}), bf16[768,768]{1,0:T(8,128)(2,1)}) %all-reduce.8.cloned.1.call-update) | async-done | bytes 1179664 | tf_op jit(solution)/shard_map/psum | solution.py:1478
  375.9 157.9 %grad_sum.1 = (bf16[2304,768]{1,0:T(8,128)(2,1)}, bf16[2304,768]{1,0:T(8,128)(2,1)}, bf16[32,768]{1,0:T(8,128)(2,1)}, bf16[4,160,768]{2,1,0:T(8,128)(2,1)}, f32[...) custom-call(bf16[512,1920]{1,0:T(8,128)(2,1)} %bitcast.46, bf16[1536,1920]{1,0:T(8,128)(2,1)} %get-tuple-element.87.w_in, ...), custom_call_target="tpu_custom_call" | custom-call | tf_op jit(solution)/shard_map/grad_sum/pallas_call | solution.py:1316
  533.8 10.5 %unpack.1 = (f32[1536,768]{1,0:T(8,128)}, f32[1536,768]{1,0:T(8,128)}, f32[768,1536]{1,0:T(8,128)}, f32[1536,256]{1,0:T(8,128)}, f32[1536,12]{1,0:T(8,128)}, /*i...) custom-call(bf16[2304,768]{1,0:T(8,128)(2,1)} %get-tuple-element.135, ...), custom_call_target="tpu_custom_call" | custom-call | tf_op jit(solution)/shard_map/unpack/pallas_call | solution.py:1398
  544.4 2.0 copy.33
  546.4 0.0 copy-start.5
  546.4 0.0 copy-start.1
  546.4 3.9 copy.39
  550.3 0.0 copy-done.5
  550.3 1.7 copy.40
  552.0 0.0 copy-done.1
  (5 shorter events, 0.0 us)
Async XLA Ops:
  7.2 64.6 %copy-start = (bf16[4,256,1536]{2,1,0:T(8,128)(2,1)S(1)}, bf16[4,256,1536]{2,1,0:T(8,128)(2,1)}, u32[]{:S(2)}) copy-start(bf16[4,256,1536]{2,1,0:T(8,128)(2,1)} %param.17) | copy-start | bytes 9437188
  7.2 302.8 %all-reduce.6.cloned.1.call-start = ((), (), s32[]{:S(2)}) async-start(), calls=%async_computation | async-start | bytes 2359296 | tf_op jit(solution)/shard_map/psum | solution.py:1473
  35.3 8.6 %copy-start.2 = (bf16[2,256,1536]{2,1,0:T(8,128)(2,1)}, bf16[2,256,1536]{2,1,0:T(8,128)(2,1)S(1)}, u32[]{:S(2)}) copy-start(bf16[2,256,1536]{2,1,0:T(8,128)(2,1)S(1)} %get-tuple-element.171) | copy-start | bytes 4718596
  71.8 2.2 copy-start.6
  71.9 4.7 copy-start.4
  254.5 121.4 %all-reduce.8.cloned.1.call-start = ((), (), s32[]{:S(2)}) async-start(), calls=%async_computation.1 | async-start | bytes 2359296 | tf_op jit(solution)/shard_map/psum | solution.py:1478
  313.8 47.9 %copy-start.3 = (bf16[2,256,1536]{2,1,0:T(8,128)(2,1)S(1)}, bf16[2,256,1536]{2,1,0:T(8,128)(2,1)}, u32[]{:S(2)}) copy-start(bf16[2,256,1536]{2,1,0:T(8,128)(2,1)} %copy-done.2) | copy-start | bytes 4718596
  546.4 3.9 copy-start.5
  546.4 5.6 copy-start.1
Sparse Core Ops, SparseCore 0:
  254.7 52.9 all-reduce.5
  310.6 65.2 all-reduce.7
